TPU v7x, 512 devices: a whole 4x4x16 slice. The times are simulated.
512 devices in a mesh: scen: 8 (over x, core), dom: 64 (over z, y).
Axes of the slice: x: 4, y: 4, z: 16, core: 2. Of those that a mesh axis runs over, the one named last changes fastest.
Arguments:
- demand: int32 [2048, 2048], P('dom', 'scen'), may hold values from 0 to 17, as said below
- recourse_init: float32 [2048, 2048], P('dom', 'scen'), may hold values from 0 to 4
- transship: bfloat16 [2048, 2048], P('dom'), may hold values from -0.125 to 0.125
- counts: int32 [2048], P('scen'), may hold values from 1 to 8
- assign: int32 [65536], P('dom'), may hold values from 0 to 2047, as said below
- hold_cost: float32 [65536], P('dom'), may hold values from 0.2 to 3
- stock_init: float32 [65536], P('dom'), may hold values from 0 to 0.5
- mult_init: float32 [8, 65536], P('scen', 'dom'), may hold values from -3 to 3
Outputs:
- consensus: float32 [65536], P('dom')
- multipliers: float32 [8, 65536], P('scen', 'dom')
- recourse: float32 [2048, 2048], P('dom', 'scen')
Inputs may be any that keep to these rules, and one draw needn't show every extreme that they name: Sites of higher index have no smaller range of demand. `assign`: parts of the p-th block of 1024 parts are stocked at sites of the p-th block of 32 sites.
All inputs are finite; a program needn't handle non-finite values.
Results may differ from a plain program's by a relative error of at most 0.0004.
Values may be sent and summed in bfloat16 or wider, within the bound.
No kernel may reach another device: no remote copies, remote signals or barrier semaphores. Data moves between devices by JAX's collectives and lax.ppermute only.
A program may use at most 64 MiB of HBM per device.

v0:
```python
import jax
import jax.numpy as jnp
from jax import lax
from jax.sharding import PartitionSpec as P

SITE_COUNT = 2048


penalty = 1.0
stride = 0.5
prox_weight = 2.0
learn_rate = 0.05
epsilon = 1e-05


def renew_stock(stock, consensus, multipliers, hold_cost, member, pull, total):
    pull_parts = jnp.dot(member, pull, precision=lax.Precision.HIGHEST)
    step = hold_cost + multipliers - pull_parts + prox_weight * (stock - consensus)
    stock = jnp.maximum(stock - learn_rate * step, 0.0)
    weighted, weight_sum = lax.psum((stock * total, total), "scen")
    consensus = weighted / weight_sum
    multipliers = multipliers + prox_weight * (stock - consensus)
    return (stock, consensus, multipliers)


def per_device(demand, recourse_init, transship, counts, assign, hold_cost, stock_init, mult_init):
    site_dev = demand.shape[0]
    dom_rank = lax.axis_index("dom")
    local_site = assign - dom_rank * site_dev
    member = (local_site[:, None] == jnp.arange(site_dev, dtype=jnp.int32)[None, :]).astype(
        jnp.float32
    )
    weights = counts.astype(jnp.float32)
    total = jnp.sum(weights)
    share = weights / total
    stock = stock_init
    consensus = stock_init
    multipliers = mult_init[0]
    demand_draw = demand.astype(jnp.float32)
    recourse = recourse_init
    for outer in range(2):
        stock_by_site = jnp.dot(stock, member, precision=lax.Precision.HIGHEST)
        shortfall = demand_draw - stock_by_site[:, None]
        for inner in range(2):
            rounded = recourse.astype(jnp.bfloat16)
            image = jnp.dot(
                transship,
                lax.all_gather(rounded, "dom", axis=0, tiled=True),
                preferred_element_type=jnp.float32,
            )
            grad = image - penalty * (shortfall - recourse)
            square_sum = lax.psum(jnp.sum(grad * grad, axis=0), "dom")
            scale = jnp.sqrt(square_sum / SITE_COUNT + epsilon)
            recourse = jnp.maximum(recourse - stride * grad / scale[None, :], 0.0)
        pull = penalty * jnp.dot(shortfall - recourse, share, precision=lax.Precision.HIGHEST)
        stock, consensus, multipliers = renew_stock(
            stock, consensus, multipliers, hold_cost, member, pull, total
        )
    return (consensus, multipliers[None, :], recourse)


def solution(mesh):
    in_specs = (
        P("dom", "scen"),
        P("dom", "scen"),
        P("dom", None),
        P("scen"),
        P("dom"),
        P("dom"),
        P("dom"),
        P("scen", "dom"),
    )
    out_specs = (P("dom"), P("scen", "dom"), P("dom", "scen"))
    return jax.shard_map(
        per_device, mesh=mesh, in_specs=in_specs, out_specs=out_specs, check_vma=False
    )
```

profile of v0, /device:TPU:1, one launch (start us, length us, event | category | flops | bytes accessed | tf_op | source)
XLA Modules:
  0.0 1150.5 jit_solution(1712808168407788159)
XLA Ops:
  7.2 0.0 copy-start
  7.2 0.0 all-gather.5.cloned.1.call-start
  7.2 1.4 convert_element_type.20
  8.6 0.0 all-gather.5.cloned.1.call-update
  8.6 0.0 copy-start.7
  8.7 0.0 all-gather.7.cloned.1.call-start
  8.7 0.6 copy-done.7
  9.3 0.7 copy-done.6
  10.0 0.4 convolution_bitcast_fusion.6
  10.4 135.9 %all-gather.5.cloned.1.call-done = bf16[2048,256]{1,0:T(8,128)(2,1)} async-done(((bf16[32,256]{1,0:T(8,128)(2,1)}), bf16[2048,256]{1,0:T(8,128)(2,1)}) %all-gather.5.cloned.1.call-update) | async-done | bytes 1048592 | tf_op jit(solution)/shard_map/all_gather | solution.py:48
  146.3 0.0 copy-done
  146.3 0.0 copy-done.1
  146.4 1.5 multiply_reduce_fusion.3
  147.9 113.9 %psum.52 = f32[256]{0:T(256)S(1)} all-reduce(f32[256]{0:T(256)S(1)} %get-tuple-element.17), channel_id=1, replica_groups=mesh['scen'=8,'dom'=64] {'dom'}, use_global_device_ids=true, to_apply=%region_1.0 | all-reduce | flops 256 | bytes 2048 | tf_op jit(solution)/shard_map/psum | solution.py:52
  261.8 0.6 fusion.16
  262.4 0.0 all-gather.7.cloned.1.call-update
  262.4 0.0 all-gather.9.cloned.1.call-start
  262.5 160.2 %all-gather.7.cloned.1.call-done = bf16[2048,256]{1,0:T(8,128)(2,1)} async-done(((bf16[32,256]{1,0:T(8,128)(2,1)}), bf16[2048,256]{1,0:T(8,128)(2,1)}) %all-gather.7.cloned.1.call-update) | async-done | bytes 1048592 | tf_op jit(solution)/shard_map/all_gather | solution.py:48
  422.6 1.5 multiply_reduce_fusion.2
  424.1 113.9 %psum.53 = f32[256]{0:T(256)S(1)} all-reduce(f32[256]{0:T(256)S(1)} %get-tuple-element.19), channel_id=1, replica_groups=mesh['scen'=8,'dom'=64] {'dom'}, use_global_device_ids=true, to_apply=%region_3.0 | all-reduce | flops 256 | bytes 2048 | tf_op jit(solution)/shard_map/psum | solution.py:52
  538.0 0.6 fusion.15
  538.6 0.0 all-gather.9.cloned.1.call-update
  538.7 0.0 all-gather.11.cloned.1.call-start
  538.7 0.6 copy-done.8
  539.3 0.6 convert_reduce_fusion
  539.9 0.6 convert_divide_fusion
  540.6 0.2 convolution_bitcast_fusion.4
  540.8 0.5 fusion.4
  541.2 0.2 copy-done.4
  541.5 0.0 copy-done.5
  541.5 0.7 broadcast_multiply_fusion.1
  542.2 0.4 convolution_bitcast_fusion.5
  542.5 156.3 %all-gather.9.cloned.1.call-done = bf16[2048,256]{1,0:T(8,128)(2,1)} async-done(((bf16[32,256]{1,0:T(8,128)(2,1)}), bf16[2048,256]{1,0:T(8,128)(2,1)}) %all-gather.9.cloned.1.call-update) | async-done | bytes 1048592 | tf_op jit(solution)/shard_map/all_gather | solution.py:48
  698.9 1.5 multiply_reduce_fusion.1
  700.4 113.9 %psum.56 = f32[256]{0:T(256)S(1)} all-reduce(f32[256]{0:T(256)S(1)} %get-tuple-element.21), channel_id=1, replica_groups=mesh['scen'=8,'dom'=64] {'dom'}, use_global_device_ids=true, to_apply=%region_8.0 | all-reduce | flops 256 | bytes 2048 | tf_op jit(solution)/shard_map/psum | solution.py:52
  814.3 0.6 fusion.14
  814.9 0.0 all-gather.11.cloned.1.call-update
  814.9 50.6 %all-reduce = (f32[1024]{0:T(1024)S(1)}, f32[]{:T(128)}) all-reduce(f32[1024]{0:T(1024)S(1)} %get-tuple-element.9, f32[]{:T(128)} %convert_reduce_fusion), channel_id=1, replica_groups=mesh['scen'=8,'dom'=64] {'scen'}, use_global_device_ids=true, to_apply=%region_5.0 | all-reduce | flops 1025 | bytes 8200 | tf_op jit(solution)/shard_map/psum | solution.py:20
  865.5 109.6 %all-gather.11.cloned.1.call-done = bf16[2048,256]{1,0:T(8,128)(2,1)} async-done(((bf16[32,256]{1,0:T(8,128)(2,1)}), bf16[2048,256]{1,0:T(8,128)(2,1)}) %all-gather.11.cloned.1.call-update) | async-done | bytes 1048592 | tf_op jit(solution)/shard_map/all_gather | solution.py:48
  975.1 1.5 multiply_reduce_fusion
  976.7 113.9 %psum.57 = f32[256]{0:T(256)S(1)} all-reduce(f32[256]{0:T(256)S(1)} %get-tuple-element.23), channel_id=1, replica_groups=mesh['scen'=8,'dom'=64] {'dom'}, use_global_device_ids=true, to_apply=%region_10.0 | all-reduce | flops 256 | bytes 2048 | tf_op jit(solution)/shard_map/psum | solution.py:52
  1090.6 0.0 copy-start.3
  1090.6 0.2 convolution_bitcast_fusion.3
  1090.8 0.4 copy-done.3
  1091.2 0.4 fusion.3
  1091.6 1.4 broadcast_multiply_fusion
  1093.0 49.7 %psum.58 = f32[1024]{0:T(1024)S(1)} all-reduce(f32[1024]{0:T(1024)S(1)} %get-tuple-element.7), channel_id=1, replica_groups=mesh['scen'=8,'dom'=64] {'scen'}, use_global_device_ids=true, to_apply=%region_11.0 | all-reduce | flops 1024 | bytes 8192 | tf_op jit(solution)/shard_map/psum | solution.py:20
  1142.7 1.3 multiply_add_fusion
  (13 shorter events, 0.1 us)
Async XLA Ops:
  7.2 139.2 %copy-start = (bf16[32,2048]{1,0:T(8,128)(2,1)S(1)}, bf16[32,2048]{1,0:T(8,128)(2,1)}, u32[]{:S(2)}) copy-start(bf16[32,2048]{1,0:T(8,128)(2,1)} %param.10) | copy-start | bytes 393220
  7.2 139.2 %all-gather.5.cloned.1.call-start = ((), (), s32[]{:S(2)}) async-start(), calls=%async_computation | async-start | bytes 1064960 | tf_op jit(solution)/shard_map/all_gather | solution.py:48
  8.6 0.7 copy-start.7
  8.7 414.0 %all-gather.7.cloned.1.call-start = ((), (), s32[]{:S(2)}) async-start(), calls=%async_computation.1 | async-start | bytes 1064960 | tf_op jit(solution)/shard_map/all_gather | solution.py:48
  9.3 0.7 copy-start.6
  10.0 136.3 %copy-start.1 = (s32[32,256]{1,0:T(8,128)S(1)}, s32[32,256]{1,0:T(8,128)}, u32[]{:S(2)}) copy-start(s32[32,256]{1,0:T(8,128)} %param.8) | copy-start | bytes 98308
  10.0 136.3 %copy-start.2 = (f32[32,256]{1,0:T(8,128)S(1)}, f32[32,256]{1,0:T(8,128)}, u32[]{:S(2)}) copy-start(f32[32,256]{1,0:T(8,128)} %param.9) | copy-start | bytes 98308
  262.4 436.5 %all-gather.9.cloned.1.call-start = ((), (), s32[]{:S(2)}) async-start(), calls=%async_computation.2 | async-start | bytes 1064960 | tf_op jit(solution)/shard_map/all_gather | solution.py:48
  538.6 0.7 copy-start.8
  538.7 436.5 %all-gather.11.cloned.1.call-start = ((), (), s32[]{:S(2)}) async-start(), calls=%async_computation.3 | async-start | bytes 1064960 | tf_op jit(solution)/shard_map/all_gather | solution.py:48
  540.8 0.7 copy-start.4
  540.8 0.7 copy-start.5
  1090.6 0.6 copy-start.3
Sparse Core Ops, SparseCore 0:
  11.5 134.7 all-gather.4
  262.5 160.0 all-gather.6
  538.8 160.0 all-gather.8
  815.0 160.0 all-gather.10
where the time goes:
time: 1150 us
  waiting for transfers between devices  562 us (49%)
  blocking collectives  556 us (48%)
  between operations  13.8 us (1%)
    all_gather x4, waiting for transfers between devices, per_device(): lax.all_gather(rounded, 'dom', axis=0, tiled=True)  562 us
    psum x4, blocking collectives, per_device(): square_sum = lax.psum(jnp.sum(grad * grad, axis=0), 'dom')  455 us
    psum x2, blocking collectives, renew_stock(): weighted, weight_sum = lax.psum((stock * total, total), 'scen')  100 us
  transfers between devices with their start and end apart: 4, of which 4 were waited for; matrix products, arithmetic and copies ran while one was open for 0% of the time, Pallas kernels for 0%

commit v1 on v0

v1 whole, which is shorter than its diff:
```python
import functools

import jax
import jax.numpy as jnp
from jax import lax
from jax.experimental import pallas as pl
from jax.experimental.pallas import tpu as pltpu
from jax.sharding import Mesh, PartitionSpec as P

SITE_COUNT = 2048
X, CORE, Z, Y = 4, 2, 16, 4
ROWS = 32
COLS = 256
SCEN = 64
PACK = 56

penalty = 1.0
stride = 0.5
prox_weight = 2.0
learn_rate = 0.05
epsilon = 1e-05


def gather_blocks(block, axes, count):
    spread = jnp.broadcast_to(block[None], (count,) + block.shape)
    return lax.all_to_all(spread, axes, 0, 0, tiled=True)


def to_column(row, start):
    lane = lax.broadcasted_iota(jnp.int32, (ROWS, 128), 1)
    sub = lax.broadcasted_iota(jnp.int32, (ROWS, 128), 0)
    picked = jnp.where(lane == sub + start, jnp.broadcast_to(row, (ROWS, 128)), 0.0)
    return jnp.sum(picked, axis=1, keepdims=True)


def recourse_steps(core_ref, mine_ref, other_ref, rec_ref, short_ref, grad_ref, rounded_ref):
    core = core_ref[0]
    for inner in range(2):

        def tile(j, square):
            y = j // 2
            half = j % 2
            acc = jnp.zeros((256, 128), jnp.float32)
            for x in range(X):
                for ref, chunk in ((mine_ref, 2 * x + core), (other_ref, 2 * x + 1 - core)):
                    at = pl.multiple_of(chunk * COLS, COLS)
                    rows = pl.ds(pl.multiple_of(half * 256, 256), 256)
                    acc = acc + jnp.dot(
                        ref[x * Y + y, rows, :],
                        rounded_ref[pl.ds(at, COLS), :],
                        preferred_element_type=jnp.float32,
                    )
            for k in range(8):
                at = pl.ds(pl.multiple_of(((half * 8 + k) * Y + y) * ROWS, ROWS), ROWS)
                grad = acc[k * ROWS : (k + 1) * ROWS] - penalty * (short_ref[at, :] - rec_ref[at, :])
                grad_ref[at, :] = grad
                square = square + grad * grad
            return square

        square = lax.fori_loop(0, 8, tile, jnp.zeros((ROWS, 128), jnp.float32))
        square = jnp.sum(square, axis=0, keepdims=True)
        factor = stride / jnp.sqrt(square / SITE_COUNT + epsilon)

        def renew(j, carry):
            at = pl.ds(pl.multiple_of(j * 256, 256), 256)
            rec = jnp.maximum(rec_ref[at, :] - grad_ref[at, :] * factor, 0.0)
            rec_ref[at, :] = rec
            rounded_ref[at, :] = rec.astype(jnp.bfloat16)
            return carry

        lax.fori_loop(0, 8, renew, 0)


def pull_sums(share_ref, rec_ref, short_ref, pull_ref):
    for j in range(8):
        at = pl.ds(j * 256, 256)
        gap = short_ref[at, :] - rec_ref[at, :]
        pull_ref[:, at] = penalty * lax.dot_general(
            share_ref[...],
            gap,
            (((1,), (1,)), ((), ())),
            precision=lax.Precision.HIGHEST,
            preferred_element_type=jnp.float32,
        )


def first_kernel(
    core_ref, share_ref, mine_ref, other_ref, pack_ref, rec_ref, short_ref, pull_ref, grad_ref, rounded_ref
):
    def load(b, carry):
        at = pl.ds(pl.multiple_of(b * ROWS, ROWS), ROWS)
        both = pack_ref[b, 0:ROWS, :]
        rec_ref[at, :] = both
        rounded_ref[at, :] = both.astype(jnp.bfloat16)
        short_ref[at, :] = pltpu.roll(both, SCEN, 1)
        return carry

    lax.fori_loop(0, Z * Y, load, 0)
    recourse_steps(core_ref, mine_ref, other_ref, rec_ref, short_ref, grad_ref, rounded_ref)
    pull_sums(share_ref, rec_ref, short_ref, pull_ref)


def second_kernel(
    core_ref,
    share_ref,
    mine_ref,
    other_ref,
    pack_ref,
    rec_in_ref,
    short_in_ref,
    pulled_ref,
    rec_ref,
    pull_ref,
    short_ref,
    grad_ref,
    rounded_ref,
):
    def load(b, carry):
        at = pl.ds(pl.multiple_of(b * ROWS, ROWS), ROWS)
        z = b // Y
        y = b % Y
        pull = to_column(pulled_ref[pl.ds(z, 1), :], y * ROWS)
        site = lax.broadcasted_iota(jnp.int32, (ROWS, 128), 0).astype(jnp.float32)
        total = jnp.zeros((ROWS, 128), jnp.float32)
        gain = jnp.broadcast_to(learn_rate * pull, (ROWS, 128))
        for k in range(8):
            base = pack_ref[b, ROWS + k : ROWS + k + 1, :]
            index = pack_ref[b, ROWS + 8 + k : ROWS + 9 + k, :]
            stock = jnp.maximum(base + gain, 0.0)
            total = total + jnp.where(index == site, stock, 0.0)
        new_sum = jnp.sum(total, axis=1, keepdims=True)
        old_sum = to_column(pack_ref[b, ROWS + 16 : ROWS + 17, :], 0)
        rec = rec_in_ref[at, :]
        rec_ref[at, :] = rec
        rounded_ref[at, :] = rec.astype(jnp.bfloat16)
        short_ref[at, :] = short_in_ref[at, :] + (old_sum - new_sum)
        return carry

    lax.fori_loop(0, Z * Y, load, 0)
    recourse_steps(core_ref, mine_ref, other_ref, rec_ref, short_ref, grad_ref, rounded_ref)
    pull_sums(share_ref, rec_ref, short_ref, pull_ref)


def run_kernel(kernel, outs, scratch, *args):
    vmem = pl.BlockSpec(memory_space=pltpu.VMEM)
    return pl.pallas_call(
        kernel,
        out_shape=outs,
        in_specs=[pl.BlockSpec(memory_space=pltpu.SMEM)] + [vmem] * (len(args) - 1),
        out_specs=[vmem] * len(outs),
        scratch_shapes=scratch,
        compiler_params=pltpu.CompilerParams(vmem_limit_bytes=40 * 1024 * 1024),
    )(*args)


def per_device(demand, recourse_init, transship, counts, assign, hold_cost, stock_init, mult_init):
    core = lax.axis_index("core")
    column = lax.axis_index("x") * CORE + core
    y = lax.axis_index("y")
    z = lax.axis_index("z")
    f32 = jnp.float32
    wide = jax.ShapeDtypeStruct((SITE_COUNT, 128), f32)
    sums = jax.ShapeDtypeStruct((8, SITE_COUNT), f32)

    multipliers = mult_init[0]
    local_site = assign - (z * Y + y) * ROWS
    member = (local_site[:, None] == jnp.arange(ROWS, dtype=jnp.int32)[None, :]).astype(f32)
    stock_sum = jnp.dot(stock_init, member, precision=lax.Precision.HIGHEST)
    short = demand.astype(f32) - stock_sum[:, None]
    base = stock_init - learn_rate * (hold_cost + multipliers)
    sites = jnp.concatenate(
        [recourse_init.reshape(ROWS, Y, SCEN), short.reshape(ROWS, Y, SCEN)], axis=2
    ).transpose(1, 0, 2)
    parts = jnp.concatenate(
        [
            base.reshape(8, 128),
            local_site.astype(f32).reshape(8, 128),
            jnp.broadcast_to(jnp.pad(stock_sum, (0, 128 - ROWS))[None], (8, 128)),
        ],
        axis=0,
    )
    packed = jnp.concatenate([sites, jnp.broadcast_to(parts[None], (Y,) + parts.shape)], axis=1)
    packed = lax.all_to_all(packed, "y", 0, 0, tiled=True)
    packed = lax.all_gather(packed, "z", axis=0, tiled=True)

    block = lax.dynamic_slice(transship, (0, column * COLS), (ROWS, COLS))
    along_z = gather_blocks(block, "z", Z).reshape(Z * ROWS, COLS)
    mine = gather_blocks(along_z, ("x", "y"), X * Y)
    other = lax.ppermute(mine, "core", [(0, 1), (1, 0)])

    weights = counts.astype(f32)
    total = jnp.sum(weights)
    share = lax.dynamic_slice(weights / total, (y * SCEN,), (SCEN,))
    share = jnp.broadcast_to(jnp.pad(share, (0, 128 - SCEN))[None], (8, 128))
    core_arr = core.reshape(1).astype(jnp.int32)

    vm = pltpu.VMEM
    rec, short_all, pull1 = run_kernel(
        first_kernel,
        [wide, wide, sums],
        [vm((SITE_COUNT, 128), f32), vm((SITE_COUNT, 128), jnp.bfloat16)],
        core_arr,
        share,
        mine,
        other,
        packed,
    )
    pull1 = lax.psum(pull1[0].reshape(Z, Y * ROWS), "y")
    rec, pull2 = run_kernel(
        second_kernel,
        [wide, sums],
        [vm((SITE_COUNT, 128), f32), vm((SITE_COUNT, 128), f32), vm((SITE_COUNT, 128), jnp.bfloat16)],
        core_arr,
        share,
        mine,
        other,
        packed,
        rec,
        short_all,
        pull1,
    )
    own = lax.dynamic_slice(rec, (z * Y * ROWS, 0), (Y * ROWS, SCEN)).reshape(Y, ROWS, SCEN)
    own = lax.all_to_all(own, "y", 0, 0, tiled=True)
    recourse = own.transpose(1, 0, 2).reshape(ROWS, Y * SCEN)

    pull2 = pull2[0].reshape(Z, Y * ROWS)
    pulls = jnp.concatenate(
        [
            lax.dynamic_index_in_dim(pull1, z, 0, False).reshape(Y, 1, ROWS),
            lax.dynamic_index_in_dim(pull2, z, 0, False).reshape(Y, 1, ROWS),
            jnp.broadcast_to(total, (Y, 1, 64)),
        ],
        axis=2,
    )
    send = jnp.concatenate(
        [
            jnp.broadcast_to(multipliers.reshape(1, 8, 128), (Y, 8, 128)),
            jnp.broadcast_to(pulls, (Y, 8, 128)),
        ],
        axis=1,
    )
    send = jnp.broadcast_to(send[None], (X * CORE,) + send.shape).reshape(X * CORE * Y, 16, 128)
    got = lax.all_to_all(send, ("x", "core", "y"), 0, 0, tiled=True).reshape(X * CORE, Y, 16, 128)
    mult = lax.dynamic_index_in_dim(got, y, 1, False)[:, :8].reshape(X * CORE, 1024)
    group_total = got[:, 0, 8, 64][:, None]
    pull1 = got[:, 0, 8, 0:ROWS]
    pull2 = jnp.sum(got[:, :, 8, ROWS : 2 * ROWS], axis=1)
    pulls = jnp.dot(
        jnp.concatenate([pull1, pull2], axis=0), member.T, precision=lax.Precision.HIGHEST
    )
    step = hold_cost[None] + mult - pulls[: X * CORE]
    stock = jnp.maximum(stock_init[None] - learn_rate * step, 0.0)
    all_total = jnp.sum(group_total)
    consensus = jnp.sum(group_total * stock, axis=0) / all_total
    mult = mult + prox_weight * (stock - consensus[None])
    step = hold_cost[None] + mult - pulls[X * CORE :] + prox_weight * (stock - consensus[None])
    stock = jnp.maximum(stock - learn_rate * step, 0.0)
    consensus = jnp.sum(group_total * stock, axis=0) / all_total
    mult = mult + prox_weight * (stock - consensus[None])
    mult = lax.dynamic_slice(mult, (column, 0), (1, 1024))
    return (consensus, mult, recourse)


def solution(mesh):
    grid = Mesh(mesh.devices.reshape(X, CORE, Z, Y), ("x", "core", "z", "y"))
    scen, dom = ("x", "core"), ("z", "y")
    in_specs = (
        P(dom, scen),
        P(dom, scen),
        P(dom, None),
        P(scen),
        P(dom),
        P(dom),
        P(dom),
        P(scen, dom),
    )
    out_specs = (P(dom), P(scen, dom), P(dom, scen))
    return jax.shard_map(
        per_device, mesh=grid, in_specs=in_specs, out_specs=out_specs, check_vma=False
    )
```

time: 1150 us -> 288 us (0.25)
  blocking collectives: 556 us -> 47.7 us
  waiting for transfers between devices: 562 us -> 132 us
  Pallas kernels: 0 us -> 39.8 us
  starting transfers between devices: 0.16 us -> 34.6 us
    psum x6 -> x1, blocking collectives: 556 us -> 8.55 us  [per_device(): pull1 = lax.psum(pull1[0].reshape(Z, Y * ROWS), 'y')]
    all_gather x4 -> x1, waiting for transfers between devices: 562 us -> 70.7 us  [per_device(): packed = lax.all_gather(packed, 'z', axis=0, tiled=True)]
    all_to_all x0 -> x3, waiting for transfers between devices: none -> 60.9 us  [the longest x1 50.1 us: gather_blocks(): return lax.all_to_all(spread, axes, 0, 0, tiled=True)]
    pallas_call x0 -> x2, Pallas kernels: none -> 39.8 us  [run_kernel(): pl.pallas_call(kernel, out_shape=outs, in_specs=[pl.BlockSpec(memory_spac...]
    all_to_all x0 -> x2, blocking collectives: none -> 39.2 us  [the longest x1 28.7 us: gather_blocks(): return lax.all_to_all(spread, axes, 0, 0, tiled=True)]
    all_to_all x0 -> x3, starting transfers between devices: none -> 28.1 us  [the longest x1 17.9 us: per_device(): lax.all_to_all(send, ('x', 'core', 'y'), 0, 0, tiled=True)]
  transfers between devices with their start and end apart: 4 -> 5, of which waited for: 4 -> 4; matrix products, arithmetic and copies ran while one was open for 0% -> 2% of each run, Pallas kernels for 0% -> 0%
where the time goes in v1:
time: 288 us; the launch traced here: 287 us
  waiting for transfers between devices  132 us (46%)
  blocking collectives  47.7 us (17%)
  Pallas kernels  39.8 us (14%)
  starting transfers between devices  34.6 us (12%)
  between operations  14.4 us (5%)
  local copies, waits for them, and re-layouts  12.9 us (4%)
  other arithmetic  5.16 us (2%)
    all_gather x1, waiting for transfers between devices, per_device(): packed = lax.all_gather(packed, 'z', axis=0, tiled=True)  70.7 us
    all_to_all x1, waiting for transfers between devices, gather_blocks(): return lax.all_to_all(spread, axes, 0, 0, tiled=True)  50.1 us
    pallas_call x2, Pallas kernels, run_kernel(): pl.pallas_call(kernel, out_shape=outs, in_specs=[pl.BlockSpec(memory_spac...  39.8 us
    all_to_all x1, blocking collectives, gather_blocks(): return lax.all_to_all(spread, axes, 0, 0, tiled=True)  28.7 us
    all_to_all x1, starting transfers between devices, per_device(): lax.all_to_all(send, ('x', 'core', 'y'), 0, 0, tiled=True)  17.9 us
    all_to_all x1, blocking collectives, per_device(): packed = lax.all_to_all(packed, 'y', 0, 0, tiled=True)  10.5 us
    psum x1, blocking collectives, per_device(): pull1 = lax.psum(pull1[0].reshape(Z, Y * ROWS), 'y')  8.55 us
    all_to_all x1, starting transfers between devices, gather_blocks(): return lax.all_to_all(spread, axes, 0, 0, tiled=True)  6.95 us
  transfers between devices with their start and end apart: 5, of which 4 were waited for; matrix products, arithmetic and copies ran while one was open for 2% of the time, Pallas kernels for 0%

profile of v1, /device:TPU:1, one launch (start us, length us, event | category | flops | bytes accessed | tf_op | source)
XLA Modules:
  0.0 287.1 jit_solution(13146049405073557218)
XLA Ops:
  7.2 0.9 copy-done
  8.1 28.7 %all_to_all.25 = bf16[16,32,256]{2,1,0:T(8,128)(2,1)S(1)} all-to-all(bf16[16,32,256]{2,1,0:T(8,128)(2,1)S(1)} %broadcast_in_dim.27), channel_id=1, replica_groups=mesh['x'=4,'core'=2,'z'=16,'y'=4] {'z'}, dimensions={0} | all-to-all | bytes 524288 | tf_op jit(solution)/shard_map/all_to_all | solution.py:26
  36.8 2.4 broadcast_in_dim.29
  39.2 6.9 %all-to-all-start.1 = ((bf16[16,512,256]{2,1,0:T(8,128)(2,1)}), bf16[16,512,256]{2,1,0:T(8,128)(2,1)}, u32[]{:S(2)}, u32[]{:S(2)}) async-start(bf16[16,512,256]{2,1,0:T(8,128)(2,1)} %broadcast_in_dim.29), calls=%async_computation.1 | async-start | bytes 8388608 | tf_op jit(solution)/shard_map/all_to_all | solution.py:26
  46.2 0.0 all-gather.2.cloned.1.call-start
  46.3 0.4 convolution_bitcast_fusion
  46.6 50.1 %all-to-all-done.1.mine_ref = bf16[16,512,256]{2,1,0:T(8,128)(2,1)} async-done(((bf16[16,512,256]{2,1,0:T(8,128)(2,1)}), bf16[16,512,256]{2,1,0:T(8,128)(2,1)}, u32[]{:S(2)}, u32[]{:S(2)}) %all-to-all-start.1) | async-done | bytes 4194336 | tf_op jit(solution)/shard_map/all_to_all | solution.py:26
  96.7 6.4 %collective-permute-start = (bf16[16,512,256]{2,1,0:T(8,128)(2,1)}, bf16[16,512,256]{2,1,0:T(8,128)(2,1)}, u32[]{:S(2)}, u32[]{:S(2)}) collective-permute-start(bf16[16,512,256]{2,1,0:T(8,128)(2,1)} %all-to-all-done.1.mine_ref), channel_id=1, source_target_pairs={{0,64},{64,0},{1,65},{65,1},{2,66},{66,2},{3,67},{67,3},{4,68},{68... | collective-permute-start | bytes 12582920 | tf_op jit(solution)/shard_map/ppermute | solution.py:189
  103.2 0.1 convert_subtract_fusion
  103.2 0.1 reshape.64
  103.3 0.1 reshape.63
  103.5 0.1 maximum_bitcast_fusion
  103.7 10.5 %all_to_all.26 = f32[4,56,128]{2,1,0:T(8,128)} all-to-all(f32[4,56,128]{2,1,0:T(8,128)S(1)} %copy.18), channel_id=1, replica_groups=mesh['x'=4,'core'=2,'z'=16,'y'=4] {'y'}, dimensions={0} | all-to-all | bytes 229376 | tf_op jit(solution)/shard_map/all_to_all | solution.py:183
  114.2 0.6 convert_reduce_fusion
  114.8 0.6 convert_divide_fusion
  115.5 0.1 dynamic_slice.23
  115.5 0.6 broadcast_in_dim.32
  116.2 0.1 pad.16.clone
  116.3 70.7 %all-gather.2.cloned.1.call-done.pack_ref = f32[64,56,128]{2,1,0:T(8,128)} async-done(((f32[4,56,128]{2,1,0:T(8,128)}), f32[64,56,128]{2,1,0:T(8,128)}) %all-gather.2.cloned.1.call-update) | async-done | bytes 1835024 | tf_op jit(solution)/shard_map/all_gather | solution.py:184
  187.0 1.5 copy-done.1
  188.5 16.4 %shard_map.103 = (f32[2048,128]{1,0:T(8,128)S(1)}, f32[2048,128]{1,0:T(8,128)S(1)}, f32[8,2048]{1,0:T(8,128)S(1)}) custom-call(s32[1]{0:T(128)} %bitcast.1.core_ref, f32[8,128]{1,0:T(8,128)S(1)} %broadcast_in_dim.26.share_ref, bf16[16,512,256]{2,1,0:T(8,128)(2,1)} %all-to-all-done.1.mine_ref, bf16[16,512,256]{2,1,0:T(8,128)(2,1)} %collective-permute-done.other_ref, ...), custom_call_target="tpu_custom_call" | custom-call | tf_op jit(solution)/shard_map/pallas_call | solution.py:146
  204.9 1.0 copy-done.3
  205.9 8.6 %psum.7.pulled_ref = f32[16,128]{1,0:T(8,128)S(1)} all-reduce(f32[16,128]{1,0:T(8,128)S(1)} %bitcast.55), channel_id=1, replica_groups=mesh['x'=4,'core'=2,'z'=16,'y'=4] {'y'}, use_global_device_ids=true, to_apply=%region_1.2 | all-reduce | flops 2048 | bytes 16384 | tf_op jit(solution)/shard_map/psum | solution.py:208
  214.5 1.2 copy-done.4
  215.7 23.5 %shard_map.104 = (f32[2048,128]{1,0:T(8,128)S(1)}, f32[8,2048]{1,0:T(8,128)S(1)}) custom-call(s32[1]{0:T(128)} %bitcast.1.core_ref, f32[8,128]{1,0:T(8,128)S(1)} %broadcast_in_dim.26.share_ref, bf16[16,512,256]{2,1,0:T(8,128)(2,1)} %all-to-all-done.1.mine_ref, bf16[16,512,256]{2,1,0:T(8,128)(2,1)} %collective-permute-done.other_ref, ...), custom_call_target="tpu_custom_call" | custom-call | tf_op jit(solution)/shard_map/pallas_call | solution.py:146
  239.1 1.0 copy-done.5
  240.2 0.1 reshape.67
  240.3 0.1 reshape.68
  240.3 0.8 constant_dynamic-slice_fusion
  241.2 0.7 reshape.89
  241.9 3.3 %all-to-all-start.4 = ((f32[4,1,2048]{2,1,0:T(1,128)}), f32[4,1,2048]{2,1,0:T(1,128)S(1)}, u32[]{:S(2)}, u32[]{:S(2)}) async-start(f32[4,1,2048]{2,1,0:T(1,128)} %reshape.89), calls=%async_computation.4 | async-start | bytes 65536 | tf_op jit(solution)/shard_map/all_to_all | solution.py:223
  245.2 0.1 maximum_bitcast_fusion.1
  245.3 4.2 %all-to-all-done.4 = f32[4,1,2048]{2,1,0:T(1,128)S(1)} async-done(((f32[4,1,2048]{2,1,0:T(1,128)}), f32[4,1,2048]{2,1,0:T(1,128)S(1)}, u32[]{:S(2)}, u32[]{:S(2)}) %all-to-all-start.4) | async-done | bytes 32800 | tf_op jit(solution)/shard_map/all_to_all | solution.py:223
  249.4 0.7 broadcast_in_dim.35
  250.1 17.9 %all-to-all-start.3 = ((f32[32,16,128]{2,1,0:T(8,128)}), f32[32,16,128]{2,1,0:T(8,128)S(1)}, u32[]{:S(2)}, u32[]{:S(2)}) async-start(f32[32,16,128]{2,1,0:T(8,128)} %bitcast.12), calls=%async_computation.3 | async-start | bytes 524288 | tf_op jit(solution)/shard_map/all_to_all | solution.py:243
  268.0 0.5 broadcast.67
  268.5 0.7 reduce.12
  269.3 0.1 reshape.90
  269.4 0.7 reshape.73
  270.1 6.7 %all-to-all-done.3 = f32[32,16,128]{2,1,0:T(8,128)S(1)} async-done(((f32[32,16,128]{2,1,0:T(8,128)}), f32[32,16,128]{2,1,0:T(8,128)S(1)}, u32[]{:S(2)}, u32[]{:S(2)}) %all-to-all-start.3) | async-done | bytes 262176 | tf_op jit(solution)/shard_map/all_to_all | solution.py:243
  276.8 0.1 slice_reduce_fusion
  277.0 0.7 slice_reduce_fusion.1
  277.6 0.4 fusion
  278.1 0.1 multiply_reduce_fusion.1
  278.2 0.7 broadcast_divide_fusion.1
  278.9 0.1 multiply_reduce_fusion
  278.9 0.7 broadcast_divide_fusion
  279.6 0.6 dynamic-slice_add_fusion
  (47 shorter events, 0.3 us)
Async XLA Ops:
  7.2 0.9 copy-start
  39.2 7.1 %copy-start.12 = (s32[1024]{0:T(1024)S(1)}, s32[1024]{0:T(1024)}, u32[]{:S(2)}) copy-start(s32[1024]{0:T(1024)} %param.12) | copy-start | bytes 12292
  39.2 7.1 %copy-start.6 = (f32[1024]{0:T(1024)S(1)}, f32[1024]{0:T(1024)}, u32[]{:S(2)}) copy-start(f32[1024]{0:T(1024)} %param.14) | copy-start | bytes 12292
  39.2 64.0 %copy-start.9 = (s32[32,256]{1,0:T(8,128)S(1)}, s32[32,256]{1,0:T(8,128)}, u32[]{:S(2)}) copy-start(s32[32,256]{1,0:T(8,128)} %param.8) | copy-start | bytes 98308
  39.2 64.2 %copy-start.8 = (f32[32,256]{1,0:T(8,128)S(1)}, f32[32,256]{1,0:T(8,128)}, u32[]{:S(2)}) copy-start(f32[32,256]{1,0:T(8,128)} %param.9) | copy-start | bytes 98308
  39.2 64.3 %copy-start.7 = (f32[1024]{0:T(1024)S(1)}, f32[1024]{0:T(1024)}, u32[]{:S(2)}) copy-start(f32[1024]{0:T(1024)} %param.13) | copy-start | bytes 12292
  39.2 64.3 %copy-start.10 = (f32[1,1024]{1,0:T(1,128)S(1)}, f32[1,1024]{1,0:T(1,128)}, u32[]{:S(2)}) copy-start(f32[1,1024]{1,0:T(1,128)} %param.15) | copy-start | bytes 12292
  39.2 75.0 %copy-start.13 = (s32[256]{0:T(256)S(1)}, s32[256]{0:T(256)}, u32[]{:S(2)}) copy-start(s32[256]{0:T(256)} %param.11) | copy-start | bytes 3076
  39.2 57.5 %all-to-all-start.1 = ((bf16[16,512,256]{2,1,0:T(8,128)(2,1)}), bf16[16,512,256]{2,1,0:T(8,128)(2,1)}, u32[]{:S(2)}, u32[]{:S(2)}) async-start(bf16[16,512,256]{2,1,0:T(8,128)(2,1)} %broadcast_in_dim.29), calls=%async_computation.1 | async-start | bytes 8388608 | tf_op jit(solution)/shard_map/all_to_all | solution.py:26
  46.2 140.9 %all-gather.2.cloned.1.call-start = ((), (), s32[]{:S(2)}) async-start(), calls=%async_computation.5 | async-start | bytes 1949696 | tf_op jit(solution)/shard_map/all_gather | solution.py:184
  96.7 90.3 %collective-permute-start = (bf16[16,512,256]{2,1,0:T(8,128)(2,1)}, bf16[16,512,256]{2,1,0:T(8,128)(2,1)}, u32[]{:S(2)}, u32[]{:S(2)}) collective-permute-start(bf16[16,512,256]{2,1,0:T(8,128)(2,1)} %all-to-all-done.1.mine_ref), channel_id=1, source_target_pairs={{0,64},{64,0},{1,65},{65,1},{2,66},{66,2},{3,67},{67,3},{4,68},{68... | collective-permute-start | bytes 12582920 | tf_op jit(solution)/shard_map/ppermute | solution.py:189
  187.0 1.5 copy-start.1
  188.5 25.9 %copy-start.2 = (f32[64,56,128]{2,1,0:T(8,128)S(1)}, f32[64,56,128]{2,1,0:T(8,128)}, u32[]{:S(2)}) copy-start(f32[64,56,128]{2,1,0:T(8,128)} %all-gather.2.cloned.1.call-done.pack_ref) | copy-start | bytes 5505028
  204.9 1.0 copy-start.3
  214.4 1.2 copy-start.4
  239.1 1.0 copy-start.5
  241.9 7.5 %all-to-all-start.4 = ((f32[4,1,2048]{2,1,0:T(1,128)}), f32[4,1,2048]{2,1,0:T(1,128)S(1)}, u32[]{:S(2)}, u32[]{:S(2)}) async-start(f32[4,1,2048]{2,1,0:T(1,128)} %reshape.89), calls=%async_computation.4 | async-start | bytes 65536 | tf_op jit(solution)/shard_map/all_to_all | solution.py:223
  250.1 26.7 %all-to-all-start.3 = ((f32[32,16,128]{2,1,0:T(8,128)}), f32[32,16,128]{2,1,0:T(8,128)S(1)}, u32[]{:S(2)}, u32[]{:S(2)}) async-start(f32[32,16,128]{2,1,0:T(8,128)} %bitcast.12), calls=%async_computation.3 | async-start | bytes 524288 | tf_op jit(solution)/shard_map/all_to_all | solution.py:243
  279.6 0.6 copy-start.11
Sparse Core Ops, SparseCore 0:
  114.3 72.6 all-gather.1

commit v2 on v0

v2 whole, which is shorter than its diff:
```python
import jax
import jax.numpy as jnp
from jax import lax
from jax.experimental import pallas as pl
from jax.experimental.pallas import tpu as pltpu
from jax.sharding import Mesh, PartitionSpec as P

SITE_COUNT = 2048
X, CORE, Z, Y = 4, 2, 16, 4
GROUPS = X * CORE
ROWS = 32
COLS = 256
SCEN = 64
PARTS = 24

penalty = 1.0
stride = 0.5
prox_weight = 2.0
learn_rate = 0.05
epsilon = 1e-05

f32 = jnp.float32


def lanes_of(shape):
    return lax.broadcasted_iota(jnp.int32, shape, len(shape) - 1)


def rows_of(shape):
    return lax.broadcasted_iota(jnp.int32, shape, len(shape) - 2)


def pick(row, index):
    return jnp.take_along_axis(
        jnp.broadcast_to(row, (8, 128)), index, axis=1, mode="promise_in_bounds"
    )


def prep_kernel(
    place_ref, demand_ref, rec_ref, counts_ref, assign_ref, hold_ref, stock_ref, mult_ref, packed_ref, aux_ref
):
    z, y = place_ref[1], place_ref[2]
    weights = counts_ref[...].astype(f32)
    total = jnp.sum(jnp.sum(weights, axis=1, keepdims=True), axis=0, keepdims=True)
    row = jnp.where(y >= 2, weights[1:2], weights[0:1])
    row = jnp.where(y % 2 == 1, pltpu.roll(row, SCEN, 1), row) / total
    row = jnp.where(lanes_of((1, 128)) < SCEN, row, 0.0)
    aux_ref[0:8, :] = jnp.broadcast_to(row, (8, 128))
    aux_ref[8:16, :] = jnp.broadcast_to(total, (8, 128))

    index = assign_ref[...] - (z * Y + y) * ROWS
    stock = stock_ref[...]
    site = rows_of((ROWS, 128))
    sums = jnp.zeros((ROWS, 128), f32)
    for k in range(8):
        sums = sums + jnp.where(index[k : k + 1] == site, stock[k : k + 1], 0.0)
    column = jnp.sum(sums, axis=1, keepdims=True)
    as_row = jnp.sum(jnp.where(lanes_of((ROWS, 128)) == site, column, 0.0), axis=0, keepdims=True)
    base = stock - learn_rate * (hold_ref[...] + mult_ref[...])
    low = lanes_of((ROWS, 128)) < SCEN
    for q in range(Y):
        tile = slice(q // 2 * 128, q // 2 * 128 + 128)
        rec = rec_ref[:, tile]
        short = demand_ref[:, tile].astype(f32) - column
        if q % 2 == 0:
            both = jnp.where(low, rec, pltpu.roll(short, SCEN, 1))
        else:
            both = jnp.where(low, pltpu.roll(rec, SCEN, 1), short)
        packed_ref[q, 0:ROWS, :] = both
        packed_ref[q, ROWS : ROWS + 8, :] = base
        packed_ref[q, ROWS + 8 : ROWS + 16, :] = index.astype(f32)
        packed_ref[q, ROWS + 16 : ROWS + 24, :] = jnp.broadcast_to(as_row, (8, 128))


def spread_z_kernel(place_ref, transship_ref, packed_ref, spread_ref, parts_ref):
    parts_ref[...] = packed_ref[:, ROWS:, :]
    at = pl.ds(pl.multiple_of(place_ref[3] * COLS, COLS), COLS)
    block = transship_ref[:, at]
    for z in range(Z):
        spread_ref[z] = block


def recourse_steps(core, mine_ref, other_ref, rec_ref, short_ref, grad_ref, rounded_ref):
    def one_step(inner, carry):
        square = jnp.zeros((ROWS, 128), f32)
        for y in range(Y):
            acc = jnp.zeros((512, 128), f32)
            for x in range(X):
                for ref, chunk in ((mine_ref, 2 * x + core), (other_ref, 2 * x + 1 - core)):
                    at = pl.ds(pl.multiple_of(chunk * COLS, COLS), COLS)
                    acc = acc + jnp.dot(
                        ref[x * Y + y], rounded_ref[at, :], preferred_element_type=f32
                    )
            for z in range(Z):
                at = pl.ds((z * Y + y) * ROWS, ROWS)
                grad = acc[z * ROWS : (z + 1) * ROWS] - penalty * (short_ref[at, :] - rec_ref[at, :])
                grad_ref[at, :] = grad
                square = square + grad * grad
        square = jnp.sum(square, axis=0, keepdims=True)
        factor = stride / jnp.sqrt(square / SITE_COUNT + epsilon)
        for j in range(16):
            at = pl.ds(j * 128, 128)
            rec = jnp.maximum(rec_ref[at, :] - grad_ref[at, :] * factor, 0.0)
            rec_ref[at, :] = rec
            rounded_ref[at, :] = rec.astype(jnp.bfloat16)
        return carry

    lax.fori_loop(0, 2, one_step, 0)


def pull_sums(share, rec_ref, short_ref, put):
    for z in range(Z):
        at = pl.ds(z * 128, 128)
        gap = penalty * (short_ref[at, :] - rec_ref[at, :]) * share
        put(z, jnp.sum(gap.T, axis=0, keepdims=True))


def first_kernel(
    place_ref, aux_ref, mine_ref, other_ref, sites_ref, rec_ref, short_ref, pull_ref, grad_ref, rounded_ref
):
    def load(b, carry):
        at = pl.ds(pl.multiple_of(b * ROWS, ROWS), ROWS)
        both = sites_ref[b]
        rec_ref[at, :] = both
        rounded_ref[at, :] = both.astype(jnp.bfloat16)
        short_ref[at, :] = pltpu.roll(both, SCEN, 1)
        return carry

    lax.fori_loop(0, Z * Y, load, 0, unroll=8)
    recourse_steps(place_ref[0], mine_ref, other_ref, rec_ref, short_ref, grad_ref, rounded_ref)

    def put(z, row):
        for q in range(Y):
            pull_ref[q, z : z + 1, :] = row

    pull_sums(aux_ref[0:1, :], rec_ref, short_ref, put)


def second_kernel(
    place_ref,
    aux_ref,
    mine_ref,
    other_ref,
    parts_ref,
    rec_in_ref,
    short_in_ref,
    pulled_ref,
    mult_ref,
    send_ref,
    rec_ref,
    pull_ref,
    short_ref,
    grad_ref,
    rounded_ref,
):
    pull_ref[0] = pulled_ref[0] + pulled_ref[1] + pulled_ref[2] + pulled_ref[3]
    eye = lanes_of((ROWS, 128)) == rows_of((ROWS, 128))
    site = rows_of((ROWS, 128)).astype(f32)

    def load(b, carry):
        at = pl.ds(pl.multiple_of(b * ROWS, ROWS), ROWS)
        index = parts_ref[b, 8:16, :]
        pull = pick(pull_ref[0, pl.ds(b // Y, 1), :], index.astype(jnp.int32) + b % Y * ROWS)
        stock = jnp.maximum(parts_ref[b, 0:8, :] + learn_rate * pull, 0.0)
        change = jnp.where(eye, -parts_ref[b, 16:17, :], 0.0)
        for k in range(8):
            change = change + jnp.where(index[k : k + 1] == site, stock[k : k + 1], 0.0)
        rec = rec_in_ref[at, :]
        rec_ref[at, :] = rec
        rounded_ref[at, :] = rec.astype(jnp.bfloat16)
        short_ref[at, :] = short_in_ref[at, :] - jnp.sum(change, axis=1, keepdims=True)
        return carry

    lax.fori_loop(0, Z * Y, load, 0, unroll=8)
    recourse_steps(place_ref[0], mine_ref, other_ref, rec_ref, short_ref, grad_ref, rounded_ref)

    def put(z, row):
        pull_ref[1, z : z + 1, :] = row

    pull_sums(aux_ref[0:1, :], rec_ref, short_ref, put)
    z = place_ref[1]
    sub = rows_of((8, 128))
    pulls = jnp.where(
        sub == 0,
        pull_ref[0, pl.ds(z, 1), :],
        jnp.where(sub == 1, pull_ref[1, pl.ds(z, 1), :], aux_ref[8:9, :]),
    )
    low = lanes_of((16, 128)) < SCEN
    for q in range(Y):
        start = pl.multiple_of((z * Y + q) * ROWS, ROWS)
        upper = rec_ref[pl.ds(start, 16), :]
        lower = rec_ref[pl.ds(start + 16, 16), :]
        pair = jnp.where(low, upper, pltpu.roll(lower, SCEN, 1))
        for g in range(GROUPS):
            send_ref[g * Y + q, 0:8, :] = mult_ref[...]
            send_ref[g * Y + q, 8:16, :] = pulls
            send_ref[g * Y + q, 16:32, :] = pair


def last_kernel(
    place_ref, got_ref, assign_ref, hold_ref, stock_ref, consensus_ref, mult_ref, rec_ref, all_ref
):
    z, y, column = place_ref[1], place_ref[2], place_ref[3]
    index = assign_ref[...] - z * (Y * ROWS)
    hold = hold_ref[...]
    start = stock_ref[...]
    totals = [got_ref[g * Y, 10:11, :] for g in range(GROUPS)]
    all_total = totals[0]
    for g in range(1, GROUPS):
        all_total = all_total + totals[g]
    mults = [got_ref[g * Y + y, 0:8, :] for g in range(GROUPS)]
    stocks = []
    weighted = jnp.zeros((8, 128), f32)
    for g in range(GROUPS):
        pull = pick(got_ref[g * Y, 8:9, :], index)
        stock = jnp.maximum(start - learn_rate * (hold + mults[g] - pull), 0.0)
        weighted = weighted + totals[g] * stock
        stocks.append(stock)
    consensus = weighted / all_total
    weighted = jnp.zeros((8, 128), f32)
    for g in range(GROUPS):
        row = got_ref[g * Y, 9:10, :]
        for q in range(1, Y):
            row = row + got_ref[g * Y + q, 9:10, :]
        pull = pick(row, index)
        apart = prox_weight * (stocks[g] - consensus)
        mults[g] = mults[g] + apart
        stock = jnp.maximum(stocks[g] - learn_rate * (hold + mults[g] - pull + apart), 0.0)
        weighted = weighted + totals[g] * stock
        stocks[g] = stock
    consensus = weighted / all_total
    consensus_ref[...] = consensus
    for g in range(GROUPS):
        all_ref[g] = mults[g] + prox_weight * (stocks[g] - consensus)
    mult_ref[...] = all_ref[column]

    low = lanes_of((16, 128)) < SCEN
    for m in range(2):
        tile = slice(m * 128, m * 128 + 128)
        even = got_ref[column * Y + 2 * m, 16:32, :]
        odd = got_ref[column * Y + 2 * m + 1, 16:32, :]
        rec_ref[0:16, tile] = jnp.where(low, even, pltpu.roll(odd, SCEN, 1))
        rec_ref[16:32, tile] = jnp.where(low, pltpu.roll(even, SCEN, 1), odd)


def run_kernel(kernel, outs, scratch, *args):
    vmem = pl.BlockSpec(memory_space=pltpu.VMEM)
    outs = [out if isinstance(out, jax.ShapeDtypeStruct) else jax.ShapeDtypeStruct(out, f32) for out in outs]
    return pl.pallas_call(
        kernel,
        out_shape=outs,
        in_specs=[pl.BlockSpec(memory_space=pltpu.SMEM)] + [vmem] * (len(args) - 1),
        out_specs=[vmem] * len(outs),
        scratch_shapes=[pltpu.VMEM(*entry) for entry in scratch],
        compiler_params=pltpu.CompilerParams(vmem_limit_bytes=40 * 1024 * 1024),
    )(*args)


def one_block(always, work, *args):
    shapes = jax.eval_shape(work, *args)

    def never(*args):
        return jax.tree.map(lambda shape: jnp.zeros(shape.shape, shape.dtype), shapes)

    return lax.cond(always, work, never, *args)


def per_device(demand, recourse_init, transship, counts, assign, hold_cost, stock_init, mult_init):
    core = lax.axis_index("core")
    column = lax.axis_index("x") * CORE + core
    y = lax.axis_index("y")
    z = lax.axis_index("z")
    place = jnp.stack([core, z, y, column]).astype(jnp.int32)
    wide = (SITE_COUNT, 128)
    assign = assign.reshape(8, 128)
    hold_cost = hold_cost.reshape(8, 128)
    stock_init = stock_init.reshape(8, 128)
    mult_init = mult_init.reshape(8, 128)

    packed, aux = run_kernel(
        prep_kernel,
        [(Y, ROWS + PARTS, 128), (16, 128)],
        [],
        place,
        demand,
        recourse_init,
        counts.reshape(2, 128),
        assign,
        hold_cost,
        stock_init,
        mult_init,
    )
    packed = lax.all_to_all(packed, "y", 0, 0, tiled=True)
    sites = packed[:, :ROWS]

    bf16 = jnp.bfloat16
    always = column * COLS >= 0

    def spread_z(transship, packed):
        block, parts = run_kernel(
            spread_z_kernel,
            [jax.ShapeDtypeStruct((Z, ROWS, COLS), bf16), (Y, PARTS, 128)],
            [],
            place,
            transship,
            packed,
        )
        return lax.all_to_all(block, "z", 0, 0, tiled=True).reshape(Z * ROWS, COLS), parts

    def spread_xy(along_z):
        spread = jnp.broadcast_to(along_z[None], (X * Y, Z * ROWS, COLS))
        mine = lax.all_to_all(spread, ("x", "y"), 0, 0, tiled=True)
        return mine, lax.ppermute(mine, "core", [(0, 1), (1, 0)])

    sites = lax.all_gather(sites, "z", axis=0, tiled=True)
    along_z, parts = one_block(always, spread_z, transship, packed)
    parts = lax.all_gather(parts, "z", axis=0, tiled=True)
    mine, other = one_block(always, spread_xy, along_z)

    rec, short, pull1 = run_kernel(
        first_kernel,
        [wide, wide, (Y, Z, 128)],
        [(wide, f32), (wide, jnp.bfloat16)],
        place,
        aux,
        mine,
        other,
        sites,
    )
    pull1 = lax.all_to_all(pull1, "y", 0, 0, tiled=True)
    (send,) = run_kernel(
        second_kernel,
        [(GROUPS * Y, 32, 128)],
        [(wide, f32), ((2, Z, 128), f32), (wide, f32), (wide, f32), (wide, jnp.bfloat16)],
        place,
        aux,
        mine,
        other,
        parts,
        rec,
        short,
        pull1,
        mult_init,
    )
    got = lax.all_to_all(send, ("x", "core", "y"), 0, 0, tiled=True)
    consensus, multipliers, recourse = run_kernel(
        last_kernel,
        [(8, 128), (8, 128), (ROWS, Y * SCEN)],
        [((GROUPS, 8, 128), f32)],
        place,
        got,
        assign,
        hold_cost,
        stock_init,
    )
    return (consensus.reshape(1024), multipliers.reshape(1, 1024), recourse)


def solution(mesh):
    grid = Mesh(mesh.devices.reshape(X, CORE, Z, Y), ("x", "core", "z", "y"))
    scen, dom = ("x", "core"), ("z", "y")
    in_specs = (
        P(dom, scen),
        P(dom, scen),
        P(dom, None),
        P(scen),
        P(dom),
        P(dom),
        P(dom),
        P(scen, dom),
    )
    out_specs = (P(dom), P(scen, dom), P(dom, scen))
    return jax.shard_map(
        per_device, mesh=grid, in_specs=in_specs, out_specs=out_specs, check_vma=False
    )
```

time: 1150 us -> 205 us (0.18)
  waiting for transfers between devices: 562 us -> 7.13 us
  blocking collectives: 556 us -> 136 us
  Pallas kernels: 0 us -> 24.6 us
  starting transfers between devices: 0.16 us -> 14.7 us
    all_gather x4 -> x1, waiting for transfers between devices: 562 us -> 0.01 us  [per_device(): sites = lax.all_gather(sites, 'z', axis=0, tiled=True)]
    psum x6 -> x0, blocking collectives: 556 us -> none  [the longest x4 455 us: per_device(): square_sum = lax.psum(jnp.sum(grad * grad, axis=0), 'dom')]
    all_to_all x0 -> x4, blocking collectives: none -> 108 us  [the longest x1 46.8 us: spread_xy(): mine = lax.all_to_all(spread, ('x', 'y'), 0, 0, tiled=True)]
    all_gather x0 -> x1, blocking collectives: none -> 28.4 us  [per_device(): parts = lax.all_gather(parts, 'z', axis=0, tiled=True)]
    pallas_call x0 -> x5, Pallas kernels: none -> 24.6 us  [run_kernel(): pl.pallas_call(kernel, out_shape=outs, in_specs=[pl.BlockSpec(memory_spac...]
  transfers between devices with their start and end apart: 4 -> 3, of which waited for: 4 -> 1; matrix products, arithmetic and copies ran while one was open for 0% -> 0% of each run, Pallas kernels for 0% -> 0%
where the time goes in v2:
time: 205 us; the launch traced here: 204 us
  blocking collectives  136 us (66%)
  Pallas kernels  24.6 us (12%)
  starting transfers between devices  14.7 us (7%)
  between operations  14.1 us (7%)
  local copies, waits for them, and re-layouts  7.21 us (4%)
  waiting for transfers between devices  7.13 us (3%)
    all_to_all x1, blocking collectives, spread_xy(): mine = lax.all_to_all(spread, ('x', 'y'), 0, 0, tiled=True)  46.8 us
    all_gather x1, blocking collectives, per_device(): parts = lax.all_gather(parts, 'z', axis=0, tiled=True)  28.4 us
    all_to_all x1, blocking collectives, spread_z(): lax.all_to_all(block, 'z', 0, 0, tiled=True).reshape(Z * ROWS, COLS)  27.5 us
    pallas_call x5, Pallas kernels, run_kernel(): pl.pallas_call(kernel, out_shape=outs, in_specs=[pl.BlockSpec(memory_spac...  24.6 us
    all_to_all x1, blocking collectives, per_device(): got = lax.all_to_all(send, ('x', 'core', 'y'), 0, 0, tiled=True)  24 us
    ppermute x1, starting transfers between devices, spread_xy(): return (mine, lax.ppermute(mine, 'core', [(0, 1), (1, 0)]))  11.4 us
    all_to_all x1, blocking collectives, per_device(): packed = lax.all_to_all(packed, 'y', 0, 0, tiled=True)  9.55 us
    ppermute x1, waiting for transfers between devices, spread_xy(): return (mine, lax.ppermute(mine, 'core', [(0, 1), (1, 0)]))  7.11 us
  transfers between devices with their start and end apart: 3, of which 1 were waited for; matrix products, arithmetic and copies ran while one was open for 0% of the time, Pallas kernels for 0%

profile of v2, /device:TPU:1, one launch (start us, length us, event | category | flops | bytes accessed | tf_op | source)
XLA Modules:
  0.0 204.1 jit_solution(5502300600861391382)
XLA Ops:
  7.2 0.0 all-gather.2.cloned.1.call-start
  7.2 0.1 pad_add_fusion.place_ref
  7.3 0.0 copy-start.1
  7.3 0.8 copy-done.1
  8.1 0.0 copy-start.2
  8.1 0.8 copy-done.2
  8.8 0.0 copy-start.3
  8.8 0.7 copy-done.3
  9.5 0.0 copy-start.5
  9.5 0.7 copy-done.5
  10.2 0.0 copy-start.7
  10.2 0.7 copy-done.7
  10.9 0.0 copy-start.9
  10.9 0.7 copy-done.9
  11.6 0.0 copy-start.11
  11.6 0.7 copy-done.11
  12.2 0.7 shard_map.104
  13.0 9.6 %all_to_all.25 = f32[4,56,128]{2,1,0:T(8,128)S(1)} all-to-all(f32[4,56,128]{2,1,0:T(8,128)S(1)} %get-tuple-element.29), channel_id=1, replica_groups=mesh['x'=4,'core'=2,'z'=16,'y'=4] {'y'}, dimensions={0} | all-to-all | bytes 229376 | tf_op jit(solution)/shard_map/all_to_all | solution.py:293
  22.5 0.6 slice.4
  23.1 0.0 all-gather.2.cloned.1.call-update
  23.2 28.5 %conditional.2 = (f32[4,24,128]{2,1,0:T(8,128)S(1)}, bf16[512,256]{1,0:T(8,128)(2,1)S(1)}) conditional(s32[]{:T(128)} %convert_element_type.4, () %tuple.29, (s32[4]{0:T(128)S(1)}, bf16[32,2048]{1,0:T(8,128)(2,1)}, f32[4,56,128]{2,1,0:T(8,128)S(1)}) %tuple.30), branch_computations={%region_0.0_spmd, %region_1.0_spmd} | conditional | bytes 524304 | solution.py:265
  23.2 0.9 branch_1_fun.1
  24.1 27.5 %all_to_all.23 = bf16[16,32,256]{2,1,0:T(8,128)(2,1)S(1)} all-to-all(bf16[16,32,256]{2,1,0:T(8,128)(2,1)S(1)} %get-tuple-element.12), channel_id=1, replica_groups=mesh['x'=4,'core'=2,'z'=16,'y'=4] {'z'}, dimensions={0} | all-to-all | bytes 524288 | tf_op jit(solution)/shard_map/cond/branch_1_fun/all_to_all | solution.py:308
  51.6 65.7 %conditional.3 = (bf16[16,512,256]{2,1,0:T(8,128)(2,1)}, bf16[16,512,256]{2,1,0:T(8,128)(2,1)}) conditional(s32[]{:T(128)} %convert_element_type.4, () %tuple.28, bf16[512,256]{1,0:T(8,128)(2,1)S(1)} %get-tuple-element.30), branch_computations={%region_2.0_spmd, %region_3.0_spmd} | conditional | bytes 29622328 | solution.py:265
  51.6 0.4 broadcast_in_dim.0
  52.0 46.8 %all_to_all.24 = bf16[16,512,256]{2,1,0:T(8,128)(2,1)} all-to-all(bf16[16,512,256]{2,1,0:T(8,128)(2,1)S(1)} %broadcast_in_dim.0), channel_id=1, replica_groups=mesh['x'=4,'core'=2,'z'=16,'y'=4] {'x','y'}, dimensions={0} | all-to-all | bytes 8388608 | tf_op jit(solution)/shard_map/cond/branch_1_fun/all_to_all | solution.py:312
  98.8 11.4 %collective-permute-start = (bf16[16,512,256]{2,1,0:T(8,128)(2,1)}, bf16[16,512,256]{2,1,0:T(8,128)(2,1)}, u32[]{:S(2)}, u32[]{:S(2)}) collective-permute-start(bf16[16,512,256]{2,1,0:T(8,128)(2,1)} %all_to_all.24), channel_id=1, source_target_pairs={{0,64},{64,0},{1,65},{65,1},{2,66},{66,2},{3,67},{67,3},{4,68},{68... | collective-permute-start | bytes 12582920 | tf_op jit(solution)/shard_map/cond/branch_1_fun/ppermute | solution.py:313
  110.2 7.1 %collective-permute-done = bf16[16,512,256]{2,1,0:T(8,128)(2,1)} collective-permute-done((bf16[16,512,256]{2,1,0:T(8,128)(2,1)}, bf16[16,512,256]{2,1,0:T(8,128)(2,1)}, u32[]{:S(2)}, u32[]{:S(2)}) %collective-permute-start) | collective-permute-done | bytes 4194336 | tf_op jit(solution)/shard_map/cond/branch_1_fun/ppermute | solution.py:313
  117.3 0.0 all-gather.2.cloned.1.call-done.sites_ref
  117.3 0.0 copy-start
  117.3 1.2 copy-done
  118.5 0.0 copy-start.4
  118.5 10.5 %shard_map.105 = (f32[2048,128]{1,0:T(8,128)S(1)}, f32[2048,128]{1,0:T(8,128)S(1)}, f32[4,16,128]{2,1,0:T(8,128)}) custom-call(s32[4]{0:T(128)S(1)} %pad_add_fusion.place_ref, f32[16,128]{1,0:T(8,128)S(1)} %get-tuple-element.28.aux_ref, bf16[16,512,256]{2,1,0:T(8,128)(2,1)} %get-tuple-element.31.mine_ref, bf16[16,512,256]{2,1,0:T(8,128)(2,1)} %get-tuple-element.32.other_ref, ...), custom_call_target="tpu_custom_call" | custom-call | tf_op jit(solution)/shard_map/pallas_call | solution.py:249
  129.0 3.3 %all-to-all-start.3 = ((f32[4,16,128]{2,1,0:T(8,128)}), f32[4,16,128]{2,1,0:T(8,128)S(1)}, u32[]{:S(2)}, u32[]{:S(2)}) async-start(f32[4,16,128]{2,1,0:T(8,128)} %get-tuple-element.36), calls=%async_computation.3 | async-start | bytes 65536 | tf_op jit(solution)/shard_map/all_to_all | solution.py:330
  132.3 28.4 %all_gather.6.parts_ref = f32[64,24,128]{2,1,0:T(8,128)S(1)} all-gather(f32[4,24,128]{2,1,0:T(8,128)S(1)} %get-tuple-element.33), channel_id=1, replica_groups=mesh['x'=4,'core'=2,'z'=16,'y'=4] {'z'}, dimensions={0}, use_global_device_ids=true | all-gather | bytes 835584 | tf_op jit(solution)/shard_map/all_gather | solution.py:317
  160.7 0.0 all-to-all-done.3.pulled_ref
  160.7 0.0 copy-done.4
  160.7 0.0 copy-start.6
  160.7 0.0 copy-start.8
  160.7 0.0 copy-start.10
  160.8 11.2 %shard_map.106 = f32[32,32,128]{2,1,0:T(8,128)S(1)} custom-call(s32[4]{0:T(128)S(1)} %pad_add_fusion.place_ref, f32[16,128]{1,0:T(8,128)S(1)} %get-tuple-element.28.aux_ref, bf16[16,512,256]{2,1,0:T(8,128)(2,1)} %get-tuple-element.31.mine_ref, bf16[16,512,256]{2,1,0:T(8,128)(2,1)} %get-tuple-element.32.other_ref, f32[64,24,128]{2,1,0:T(8,128)S(1)} %all_gather.6.parts_ref, ...), custom_call_target="tpu_custom_call" | custom-call | tf_op jit(solution)/shard_map/pallas_call | solution.py:249
  172.0 24.0 %all_to_all.26.got_ref = f32[32,32,128]{2,1,0:T(8,128)S(1)} all-to-all(f32[32,32,128]{2,1,0:T(8,128)S(1)} %shard_map.106), channel_id=1, replica_groups=mesh['x'=4,'core'=2,'z'=16,'y'=4] {'x','core','y'}, dimensions={0} | all-to-all | bytes 1048576 | tf_op jit(solution)/shard_map/all_to_all | solution.py:345
  196.0 0.0 copy-done.6
  196.0 0.0 copy-done.8
  196.0 0.0 copy-done.10
  196.0 1.3 shard_map.107
Async XLA Ops:
  7.2 110.1 %all-gather.2.cloned.1.call-start = ((), (), s32[]{:S(2)}) async-start(), calls=%async_computation.5 | async-start | bytes 1114112 | tf_op jit(solution)/shard_map/all_gather | solution.py:315
  7.3 0.8 copy-start.1
  8.1 0.8 copy-start.2
  8.8 0.7 copy-start.3
  9.5 0.7 copy-start.5
  10.2 0.7 copy-start.7
  10.9 0.7 copy-start.9
  11.6 0.7 copy-start.11
  98.8 18.5 %collective-permute-start = (bf16[16,512,256]{2,1,0:T(8,128)(2,1)}, bf16[16,512,256]{2,1,0:T(8,128)(2,1)}, u32[]{:S(2)}, u32[]{:S(2)}) collective-permute-start(bf16[16,512,256]{2,1,0:T(8,128)(2,1)} %all_to_all.24), channel_id=1, source_target_pairs={{0,64},{64,0},{1,65},{65,1},{2,66},{66,2},{3,67},{67,3},{4,68},{68... | collective-permute-start | bytes 12582920 | tf_op jit(solution)/shard_map/cond/branch_1_fun/ppermute | solution.py:313
  117.3 1.2 copy-start
  118.5 42.2 %copy-start.4 = (f32[1,1024]{1,0:T(1,128)S(1)}, f32[1,1024]{1,0:T(1,128)}, u32[]{:S(2)}) copy-start(f32[1,1024]{1,0:T(1,128)} %param.19) | copy-start | bytes 12292
  129.0 31.7 %all-to-all-start.3 = ((f32[4,16,128]{2,1,0:T(8,128)}), f32[4,16,128]{2,1,0:T(8,128)S(1)}, u32[]{:S(2)}, u32[]{:S(2)}) async-start(f32[4,16,128]{2,1,0:T(8,128)} %get-tuple-element.36), calls=%async_computation.3 | async-start | bytes 65536 | tf_op jit(solution)/shard_map/all_to_all | solution.py:330
  160.7 35.2 %copy-start.6 = (s32[1024]{0:T(1024)S(1)}, s32[1024]{0:T(1024)}, u32[]{:S(2)}) copy-start(s32[1024]{0:T(1024)} %param.16) | copy-start | bytes 12292
  160.7 35.2 %copy-start.8 = (f32[1024]{0:T(1024)S(1)}, f32[1024]{0:T(1024)}, u32[]{:S(2)}) copy-start(f32[1024]{0:T(1024)} %param.17) | copy-start | bytes 12292
  160.7 35.2 %copy-start.10 = (f32[1024]{0:T(1024)S(1)}, f32[1024]{0:T(1024)}, u32[]{:S(2)}) copy-start(f32[1024]{0:T(1024)} %param.18) | copy-start | bytes 12292
Sparse Core Ops, SparseCore 0:
  23.3 69.2 all-gather.1

commit v3 on v2

--- a/solution.py
+++ b/solution.py
@@ -11,7 +11,7 @@
 ROWS = 32
 COLS = 256
 SCEN = 64
-PARTS = 24
+PARTS = 32
 
 penalty = 1.0
 stride = 0.5
@@ -36,9 +36,17 @@
     )
 
 
-def prep_kernel(
-    place_ref, demand_ref, rec_ref, counts_ref, assign_ref, hold_ref, stock_ref, mult_ref, packed_ref, aux_ref
-):
+def prep_kernel(place_ref, *refs):
+    inputs, (packed_ref, aux_ref), copies = refs[:7], refs[7:9], refs[9:16]
+    started = [
+        pltpu.make_async_copy(source, target, refs[16].at[k])
+        for k, (source, target) in enumerate(zip(inputs, copies))
+    ]
+    for copy in started:
+        copy.start()
+    for copy in started:
+        copy.wait()
+    demand_ref, rec_ref, counts_ref, assign_ref, hold_ref, stock_ref, mult_ref = copies
     z, y = place_ref[1], place_ref[2]
     weights = counts_ref[...].astype(f32)
     total = jnp.sum(jnp.sum(weights, axis=1, keepdims=True), axis=0, keepdims=True)
@@ -69,7 +77,7 @@
         packed_ref[q, 0:ROWS, :] = both
         packed_ref[q, ROWS : ROWS + 8, :] = base
         packed_ref[q, ROWS + 8 : ROWS + 16, :] = index.astype(f32)
-        packed_ref[q, ROWS + 16 : ROWS + 24, :] = jnp.broadcast_to(as_row, (8, 128))
+        packed_ref[q, ROWS + 16 : ROWS + 32, :] = jnp.broadcast_to(as_row, (16, 128))
 
 
 def spread_z_kernel(place_ref, transship_ref, packed_ref, spread_ref, parts_ref):
@@ -98,11 +106,15 @@
                 square = square + grad * grad
         square = jnp.sum(square, axis=0, keepdims=True)
         factor = stride / jnp.sqrt(square / SITE_COUNT + epsilon)
-        for j in range(16):
-            at = pl.ds(j * 128, 128)
+
+        def renew(j, carry):
+            at = pl.ds(pl.multiple_of(j * 256, 256), 256)
             rec = jnp.maximum(rec_ref[at, :] - grad_ref[at, :] * factor, 0.0)
             rec_ref[at, :] = rec
             rounded_ref[at, :] = rec.astype(jnp.bfloat16)
+            return carry
+
+        lax.fori_loop(0, 8, renew, 0)
         return carry
 
     lax.fori_loop(0, 2, one_step, 0)
@@ -243,16 +255,18 @@
         rec_ref[16:32, tile] = jnp.where(low, pltpu.roll(even, SCEN, 1), odd)
 
 
-def run_kernel(kernel, outs, scratch, *args):
+def run_kernel(kernel, outs, scratch, *args, hbm=0, vmem_mib=16):
     vmem = pl.BlockSpec(memory_space=pltpu.VMEM)
     outs = [out if isinstance(out, jax.ShapeDtypeStruct) else jax.ShapeDtypeStruct(out, f32) for out in outs]
     return pl.pallas_call(
         kernel,
         out_shape=outs,
-        in_specs=[pl.BlockSpec(memory_space=pltpu.SMEM)] + [vmem] * (len(args) - 1),
+        in_specs=[pl.BlockSpec(memory_space=pltpu.SMEM)]
+        + [pl.BlockSpec(memory_space=pl.ANY)] * hbm
+        + [vmem] * (len(args) - 1 - hbm),
         out_specs=[vmem] * len(outs),
-        scratch_shapes=[pltpu.VMEM(*entry) for entry in scratch],
-        compiler_params=pltpu.CompilerParams(vmem_limit_bytes=40 * 1024 * 1024),
+        scratch_shapes=[pltpu.VMEM(*entry) if isinstance(entry, tuple) else entry for entry in scratch],
+        compiler_params=pltpu.CompilerParams(vmem_limit_bytes=vmem_mib * 1024 * 1024),
     )(*args)
 
 
@@ -277,11 +291,7 @@
     stock_init = stock_init.reshape(8, 128)
     mult_init = mult_init.reshape(8, 128)
 
-    packed, aux = run_kernel(
-        prep_kernel,
-        [(Y, ROWS + PARTS, 128), (16, 128)],
-        [],
-        place,
+    raw = (
         demand,
         recourse_init,
         counts.reshape(2, 128),
@@ -289,6 +299,14 @@
         hold_cost,
         stock_init,
         mult_init,
+    )
+    packed, aux = run_kernel(
+        prep_kernel,
+        [(Y, ROWS + PARTS, 128), (16, 128)],
+        [(entry.shape, entry.dtype) for entry in raw] + [pltpu.SemaphoreType.DMA((7,))],
+        place,
+        *raw,
+        hbm=len(raw),
     )
     packed = lax.all_to_all(packed, "y", 0, 0, tiled=True)
     sites = packed[:, :ROWS]
@@ -309,13 +327,16 @@
 
     def spread_xy(along_z):
         spread = jnp.broadcast_to(along_z[None], (X * Y, Z * ROWS, COLS))
-        mine = lax.all_to_all(spread, ("x", "y"), 0, 0, tiled=True)
-        return mine, lax.ppermute(mine, "core", [(0, 1), (1, 0)])
+        return lax.all_to_all(spread, ("x", "y"), 0, 0, tiled=True)
+
+    def swap_cores(mine):
+        return lax.ppermute(mine, "core", [(0, 1), (1, 0)])
 
     sites = lax.all_gather(sites, "z", axis=0, tiled=True)
     along_z, parts = one_block(always, spread_z, transship, packed)
     parts = lax.all_gather(parts, "z", axis=0, tiled=True)
-    mine, other = one_block(always, spread_xy, along_z)
+    mine = one_block(always, spread_xy, along_z)
+    other = one_block(always, swap_cores, mine)
 
     rec, short, pull1 = run_kernel(
         first_kernel,

time: 205 us -> 210 us (1.024)
  waiting for transfers between devices: 7.13 us -> 34.3 us
  blocking collectives: 136 us -> 112 us
    all_gather x1 -> x0, blocking collectives: 28.4 us -> none  [per_device(): parts = lax.all_gather(parts, 'z', axis=0, tiled=True)]
    all_gather x0 -> x1, waiting for transfers between devices: none -> 27.2 us  [per_device(): parts = lax.all_gather(parts, 'z', axis=0, tiled=True)]
    all_to_all x1, blocking collectives: 24 us -> 27.9 us  [per_device(): got = lax.all_to_all(send, ('x', 'core', 'y'), 0, 0, tiled=True)]
    unnamed x24 -> x26, local copies, waits for them, and re-layouts: 6.19 us -> 7.41 us
  transfers between devices with their start and end apart: 3 -> 4, of which waited for: 1 -> 2; matrix products, arithmetic and copies ran while one was open for 0% -> 0% of each run, Pallas kernels for 0% -> 6%
where the time goes in v3:
time: 210 us; the launch traced here: 209 us
  blocking collectives  112 us (53%)
  waiting for transfers between devices  34.3 us (16%)
  Pallas kernels  25.5 us (12%)
  starting transfers between devices  14.7 us (7%)
  between operations  14.1 us (7%)
  local copies, waits for them, and re-layouts  8.43 us (4%)
    all_to_all x1, blocking collectives, spread_xy(): return lax.all_to_all(spread, ('x', 'y'), 0, 0, tiled=True)  46.8 us
    all_to_all x1, blocking collectives, per_device(): got = lax.all_to_all(send, ('x', 'core', 'y'), 0, 0, tiled=True)  27.9 us
    all_to_all x1, blocking collectives, spread_z(): lax.all_to_all(block, 'z', 0, 0, tiled=True).reshape(Z * ROWS, COLS)  27.5 us
    all_gather x1, waiting for transfers between devices, per_device(): parts = lax.all_gather(parts, 'z', axis=0, tiled=True)  27.2 us
    pallas_call x5, Pallas kernels, run_kernel(): pl.pallas_call(kernel, out_shape=outs, in_specs=[pl.BlockSpec(memory_spac...  25.5 us
    ppermute x1, starting transfers between devices, swap_cores(): return lax.ppermute(mine, 'core', [(0, 1), (1, 0)])  11.3 us
    all_to_all x1, blocking collectives, per_device(): packed = lax.all_to_all(packed, 'y', 0, 0, tiled=True)  9.64 us
    unnamed x26, local copies, waits for them, and re-layouts  7.41 us
  transfers between devices with their start and end apart: 4, of which 2 were waited for; matrix products, arithmetic and copies ran while one was open for 0% of the time, Pallas kernels for 6%

profile of v3, /device:TPU:1, one launch (start us, length us, event | category | flops | bytes accessed | tf_op | source)
XLA Modules:
  0.0 208.9 jit_solution(3106952816088425564)
XLA Ops:
  7.2 0.0 all-gather.5.cloned.1.call-start
  7.2 0.1 pad_add_fusion.place_ref
  7.3 0.0 copy-start.2
  7.3 0.8 copy-done.2
  8.1 0.0 copy-start.3
  8.1 0.8 copy-done.3
  8.8 0.7 copy-done.4
  9.5 0.0 copy-start.6
  9.5 0.7 copy-done.6
  10.2 0.0 copy-start.8
  10.2 0.7 copy-done.8
  10.9 0.0 copy-start.10
  10.9 0.7 copy-done.10
  11.6 0.0 copy-start.12
  11.6 0.7 copy-done.12
  12.2 0.9 shard_map.104
  13.1 9.6 %all_to_all.25 = f32[4,64,128]{2,1,0:T(8,128)S(1)} all-to-all(f32[4,64,128]{2,1,0:T(8,128)S(1)} %get-tuple-element.34), channel_id=1, replica_groups=mesh['x'=4,'core'=2,'z'=16,'y'=4] {'y'}, dimensions={0} | all-to-all | bytes 262144 | tf_op jit(solution)/shard_map/all_to_all | solution.py:311
  22.8 0.6 slice.4
  23.4 0.0 all-gather.5.cloned.1.call-update
  23.4 0.0 all-gather.3.cloned.1.call-start
  23.5 29.1 %conditional.3 = (f32[4,32,128]{2,1,0:T(8,128)}, bf16[512,256]{1,0:T(8,128)(2,1)S(1)}) conditional(s32[]{:T(128)} %convert_element_type.2, () %tuple.33, (s32[4]{0:T(128)S(1)}, bf16[32,2048]{1,0:T(8,128)(2,1)}, f32[4,64,128]{2,1,0:T(8,128)S(1)}) %tuple.34), branch_computations={%region_0.0_spmd, %region_1.0_spmd} | conditional | bytes 524304 | solution.py:279
  23.5 1.6 branch_1_fun.1
  25.1 27.5 %all_to_all.23 = bf16[16,32,256]{2,1,0:T(8,128)(2,1)S(1)} all-to-all(bf16[16,32,256]{2,1,0:T(8,128)(2,1)S(1)} %get-tuple-element.19), channel_id=1, replica_groups=mesh['x'=4,'core'=2,'z'=16,'y'=4] {'z'}, dimensions={0} | all-to-all | bytes 524288 | tf_op jit(solution)/shard_map/cond/branch_1_fun/all_to_all | solution.py:326
  52.5 0.0 all-gather.3.cloned.1.call-update
  52.6 47.2 %conditional.4 = (bf16[16,512,256]{2,1,0:T(8,128)(2,1)}) conditional(s32[]{:T(128)} %convert_element_type.2, () %tuple.32, bf16[512,256]{1,0:T(8,128)(2,1)S(1)} %get-tuple-element.35), branch_computations={%region_2.0_spmd, %region_3.0_spmd} | conditional | bytes 12845064 | solution.py:279
  52.6 0.4 broadcast_in_dim.0
  53.0 46.8 %all_to_all.24 = bf16[16,512,256]{2,1,0:T(8,128)(2,1)} all-to-all(bf16[16,512,256]{2,1,0:T(8,128)(2,1)S(1)} %broadcast_in_dim.0), channel_id=1, replica_groups=mesh['x'=4,'core'=2,'z'=16,'y'=4] {'x','y'}, dimensions={0} | all-to-all | bytes 8388608 | tf_op jit(solution)/shard_map/cond/branch_1_fun/all_to_all | solution.py:330
  99.8 18.5 %conditional.5 = (bf16[16,512,256]{2,1,0:T(8,128)(2,1)}) conditional(s32[]{:T(128)} %convert_element_type.2, () %tuple.35, bf16[16,512,256]{2,1,0:T(8,128)(2,1)} %get-tuple-element.49.mine_ref), branch_computations={%region_4.0_spmd, %region_5.0_spmd} | conditional | bytes 16777264 | solution.py:279
  99.8 11.3 %collective-permute-start = (bf16[16,512,256]{2,1,0:T(8,128)(2,1)}, bf16[16,512,256]{2,1,0:T(8,128)(2,1)}, u32[]{:S(2)}, u32[]{:S(2)}) collective-permute-start(bf16[16,512,256]{2,1,0:T(8,128)(2,1)} %param.5), channel_id=1, source_target_pairs={{0,64},{64,0},{1,65},{65,1},{2,66},{66,2},{3,67},{67,3},{4,68},{68... | collective-permute-start | bytes 12582920 | tf_op jit(solution)/shard_map/cond/branch_1_fun/ppermute | solution.py:333
  111.1 7.1 %collective-permute-done = bf16[16,512,256]{2,1,0:T(8,128)(2,1)} collective-permute-done((bf16[16,512,256]{2,1,0:T(8,128)(2,1)}, bf16[16,512,256]{2,1,0:T(8,128)(2,1)}, u32[]{:S(2)}, u32[]{:S(2)}) %collective-permute-start) | collective-permute-done | bytes 4194336 | tf_op jit(solution)/shard_map/cond/branch_1_fun/ppermute | solution.py:333
  118.3 0.0 copy-start.1
  118.3 1.2 copy-done.1
  119.5 0.0 copy-start.5
  119.5 10.5 %shard_map.105 = (f32[2048,128]{1,0:T(8,128)S(1)}, f32[2048,128]{1,0:T(8,128)S(1)}, f32[4,16,128]{2,1,0:T(8,128)}) custom-call(s32[4]{0:T(128)S(1)} %pad_add_fusion.place_ref, f32[16,128]{1,0:T(8,128)S(1)} %get-tuple-element.33.aux_ref, bf16[16,512,256]{2,1,0:T(8,128)(2,1)} %get-tuple-element.49.mine_ref, bf16[16,512,256]{2,1,0:T(8,128)(2,1)} %get-tuple-element.50.other_ref, ...), custom_call_target="tpu_custom_call" | custom-call | tf_op jit(solution)/shard_map/pallas_call | solution.py:261
  130.0 3.3 %all-to-all-start.3 = ((f32[4,16,128]{2,1,0:T(8,128)}), f32[4,16,128]{2,1,0:T(8,128)S(1)}, u32[]{:S(2)}, u32[]{:S(2)}) async-start(f32[4,16,128]{2,1,0:T(8,128)} %get-tuple-element.39), calls=%async_computation.3 | async-start | bytes 65536 | tf_op jit(solution)/shard_map/all_to_all | solution.py:351
  133.2 27.2 %all-gather.3.cloned.1.call-done.parts_ref = f32[64,32,128]{2,1,0:T(8,128)} async-done(((f32[4,32,128]{2,1,0:T(8,128)}), f32[64,32,128]{2,1,0:T(8,128)}) %all-gather.3.cloned.1.call-update) | async-done | bytes 1048592 | tf_op jit(solution)/shard_map/all_gather | solution.py:337
  160.4 0.0 all-to-all-done.3.pulled_ref
  160.4 0.0 copy-done.5
  160.4 0.0 copy-start
  160.4 1.2 copy-done
  161.7 0.0 copy-start.7
  161.7 0.0 copy-start.9
  161.7 11.2 %shard_map.106 = f32[32,32,128]{2,1,0:T(8,128)S(1)} custom-call(s32[4]{0:T(128)S(1)} %pad_add_fusion.place_ref, f32[16,128]{1,0:T(8,128)S(1)} %get-tuple-element.33.aux_ref, bf16[16,512,256]{2,1,0:T(8,128)(2,1)} %get-tuple-element.49.mine_ref, bf16[16,512,256]{2,1,0:T(8,128)(2,1)} %get-tuple-element.50.other_ref, f32[64,32,128]{2,1,0:T(8,128)S(1)} %copy-done, ...), custom_call_target="tpu_custom_call" | custom-call | tf_op jit(solution)/shard_map/pallas_call | solution.py:261
  172.9 27.9 %all_to_all.26.got_ref = f32[32,32,128]{2,1,0:T(8,128)S(1)} all-to-all(f32[32,32,128]{2,1,0:T(8,128)S(1)} %shard_map.106), channel_id=1, replica_groups=mesh['x'=4,'core'=2,'z'=16,'y'=4] {'x','core','y'}, dimensions={0} | all-to-all | bytes 1048576 | tf_op jit(solution)/shard_map/all_to_all | solution.py:366
  200.8 0.0 copy-done.7
  200.8 0.0 copy-done.9
  200.8 0.0 copy-done.11
  200.8 1.3 shard_map.107
  (3 shorter events, 0.0 us)
Async XLA Ops:
  7.2 111.1 %all-gather.5.cloned.1.call-start = ((), (), s32[]{:S(2)}) async-start(), calls=%async_computation.6 | async-start | bytes 1114112 | tf_op jit(solution)/shard_map/all_gather | solution.py:335
  7.3 0.8 copy-start.2
  8.1 0.8 copy-start.3
  8.8 0.7 copy-start.4
  9.5 0.7 copy-start.6
  10.2 0.7 copy-start.8
  10.9 0.7 copy-start.10
  11.6 0.7 copy-start.12
  23.4 137.0 %all-gather.3.cloned.1.call-start = ((), (), s32[]{:S(2)}) async-start(), calls=%async_computation.5 | async-start | bytes 1114112 | tf_op jit(solution)/shard_map/all_gather | solution.py:337
  99.8 18.5 %collective-permute-start = (bf16[16,512,256]{2,1,0:T(8,128)(2,1)}, bf16[16,512,256]{2,1,0:T(8,128)(2,1)}, u32[]{:S(2)}, u32[]{:S(2)}) collective-permute-start(bf16[16,512,256]{2,1,0:T(8,128)(2,1)} %param.5), channel_id=1, source_target_pairs={{0,64},{64,0},{1,65},{65,1},{2,66},{66,2},{3,67},{67,3},{4,68},{68... | collective-permute-start | bytes 12582920 | tf_op jit(solution)/shard_map/cond/branch_1_fun/ppermute | solution.py:333
  118.3 1.2 copy-start.1
  119.5 41.0 %copy-start.5 = (f32[1,1024]{1,0:T(1,128)S(1)}, f32[1,1024]{1,0:T(1,128)}, u32[]{:S(2)}) copy-start(f32[1,1024]{1,0:T(1,128)} %param.21) | copy-start | bytes 12292
  130.0 30.5 %all-to-all-start.3 = ((f32[4,16,128]{2,1,0:T(8,128)}), f32[4,16,128]{2,1,0:T(8,128)S(1)}, u32[]{:S(2)}, u32[]{:S(2)}) async-start(f32[4,16,128]{2,1,0:T(8,128)} %get-tuple-element.39), calls=%async_computation.3 | async-start | bytes 65536 | tf_op jit(solution)/shard_map/all_to_all | solution.py:351
  160.4 1.2 copy-start
  161.7 39.1 %copy-start.7 = (s32[1024]{0:T(1024)S(1)}, s32[1024]{0:T(1024)}, u32[]{:S(2)}) copy-start(s32[1024]{0:T(1024)} %param.18) | copy-start | bytes 12292
  161.7 39.1 %copy-start.9 = (f32[1024]{0:T(1024)S(1)}, f32[1024]{0:T(1024)}, u32[]{:S(2)}) copy-start(f32[1024]{0:T(1024)} %param.19) | copy-start | bytes 12292
  161.7 39.1 %copy-start.11 = (f32[1024]{0:T(1024)S(1)}, f32[1024]{0:T(1024)}, u32[]{:S(2)}) copy-start(f32[1024]{0:T(1024)} %param.20) | copy-start | bytes 12292
Sparse Core Ops, SparseCore 0:
  23.6 69.8 all-gather.4
  95.5 64.8 all-gather.2

commit v4 on v3

--- a/solution.py
+++ b/solution.py
@@ -11,7 +11,7 @@
 ROWS = 32
 COLS = 256
 SCEN = 64
-PARTS = 32
+PARTS = 24
 
 penalty = 1.0
 stride = 0.5
@@ -77,11 +77,10 @@
         packed_ref[q, 0:ROWS, :] = both
         packed_ref[q, ROWS : ROWS + 8, :] = base
         packed_ref[q, ROWS + 8 : ROWS + 16, :] = index.astype(f32)
-        packed_ref[q, ROWS + 16 : ROWS + 32, :] = jnp.broadcast_to(as_row, (16, 128))
-
-
-def spread_z_kernel(place_ref, transship_ref, packed_ref, spread_ref, parts_ref):
-    parts_ref[...] = packed_ref[:, ROWS:, :]
+        packed_ref[q, ROWS + 16 : ROWS + 24, :] = jnp.broadcast_to(as_row, (8, 128))
+
+
+def spread_z_kernel(place_ref, packed_ref, transship_ref, spread_ref):
     at = pl.ds(pl.multiple_of(place_ref[3] * COLS, COLS), COLS)
     block = transship_ref[:, at]
     for z in range(Z):
@@ -128,11 +127,11 @@
 
 
 def first_kernel(
-    place_ref, aux_ref, mine_ref, other_ref, sites_ref, rec_ref, short_ref, pull_ref, grad_ref, rounded_ref
+    place_ref, aux_ref, mine_ref, other_ref, packed_ref, rec_ref, short_ref, pull_ref, grad_ref, rounded_ref
 ):
     def load(b, carry):
         at = pl.ds(pl.multiple_of(b * ROWS, ROWS), ROWS)
-        both = sites_ref[b]
+        both = packed_ref[b, 0:ROWS, :]
         rec_ref[at, :] = both
         rounded_ref[at, :] = both.astype(jnp.bfloat16)
         short_ref[at, :] = pltpu.roll(both, SCEN, 1)
@@ -153,7 +152,7 @@
     aux_ref,
     mine_ref,
     other_ref,
-    parts_ref,
+    packed_ref,
     rec_in_ref,
     short_in_ref,
     pulled_ref,
@@ -171,10 +170,10 @@
 
     def load(b, carry):
         at = pl.ds(pl.multiple_of(b * ROWS, ROWS), ROWS)
-        index = parts_ref[b, 8:16, :]
+        index = packed_ref[b, ROWS + 8 : ROWS + 16, :]
         pull = pick(pull_ref[0, pl.ds(b // Y, 1), :], index.astype(jnp.int32) + b % Y * ROWS)
-        stock = jnp.maximum(parts_ref[b, 0:8, :] + learn_rate * pull, 0.0)
-        change = jnp.where(eye, -parts_ref[b, 16:17, :], 0.0)
+        stock = jnp.maximum(packed_ref[b, ROWS : ROWS + 8, :] + learn_rate * pull, 0.0)
+        change = jnp.where(eye, -packed_ref[b, ROWS + 16 : ROWS + 17, :], 0.0)
         for k in range(8):
             change = change + jnp.where(index[k : k + 1] == site, stock[k : k + 1], 0.0)
         rec = rec_in_ref[at, :]
@@ -307,23 +306,23 @@
         place,
         *raw,
         hbm=len(raw),
+        vmem_mib=60,
     )
     packed = lax.all_to_all(packed, "y", 0, 0, tiled=True)
-    sites = packed[:, :ROWS]
-
     bf16 = jnp.bfloat16
     always = column * COLS >= 0
 
     def spread_z(transship, packed):
-        block, parts = run_kernel(
+        (block,) = run_kernel(
             spread_z_kernel,
-            [jax.ShapeDtypeStruct((Z, ROWS, COLS), bf16), (Y, PARTS, 128)],
+            [jax.ShapeDtypeStruct((Z, ROWS, COLS), bf16)],
             [],
             place,
+            packed,
             transship,
-            packed,
+            hbm=1,
         )
-        return lax.all_to_all(block, "z", 0, 0, tiled=True).reshape(Z * ROWS, COLS), parts
+        return lax.all_to_all(block, "z", 0, 0, tiled=True).reshape(Z * ROWS, COLS)
 
     def spread_xy(along_z):
         spread = jnp.broadcast_to(along_z[None], (X * Y, Z * ROWS, COLS))
@@ -332,9 +331,8 @@
     def swap_cores(mine):
         return lax.ppermute(mine, "core", [(0, 1), (1, 0)])
 
-    sites = lax.all_gather(sites, "z", axis=0, tiled=True)
-    along_z, parts = one_block(always, spread_z, transship, packed)
-    parts = lax.all_gather(parts, "z", axis=0, tiled=True)
+    gathered = lax.all_gather(packed, "z", axis=0, tiled=True)
+    along_z = one_block(always, spread_z, transship, packed)
     mine = one_block(always, spread_xy, along_z)
     other = one_block(always, swap_cores, mine)
 
@@ -346,7 +344,7 @@
         aux,
         mine,
         other,
-        sites,
+        gathered,
     )
     pull1 = lax.all_to_all(pull1, "y", 0, 0, tiled=True)
     (send,) = run_kernel(
@@ -357,7 +355,7 @@
         aux,
         mine,
         other,
-        parts,
+        gathered,
         rec,
         short,
         pull1,

time: 210 us -> 168 us (0.80)
  waiting for transfers between devices: 34.3 us -> 7.12 us
  local copies, waits for them, and re-layouts: 8.43 us -> 1.93 us
  blocking collectives: 112 us -> 107 us
  starting transfers between devices: 14.7 us -> 11.2 us
    all_gather x2 -> x1, waiting for transfers between devices: 27.2 us -> 0.01 us  [per_device(): gathered = lax.all_gather(packed, 'z', axis=0, tiled=True)]
    all_to_all x1, blocking collectives: 27.9 us -> 15.8 us  [per_device(): got = lax.all_to_all(send, ('x', 'core', 'y'), 0, 0, tiled=True)]
    all_to_all x1 -> x2, blocking collectives: 27.5 us -> 34.2 us  [the longest x1 27.5 us: spread_z(): return lax.all_to_all(block, 'z', 0, 0, tiled=True).reshape(Z * ROWS, COLS)]
    unnamed x26 -> x16, local copies, waits for them, and re-layouts: 7.41 us -> 1.53 us
    all_to_all x1 -> x0, starting transfers between devices: 3.26 us -> none  [per_device(): pull1 = lax.all_to_all(pull1, 'y', 0, 0, tiled=True)]
  transfers between devices with their start and end apart: 4 -> 2, of which waited for: 2 -> 1; matrix products, arithmetic and copies ran while one was open for 0% -> 0% of each run, Pallas kernels for 6% -> 1%
where the time goes in v4:
time: 168 us; the launch traced here: 166 us
  blocking collectives  107 us (64%)
  Pallas kernels  24.2 us (14%)
  between operations  14.1 us (8%)
  starting transfers between devices  11.2 us (7%)
  waiting for transfers between devices  7.12 us (4%)
  local copies, waits for them, and re-layouts  1.93 us (1%)
    all_to_all x1, blocking collectives, spread_xy(): return lax.all_to_all(spread, ('x', 'y'), 0, 0, tiled=True)  47.3 us
    all_to_all x1, blocking collectives, spread_z(): return lax.all_to_all(block, 'z', 0, 0, tiled=True).reshape(Z * ROWS, COLS)  27.5 us
    pallas_call x5, Pallas kernels, run_kernel(): pl.pallas_call(kernel, out_shape=outs, in_specs=[pl.BlockSpec(memory_spac...  24.2 us
    all_to_all x1, blocking collectives, per_device(): got = lax.all_to_all(send, ('x', 'core', 'y'), 0, 0, tiled=True)  15.8 us
    ppermute x1, starting transfers between devices, swap_cores(): return lax.ppermute(mine, 'core', [(0, 1), (1, 0)])  11.2 us
    all_to_all x1, blocking collectives, per_device(): packed = lax.all_to_all(packed, 'y', 0, 0, tiled=True)  9.87 us
    ppermute x1, waiting for transfers between devices, swap_cores(): return lax.ppermute(mine, 'core', [(0, 1), (1, 0)])  7.11 us
    all_to_all x1, blocking collectives, per_device(): pull1 = lax.all_to_all(pull1, 'y', 0, 0, tiled=True)  6.65 us
  transfers between devices with their start and end apart: 2, of which 1 were waited for; matrix products, arithmetic and copies ran while one was open for 0% of the time, Pallas kernels for 1%

profile of v4, /device:TPU:1, one launch (start us, length us, event | category | flops | bytes accessed | tf_op | source)
XLA Modules:
  0.0 165.8 jit_solution(2027378751347192495)
XLA Ops:
  7.2 0.0 all-gather.2.cloned.1.call-start
  7.2 0.1 pad_add_fusion.place_ref
  7.3 2.2 %shard_map.104 = (f32[4,56,128]{2,1,0:T(8,128)}, f32[16,128]{1,0:T(8,128)}) custom-call(s32[4]{0:T(128)S(1)} %pad_add_fusion.place_ref, s32[32,256]{1,0:T(8,128)} %refs_0_.1, f32[32,256]{1,0:T(8,128)} %refs_1_.1, s32[2,128]{1,0:T(2,128)} %bitcast.21, s32[8,128]{1,0:T(8,128)} %bitcast.14, f32[8,128]{1,0:T(8,128)} %bitcast.16, f32[8,128]{1,0:T(8,128)} %bitcast.18, ...), custom_call_target="tpu_custom_call" | custom-call | tf_op jit(solution)/shard_map/pallas_call | solution.py:260
  9.5 9.9 %all_to_all.25 = f32[4,56,128]{2,1,0:T(8,128)} all-to-all(f32[4,56,128]{2,1,0:T(8,128)} %get-tuple-element.32), channel_id=1, replica_groups=mesh['x'=4,'core'=2,'z'=16,'y'=4] {'y'}, dimensions={0} | all-to-all | bytes 229376 | tf_op jit(solution)/shard_map/all_to_all | solution.py:311
  19.4 0.0 all-gather.2.cloned.1.call-update
  19.4 28.5 %conditional.3 = (bf16[512,256]{1,0:T(8,128)(2,1)S(1)}) conditional(s32[]{:T(128)} %convert_element_type.2, () %tuple.27, (s32[4]{0:T(128)S(1)}, f32[4,56,128]{2,1,0:T(8,128)}, bf16[32,2048]{1,0:T(8,128)(2,1)}) %tuple.28), branch_computations={%region_0.0_spmd, %region_1.0_spmd} | conditional | bytes 524296 | solution.py:278
  19.4 0.9 branch_1_fun.1
  20.4 27.5 %all_to_all.23 = bf16[16,32,256]{2,1,0:T(8,128)(2,1)S(1)} all-to-all(bf16[16,32,256]{2,1,0:T(8,128)(2,1)S(1)} %branch_1_fun.1), channel_id=1, replica_groups=mesh['x'=4,'core'=2,'z'=16,'y'=4] {'z'}, dimensions={0} | all-to-all | bytes 524288 | tf_op jit(solution)/shard_map/cond/branch_1_fun/all_to_all | solution.py:325
  47.9 47.7 %conditional.4 = (bf16[16,512,256]{2,1,0:T(8,128)(2,1)}) conditional(s32[]{:T(128)} %convert_element_type.2, () %tuple.26, bf16[512,256]{1,0:T(8,128)(2,1)S(1)} %get-tuple-element.41), branch_computations={%region_2.0_spmd, %region_3.0_spmd} | conditional | bytes 12845064 | solution.py:278
  47.9 0.4 broadcast_in_dim.0
  48.3 47.3 %all_to_all.24 = bf16[16,512,256]{2,1,0:T(8,128)(2,1)} all-to-all(bf16[16,512,256]{2,1,0:T(8,128)(2,1)S(1)} %broadcast_in_dim.0), channel_id=1, replica_groups=mesh['x'=4,'core'=2,'z'=16,'y'=4] {'x','y'}, dimensions={0} | all-to-all | bytes 8388608 | tf_op jit(solution)/shard_map/cond/branch_1_fun/all_to_all | solution.py:329
  95.5 0.0 copy-start.2
  95.5 18.3 %conditional.5 = (bf16[16,512,256]{2,1,0:T(8,128)(2,1)}) conditional(s32[]{:T(128)} %convert_element_type.2, () %tuple.29, bf16[16,512,256]{2,1,0:T(8,128)(2,1)} %get-tuple-element.42.mine_ref), branch_computations={%region_4.0_spmd, %region_5.0_spmd} | conditional | bytes 16777264 | solution.py:278
  95.5 11.2 %collective-permute-start = (bf16[16,512,256]{2,1,0:T(8,128)(2,1)}, bf16[16,512,256]{2,1,0:T(8,128)(2,1)}, u32[]{:S(2)}, u32[]{:S(2)}) collective-permute-start(bf16[16,512,256]{2,1,0:T(8,128)(2,1)} %param.5), channel_id=1, source_target_pairs={{0,64},{64,0},{1,65},{65,1},{2,66},{66,2},{3,67},{67,3},{4,68},{68... | collective-permute-start | bytes 12582920 | tf_op jit(solution)/shard_map/cond/branch_1_fun/ppermute | solution.py:332
  106.7 7.1 %collective-permute-done = bf16[16,512,256]{2,1,0:T(8,128)(2,1)} collective-permute-done((bf16[16,512,256]{2,1,0:T(8,128)(2,1)}, bf16[16,512,256]{2,1,0:T(8,128)(2,1)}, u32[]{:S(2)}, u32[]{:S(2)}) %collective-permute-start) | collective-permute-done | bytes 4194336 | tf_op jit(solution)/shard_map/cond/branch_1_fun/ppermute | solution.py:332
  113.8 0.0 all-gather.2.cloned.1.call-done.packed_ref
  113.8 0.0 copy-done.2
  113.8 0.0 copy-start
  113.8 1.5 copy-done
  115.3 0.0 copy-start.1
  115.3 0.0 copy-start.3
  115.3 0.0 copy-start.7
  115.3 9.9 %shard_map.105 = (f32[2048,128]{1,0:T(8,128)S(1)}, f32[2048,128]{1,0:T(8,128)S(1)}, f32[4,16,128]{2,1,0:T(8,128)S(1)}) custom-call(s32[4]{0:T(128)S(1)} %pad_add_fusion.place_ref, f32[16,128]{1,0:T(8,128)S(1)} %copy-done.2, bf16[16,512,256]{2,1,0:T(8,128)(2,1)} %get-tuple-element.42.mine_ref, bf16[16,512,256]{2,1,0:T(8,128)(2,1)} %get-tuple-element.43.other_ref, ...), custom_call_target="tpu_custom_call" | custom-call | tf_op jit(solution)/shard_map/pallas_call | solution.py:260
  125.2 6.7 %all_to_all.26.pulled_ref = f32[4,16,128]{2,1,0:T(8,128)S(1)} all-to-all(f32[4,16,128]{2,1,0:T(8,128)S(1)} %get-tuple-element.35), channel_id=1, replica_groups=mesh['x'=4,'core'=2,'z'=16,'y'=4] {'y'}, dimensions={0} | all-to-all | bytes 65536 | tf_op jit(solution)/shard_map/all_to_all | solution.py:349
  131.9 0.0 copy-done.1
  131.9 0.0 copy-done.3
  131.9 0.0 copy-done.7
  131.9 0.0 copy-start.4
  131.9 0.0 copy-start.5
  131.9 0.0 copy-start.6
  131.9 9.9 %shard_map.106 = f32[32,32,128]{2,1,0:T(8,128)S(1)} custom-call(s32[4]{0:T(128)S(1)} %pad_add_fusion.place_ref, f32[16,128]{1,0:T(8,128)S(1)} %copy-done.2, bf16[16,512,256]{2,1,0:T(8,128)(2,1)S(1)} %copy-done.7, bf16[16,512,256]{2,1,0:T(8,128)(2,1)} %get-tuple-element.43.other_ref, f32[64,56,128]{2,1,0:T(8,128)S(1)} %copy-done.1, ...), custom_call_target="tpu_custom_call" | custom-call | tf_op jit(solution)/shard_map/pallas_call | solution.py:260
  141.8 15.8 %all_to_all.27.got_ref = f32[32,32,128]{2,1,0:T(8,128)S(1)} all-to-all(f32[32,32,128]{2,1,0:T(8,128)S(1)} %shard_map.106), channel_id=1, replica_groups=mesh['x'=4,'core'=2,'z'=16,'y'=4] {'x','core','y'}, dimensions={0} | all-to-all | bytes 1048576 | tf_op jit(solution)/shard_map/all_to_all | solution.py:364
  157.6 0.0 copy-done.4
  157.6 0.0 copy-done.5
  157.7 0.0 copy-done.6
  157.7 1.3 shard_map.107
Async XLA Ops:
  7.2 106.7 %all-gather.2.cloned.1.call-start = ((), (), s32[]{:S(2)}) async-start(), calls=%async_computation.5 | async-start | bytes 1949696 | tf_op jit(solution)/shard_map/all_gather | solution.py:334
  95.5 18.3 %copy-start.2 = (f32[16,128]{1,0:T(8,128)S(1)}, f32[16,128]{1,0:T(8,128)}, u32[]{:S(2)}) copy-start(f32[16,128]{1,0:T(8,128)} %get-tuple-element.31.aux_ref) | copy-start | bytes 24580
  95.5 18.3 %collective-permute-start = (bf16[16,512,256]{2,1,0:T(8,128)(2,1)}, bf16[16,512,256]{2,1,0:T(8,128)(2,1)}, u32[]{:S(2)}, u32[]{:S(2)}) collective-permute-start(bf16[16,512,256]{2,1,0:T(8,128)(2,1)} %param.5), channel_id=1, source_target_pairs={{0,64},{64,0},{1,65},{65,1},{2,66},{66,2},{3,67},{67,3},{4,68},{68... | collective-permute-start | bytes 12582920 | tf_op jit(solution)/shard_map/cond/branch_1_fun/ppermute | solution.py:332
  113.8 1.5 copy-start
  115.3 16.5 %copy-start.1 = (f32[64,56,128]{2,1,0:T(8,128)S(1)}, f32[64,56,128]{2,1,0:T(8,128)}, u32[]{:S(2)}) copy-start(f32[64,56,128]{2,1,0:T(8,128)} %all-gather.2.cloned.1.call-done.packed_ref) | copy-start | bytes 5505028
  115.3 16.5 %copy-start.3 = (f32[1,1024]{1,0:T(1,128)S(1)}, f32[1,1024]{1,0:T(1,128)}, u32[]{:S(2)}) copy-start(f32[1,1024]{1,0:T(1,128)} %param.21) | copy-start | bytes 12292
  115.3 16.5 %copy-start.7 = (bf16[16,512,256]{2,1,0:T(8,128)(2,1)S(1)}, bf16[16,512,256]{2,1,0:T(8,128)(2,1)}, u32[]{:S(2)}) copy-start(bf16[16,512,256]{2,1,0:T(8,128)(2,1)} %get-tuple-element.42.mine_ref) | copy-start | bytes 12582916
  131.9 25.8 %copy-start.4 = (s32[1024]{0:T(1024)S(1)}, s32[1024]{0:T(1024)}, u32[]{:S(2)}) copy-start(s32[1024]{0:T(1024)} %param.18) | copy-start | bytes 12292
  131.9 25.8 %copy-start.5 = (f32[1024]{0:T(1024)S(1)}, f32[1024]{0:T(1024)}, u32[]{:S(2)}) copy-start(f32[1024]{0:T(1024)} %param.19) | copy-start | bytes 12292
  131.9 25.8 %copy-start.6 = (f32[1024]{0:T(1024)S(1)}, f32[1024]{0:T(1024)}, u32[]{:S(2)}) copy-start(f32[1024]{0:T(1024)} %param.20) | copy-start | bytes 12292
Sparse Core Ops, SparseCore 0:
  19.5 73.4 all-gather.1

commit v5 on v4

--- a/solution.py
+++ b/solution.py
@@ -12,6 +12,7 @@
 COLS = 256
 SCEN = 64
 PARTS = 24
+MIDDLE = Z + Z * 16 + Z
 
 penalty = 1.0
 stride = 0.5
@@ -74,10 +75,10 @@
             both = jnp.where(low, rec, pltpu.roll(short, SCEN, 1))
         else:
             both = jnp.where(low, pltpu.roll(rec, SCEN, 1), short)
-        packed_ref[q, 0:ROWS, :] = both
-        packed_ref[q, ROWS : ROWS + 8, :] = base
-        packed_ref[q, ROWS + 8 : ROWS + 16, :] = index.astype(f32)
-        packed_ref[q, ROWS + 16 : ROWS + 24, :] = jnp.broadcast_to(as_row, (8, 128))
+        packed_ref[q * ROWS : (q + 1) * ROWS, :] = both
+    packed_ref[Y * ROWS : Y * ROWS + 8, :] = base
+    packed_ref[Y * ROWS + 8 : Y * ROWS + 16, :] = index.astype(f32)
+    packed_ref[Y * ROWS + 16 : Y * ROWS + 24, :] = jnp.broadcast_to(as_row, (8, 128))
 
 
 def spread_z_kernel(place_ref, packed_ref, transship_ref, spread_ref):
@@ -126,12 +127,45 @@
         put(z, jnp.sum(gap.T, axis=0, keepdims=True))
 
 
+def arrange_kernel(place_ref, gathered_ref, sites_ref, parts_ref, sums_ref, padded_ref, sems):
+    started = [
+        pltpu.make_async_copy(
+            gathered_ref.at[:, pl.ds(q * ROWS, ROWS), :], sites_ref.at[q], sems.at[q]
+        )
+        for q in range(Y)
+    ]
+    start = Y * ROWS
+    started.append(
+        pltpu.make_async_copy(gathered_ref.at[:, pl.ds(start, 16), :], parts_ref, sems.at[Y])
+    )
+    started.append(
+        pltpu.make_async_copy(gathered_ref.at[:, pl.ds(start + 16, 8), :], padded_ref, sems.at[Y + 1])
+    )
+    for copy in started:
+        copy.start()
+    for copy in started:
+        copy.wait()
+    for z in range(Z):
+        sums_ref[z : z + 1, :] = padded_ref[z, 0:1, :]
+
+
 def first_kernel(
-    place_ref, aux_ref, mine_ref, other_ref, packed_ref, rec_ref, short_ref, pull_ref, grad_ref, rounded_ref
+    place_ref,
+    aux_ref,
+    mine_ref,
+    other_ref,
+    sites_ref,
+    parts_ref,
+    sums_ref,
+    rec_ref,
+    short_ref,
+    middle_ref,
+    grad_ref,
+    rounded_ref,
 ):
     def load(b, carry):
         at = pl.ds(pl.multiple_of(b * ROWS, ROWS), ROWS)
-        both = packed_ref[b, 0:ROWS, :]
+        both = sites_ref[b % Y, b // Y]
         rec_ref[at, :] = both
         rounded_ref[at, :] = both.astype(jnp.bfloat16)
         short_ref[at, :] = pltpu.roll(both, SCEN, 1)
@@ -142,9 +176,12 @@
 
     def put(z, row):
         for q in range(Y):
-            pull_ref[q, z : z + 1, :] = row
+            middle_ref[q, z : z + 1, :] = row
+            middle_ref[q, Z + z * 16 : Z + z * 16 + 16, :] = parts_ref[z]
 
     pull_sums(aux_ref[0:1, :], rec_ref, short_ref, put)
+    for q in range(Y):
+        middle_ref[q, MIDDLE - Z : MIDDLE, :] = sums_ref[...]
 
 
 def second_kernel(
@@ -152,10 +189,9 @@
     aux_ref,
     mine_ref,
     other_ref,
-    packed_ref,
+    middle_ref,
     rec_in_ref,
     short_in_ref,
-    pulled_ref,
     mult_ref,
     send_ref,
     rec_ref,
@@ -164,16 +200,18 @@
     grad_ref,
     rounded_ref,
 ):
-    pull_ref[0] = pulled_ref[0] + pulled_ref[1] + pulled_ref[2] + pulled_ref[3]
+    pull_ref[0] = middle_ref[0, 0:Z] + middle_ref[1, 0:Z] + middle_ref[2, 0:Z] + middle_ref[3, 0:Z]
     eye = lanes_of((ROWS, 128)) == rows_of((ROWS, 128))
     site = rows_of((ROWS, 128)).astype(f32)
 
     def load(b, carry):
         at = pl.ds(pl.multiple_of(b * ROWS, ROWS), ROWS)
-        index = packed_ref[b, ROWS + 8 : ROWS + 16, :]
-        pull = pick(pull_ref[0, pl.ds(b // Y, 1), :], index.astype(jnp.int32) + b % Y * ROWS)
-        stock = jnp.maximum(packed_ref[b, ROWS : ROWS + 8, :] + learn_rate * pull, 0.0)
-        change = jnp.where(eye, -packed_ref[b, ROWS + 16 : ROWS + 17, :], 0.0)
+        z, y = b // Y, b % Y
+        start = pl.multiple_of(Z + z * 16, 8)
+        index = middle_ref[y, pl.ds(start + 8, 8), :]
+        pull = pick(pull_ref[0, pl.ds(z, 1), :], index.astype(jnp.int32) + y * ROWS)
+        stock = jnp.maximum(middle_ref[y, pl.ds(start, 8), :] + learn_rate * pull, 0.0)
+        change = jnp.where(eye, -middle_ref[y, pl.ds(MIDDLE - Z + z, 1), :], 0.0)
         for k in range(8):
             change = change + jnp.where(index[k : k + 1] == site, stock[k : k + 1], 0.0)
         rec = rec_in_ref[at, :]
@@ -254,7 +292,7 @@
         rec_ref[16:32, tile] = jnp.where(low, pltpu.roll(even, SCEN, 1), odd)
 
 
-def run_kernel(kernel, outs, scratch, *args, hbm=0, vmem_mib=16):
+def run_kernel(kernel, outs, scratch, *args, hbm=0, vmem_mib=16, flops=0):
     vmem = pl.BlockSpec(memory_space=pltpu.VMEM)
     outs = [out if isinstance(out, jax.ShapeDtypeStruct) else jax.ShapeDtypeStruct(out, f32) for out in outs]
     return pl.pallas_call(
@@ -265,6 +303,7 @@
         + [vmem] * (len(args) - 1 - hbm),
         out_specs=[vmem] * len(outs),
         scratch_shapes=[pltpu.VMEM(*entry) if isinstance(entry, tuple) else entry for entry in scratch],
+        cost_estimate=pl.CostEstimate(flops=flops, bytes_accessed=0, transcendentals=0) if flops else None,
         compiler_params=pltpu.CompilerParams(vmem_limit_bytes=vmem_mib * 1024 * 1024),
     )(*args)
 
@@ -301,14 +340,13 @@
     )
     packed, aux = run_kernel(
         prep_kernel,
-        [(Y, ROWS + PARTS, 128), (16, 128)],
+        [(Y * ROWS + PARTS, 128), (16, 128)],
         [(entry.shape, entry.dtype) for entry in raw] + [pltpu.SemaphoreType.DMA((7,))],
         place,
         *raw,
         hbm=len(raw),
         vmem_mib=60,
     )
-    packed = lax.all_to_all(packed, "y", 0, 0, tiled=True)
     bf16 = jnp.bfloat16
     always = column * COLS >= 0
 
@@ -328,25 +366,38 @@
         spread = jnp.broadcast_to(along_z[None], (X * Y, Z * ROWS, COLS))
         return lax.all_to_all(spread, ("x", "y"), 0, 0, tiled=True)
 
-    def swap_cores(mine):
-        return lax.ppermute(mine, "core", [(0, 1), (1, 0)])
-
-    gathered = lax.all_gather(packed, "z", axis=0, tiled=True)
+    gathered = lax.all_gather(packed, "z", axis=0)
     along_z = one_block(always, spread_z, transship, packed)
     mine = one_block(always, spread_xy, along_z)
-    other = one_block(always, swap_cores, mine)
-
-    rec, short, pull1 = run_kernel(
+    sites, parts, sums = run_kernel(
+        arrange_kernel,
+        [(Y, Z, ROWS, 128), (Z, 16, 128), (Z, 128)],
+        [((Z, 8, 128), f32), pltpu.SemaphoreType.DMA((Y + 2,))],
+        place,
+        gathered,
+        hbm=1,
+        vmem_mib=16,
+        flops=0,
+    )
+
+    def exchange(mine, sites):
+        other = lax.ppermute(mine, "core", [(0, 1), (1, 0)])
+        return other, lax.all_to_all(sites, "y", 0, 0, tiled=True)
+
+    other, sites = one_block(always, exchange, mine, sites)
+    rec, short, middle = run_kernel(
         first_kernel,
-        [wide, wide, (Y, Z, 128)],
-        [(wide, f32), (wide, jnp.bfloat16)],
+        [wide, wide, (Y, MIDDLE, 128)],
+        [(wide, f32), (wide, bf16)],
         place,
         aux,
         mine,
         other,
-        gathered,
-    )
-    pull1 = lax.all_to_all(pull1, "y", 0, 0, tiled=True)
+        sites,
+        parts,
+        sums,
+    )
+    middle = lax.all_to_all(middle, "y", 0, 0, tiled=True)
     (send,) = run_kernel(
         second_kernel,
         [(GROUPS * Y, 32, 128)],
@@ -355,10 +406,9 @@
         aux,
         mine,
         other,
-        gathered,
+        middle,
         rec,
         short,
-        pull1,
         mult_init,
     )
     got = lax.all_to_all(send, ("x", "core", "y"), 0, 0, tiled=True)

time: 168 us -> 179 us (1.065)
  the two profiles are of different devices: /device:TPU:1 before, /device:TPU:32 now
where the time goes in v5:
time: 179 us; the launch traced here: 178 us
  blocking collectives  135 us (75%)
  Pallas kernels  25 us (14%)
  between operations  14.1 us (8%)
  starting transfers between devices  1.96 us (1%)
    all_to_all x1, blocking collectives, spread_xy(): return lax.all_to_all(spread, ('x', 'y'), 0, 0, tiled=True)  55.8 us
    all_to_all x1, blocking collectives, spread_z(): return lax.all_to_all(block, 'z', 0, 0, tiled=True).reshape(Z * ROWS, COLS)  33.7 us
    pallas_call x6, Pallas kernels, run_kernel(): pl.pallas_call(kernel, out_shape=outs, in_specs=[pl.BlockSpec(memory_spac...  25 us
    all_to_all x1, blocking collectives, exchange(): return (other, lax.all_to_all(sites, 'y', 0, 0, tiled=True))  18.5 us
    all_to_all x1, blocking collectives, per_device(): got = lax.all_to_all(send, ('x', 'core', 'y'), 0, 0, tiled=True)  15 us
    all_to_all x1, blocking collectives, per_device(): middle = lax.all_to_all(middle, 'y', 0, 0, tiled=True)  12.4 us
  transfers between devices with their start and end apart: 2, of which 0 were waited for; matrix products, arithmetic and copies ran while one was open for 0% of the time, Pallas kernels for 1%

profile of v5, /device:TPU:32, one launch (start us, length us, event | category | flops | bytes accessed | tf_op | source)
XLA Modules:
  0.0 178.2 jit_solution(16082033330472983808)
XLA Ops:
  7.2 0.0 all-gather.3.cloned.1.call-start
  7.2 0.1 pad_add_fusion.place_ref
  7.3 2.2 %shard_map.104 = (f32[152,128]{1,0:T(8,128)}, f32[16,128]{1,0:T(8,128)}) custom-call(s32[4]{0:T(128)S(1)} %pad_add_fusion.place_ref, s32[32,256]{1,0:T(8,128)} %refs_0_.1, f32[32,256]{1,0:T(8,128)} %refs_1_.1, s32[2,128]{1,0:T(2,128)} %bitcast.23, s32[8,128]{1,0:T(8,128)} %bitcast.16, f32[8,128]{1,0:T(8,128)} %bitcast.18, f32[8,128]{1,0:T(8,128)} %bitcast.20, ...), custom_call_target="tpu_custom_call" | custom-call | tf_op jit(solution)/shard_map/pallas_call | solution.py:298
  9.5 0.0 all-gather.3.cloned.1.call-update
  9.5 34.7 %conditional.3 = (bf16[512,256]{1,0:T(8,128)(2,1)S(1)}) conditional(s32[]{:T(128)} %convert_element_type.2, () %tuple.29, (s32[4]{0:T(128)S(1)}, f32[152,128]{1,0:T(8,128)}, bf16[32,2048]{1,0:T(8,128)(2,1)}) %tuple.30), branch_computations={%region_0.0_spmd, %region_1.0_spmd} | conditional | bytes 524296 | solution.py:317
  9.5 0.9 branch_1_fun.1
  10.5 33.7 %all_to_all.22 = bf16[16,32,256]{2,1,0:T(8,128)(2,1)S(1)} all-to-all(bf16[16,32,256]{2,1,0:T(8,128)(2,1)S(1)} %branch_1_fun.1), channel_id=1, replica_groups=mesh['x'=4,'core'=2,'z'=16,'y'=4] {'z'}, dimensions={0} | all-to-all | bytes 524288 | tf_op jit(solution)/shard_map/cond/branch_1_fun/all_to_all | solution.py:363
  44.2 56.2 %conditional.4 = (bf16[16,512,256]{2,1,0:T(8,128)(2,1)}) conditional(s32[]{:T(128)} %convert_element_type.2, () %tuple.28, bf16[512,256]{1,0:T(8,128)(2,1)S(1)} %get-tuple-element.57), branch_computations={%region_2.0_spmd, %region_3.0_spmd} | conditional | bytes 12845064 | solution.py:317
  44.2 0.4 broadcast_in_dim.0
  44.6 55.8 %all_to_all.23 = bf16[16,512,256]{2,1,0:T(8,128)(2,1)} all-to-all(bf16[16,512,256]{2,1,0:T(8,128)(2,1)S(1)} %broadcast_in_dim.0), channel_id=1, replica_groups=mesh['x'=4,'core'=2,'z'=16,'y'=4] {'x','y'}, dimensions={0} | all-to-all | bytes 8388608 | tf_op jit(solution)/shard_map/cond/branch_1_fun/all_to_all | solution.py:367
  100.4 0.0 all-gather.3.cloned.1.call-done
  100.4 0.0 copy-start
  100.4 1.3 copy-done
  101.7 0.0 copy-start.1
  101.7 0.7 shard_map.105
  102.4 20.4 %conditional.5 = (bf16[16,512,256]{2,1,0:T(8,128)(2,1)}, f32[4,16,32,128]{3,2,1,0:T(8,128)S(1)}) conditional(s32[]{:T(128)} %convert_element_type.2, () %tuple.31, (bf16[16,512,256]{2,1,0:T(8,128)(2,1)}, f32[4,16,32,128]{3,2,1,0:T(8,128)S(1)}) %tuple.32), branch_computations={%region_4.0_spmd, %region_5.0_spmd} | conditional | bytes 18874424 | solution.py:317
  102.4 1.9 %collective-permute-start = (bf16[16,512,256]{2,1,0:T(8,128)(2,1)}, bf16[16,512,256]{2,1,0:T(8,128)(2,1)}, u32[]{:S(2)}, u32[]{:S(2)}) collective-permute-start(bf16[16,512,256]{2,1,0:T(8,128)(2,1)} %get-tuple-element.20), channel_id=1, source_target_pairs={{0,64},{64,0},{1,65},{65,1},{2,66},{66,2},{3,67},{67,3},{4,68},{68... | collective-permute-start | bytes 12582920 | tf_op jit(solution)/shard_map/cond/branch_1_fun/ppermute | solution.py:384
  104.3 18.5 %all_to_all.24 = f32[4,16,32,128]{3,2,1,0:T(8,128)S(1)} all-to-all(f32[4,16,32,128]{3,2,1,0:T(8,128)S(1)} %get-tuple-element.21), channel_id=1, replica_groups=mesh['x'=4,'core'=2,'z'=16,'y'=4] {'y'}, dimensions={0} | all-to-all | bytes 2097152 | tf_op jit(solution)/shard_map/cond/branch_1_fun/all_to_all | solution.py:385
  122.8 0.0 collective-permute-done
  122.8 0.0 copy-done.1
  122.8 0.0 copy-start.2
  122.8 0.0 copy-start.6
  122.8 9.9 %shard_map.106 = (f32[2048,128]{1,0:T(8,128)S(1)}, f32[2048,128]{1,0:T(8,128)S(1)}, f32[4,288,128]{2,1,0:T(8,128)S(1)}) custom-call(s32[4]{0:T(128)S(1)} %pad_add_fusion.place_ref, f32[16,128]{1,0:T(8,128)S(1)} %copy-done.1, bf16[16,512,256]{2,1,0:T(8,128)(2,1)} %get-tuple-element.58.mine_ref, bf16[16,512,256]{2,1,0:T(8,128)(2,1)} %get-tuple-element.41.other_ref, ...), custom_call_target="tpu_custom_call" | custom-call | tf_op jit(solution)/shard_map/pallas_call | solution.py:298
  132.8 12.4 %all_to_all.25.middle_ref = f32[4,288,128]{2,1,0:T(8,128)S(1)} all-to-all(f32[4,288,128]{2,1,0:T(8,128)S(1)} %get-tuple-element.45), channel_id=1, replica_groups=mesh['x'=4,'core'=2,'z'=16,'y'=4] {'y'}, dimensions={0} | all-to-all | bytes 1179648 | tf_op jit(solution)/shard_map/all_to_all | solution.py:400
  145.2 0.0 copy-done.2
  145.2 0.0 copy-done.6
  145.2 0.0 copy-start.3
  145.2 0.0 copy-start.4
  145.2 0.0 copy-start.5
  145.2 9.9 %shard_map.107 = f32[32,32,128]{2,1,0:T(8,128)S(1)} custom-call(s32[4]{0:T(128)S(1)} %pad_add_fusion.place_ref, f32[16,128]{1,0:T(8,128)S(1)} %copy-done.1, bf16[16,512,256]{2,1,0:T(8,128)(2,1)S(1)} %copy-done.6, bf16[16,512,256]{2,1,0:T(8,128)(2,1)} %get-tuple-element.41.other_ref, f32[4,288,128]{2,1,0:T(8,128)S(1)} %all_to_all.25.middle_ref, ...), custom_call_target="tpu_custom_call" | custom-call | tf_op jit(solution)/shard_map/pallas_call | solution.py:298
  155.1 15.0 %all_to_all.26.got_ref = f32[32,32,128]{2,1,0:T(8,128)S(1)} all-to-all(f32[32,32,128]{2,1,0:T(8,128)S(1)} %shard_map.107), channel_id=1, replica_groups=mesh['x'=4,'core'=2,'z'=16,'y'=4] {'x','core','y'}, dimensions={0} | all-to-all | bytes 1048576 | tf_op jit(solution)/shard_map/all_to_all | solution.py:414
  170.1 0.0 copy-done.3
  170.1 0.0 copy-done.4
  170.1 0.0 copy-done.5
  170.1 1.3 shard_map.108
Async XLA Ops:
  7.2 93.2 %all-gather.3.cloned.1.call-start = ((), (), s32[]{:S(2)}) async-start(), calls=%async_computation.5 | async-start | bytes 1323008 | tf_op jit(solution)/shard_map/all_gather | solution.py:369
  100.4 1.3 copy-start
  101.7 21.1 %copy-start.1 = (f32[16,128]{1,0:T(8,128)S(1)}, f32[16,128]{1,0:T(8,128)}, u32[]{:S(2)}) copy-start(f32[16,128]{1,0:T(8,128)} %get-tuple-element.38.aux_ref) | copy-start | bytes 24580
  102.4 20.4 %collective-permute-start = (bf16[16,512,256]{2,1,0:T(8,128)(2,1)}, bf16[16,512,256]{2,1,0:T(8,128)(2,1)}, u32[]{:S(2)}, u32[]{:S(2)}) collective-permute-start(bf16[16,512,256]{2,1,0:T(8,128)(2,1)} %get-tuple-element.20), channel_id=1, source_target_pairs={{0,64},{64,0},{1,65},{65,1},{2,66},{66,2},{3,67},{67,3},{4,68},{68... | collective-permute-start | bytes 12582920 | tf_op jit(solution)/shard_map/cond/branch_1_fun/ppermute | solution.py:384
  122.8 22.4 %copy-start.2 = (f32[1,1024]{1,0:T(1,128)S(1)}, f32[1,1024]{1,0:T(1,128)}, u32[]{:S(2)}) copy-start(f32[1,1024]{1,0:T(1,128)} %param.21) | copy-start | bytes 12292
  122.8 22.4 %copy-start.6 = (bf16[16,512,256]{2,1,0:T(8,128)(2,1)S(1)}, bf16[16,512,256]{2,1,0:T(8,128)(2,1)}, u32[]{:S(2)}) copy-start(bf16[16,512,256]{2,1,0:T(8,128)(2,1)} %get-tuple-element.58.mine_ref) | copy-start | bytes 12582916
  145.2 24.9 %copy-start.3 = (s32[1024]{0:T(1024)S(1)}, s32[1024]{0:T(1024)}, u32[]{:S(2)}) copy-start(s32[1024]{0:T(1024)} %param.18) | copy-start | bytes 12292
  145.2 24.9 %copy-start.4 = (f32[1024]{0:T(1024)S(1)}, f32[1024]{0:T(1024)}, u32[]{:S(2)}) copy-start(f32[1024]{0:T(1024)} %param.19) | copy-start | bytes 12292
  145.2 24.9 %copy-start.5 = (f32[1024]{0:T(1024)S(1)}, f32[1024]{0:T(1024)}, u32[]{:S(2)}) copy-start(f32[1024]{0:T(1024)} %param.20) | copy-start | bytes 12292
Sparse Core Ops, SparseCore 0:
  10.1 77.4 all-gather.2

commit v6 on v4

v6 whole, which is shorter than its diff:
```python
import jax
import jax.numpy as jnp
from jax import lax
from jax.experimental import pallas as pl
from jax.experimental.pallas import tpu as pltpu
from jax.sharding import Mesh, PartitionSpec as P

SITE_COUNT = 2048
X, CORE, Z, Y = 4, 2, 16, 4
GROUPS = X * CORE
ROWS = 32
COLS = 256
SCEN = 16
HALF = 64
BLOCK = 64
LOCAL = 48

penalty = 1.0
stride = 0.5
prox_weight = 2.0
learn_rate = 0.05
epsilon = 1e-05

f32, bf16 = jnp.float32, jnp.bfloat16


def lanes_of(shape):
    return lax.broadcasted_iota(jnp.int32, shape, len(shape) - 1)


def rows_of(shape):
    return lax.broadcasted_iota(jnp.int32, shape, len(shape) - 2)


def pick(row, index):
    return jnp.take_along_axis(
        jnp.broadcast_to(row, (8, 128)), index, axis=1, mode="promise_in_bounds"
    )


def narrow(value):
    return value.astype(bf16).astype(f32)


def turn(value, shift):
    return pltpu.roll(value, shift % 128, len(value.shape) - 1)


def prep_kernel(place_ref, transship_ref, *refs):
    inputs, (send_ref, aux_ref), copies = refs[:7], refs[7:9], refs[9:16]
    block_ref, sems = refs[16], refs[17]
    z, y, column = place_ref[1], place_ref[2], place_ref[3]
    at = pl.ds(pl.multiple_of(column * COLS, COLS), COLS)
    started = [
        pltpu.make_async_copy(source, target, sems.at[k])
        for k, (source, target) in enumerate(zip(inputs, copies))
    ]
    started.append(pltpu.make_async_copy(transship_ref.at[:, at], block_ref, sems.at[7]))
    for copy in started:
        copy.start()
    for copy in started:
        copy.wait()
    demand_ref, rec_ref, counts_ref, assign_ref, hold_ref, stock_ref, mult_ref = copies

    weights = counts_ref[...].astype(f32)
    total = jnp.sum(jnp.sum(weights, axis=1, keepdims=True), axis=0, keepdims=True)
    row = jnp.broadcast_to(jnp.where(z >= 8, weights[1:2], weights[0:1]) / total, (8, 128))
    row = pltpu.roll(row, (128 - z % 8 * SCEN) % 128, 1)
    aux_ref[0:8, :] = jnp.where(lanes_of((8, 128)) < SCEN, row, 0.0)
    aux_ref[8:16, :] = jnp.broadcast_to(total, (8, 128))

    index = assign_ref[...] - (z * Y + y) * ROWS
    stock = stock_ref[...]
    site = rows_of((ROWS, 128))
    lane = lanes_of((ROWS, 128))
    sums = jnp.zeros((ROWS, 128), f32)
    for k in range(8):
        sums = sums + jnp.where(index[k : k + 1] == site, stock[k : k + 1], 0.0)
    column_sum = jnp.sum(sums, axis=1, keepdims=True)
    high = narrow(column_sum)
    middle = narrow(column_sum - high)
    spread = jnp.where(lane == site, high, 0.0)
    spread = jnp.where(lane == site + ROWS, middle, spread)
    spread = jnp.where(lane == site + 2 * ROWS, column_sum - high - middle, spread)
    sum_row = jnp.broadcast_to(jnp.sum(spread, axis=0, keepdims=True), (8, 128))
    base = stock - learn_rate * (hold_ref[...] + mult_ref[...])
    parts = jnp.concatenate([narrow(base), base - narrow(base), index.astype(f32), sum_row], axis=0)
    parts = parts.astype(bf16)
    for n in range(Z):
        tile = slice(n // 8 * 128, n // 8 * 128 + 128)
        at = n % 8 * SCEN
        rec = rec_ref[:, tile]
        rounded = narrow(rec)
        both = jnp.where(
            lane < SCEN,
            turn(rounded, -at),
            jnp.where(
                lane < 2 * SCEN,
                turn(rec - rounded, SCEN - at),
                turn(demand_ref[:, tile].astype(f32), 2 * SCEN - at),
            ),
        )
        both = jnp.where(lane[0:16] < HALF, both[0:16], turn(both[16:32], HALF))
        send_ref[n, 0:ROWS, :] = block_ref[:, 0:128]
        send_ref[n, ROWS:BLOCK, :] = block_ref[:, 128:256]
        send_ref[n, BLOCK : BLOCK + 16, :] = both.astype(bf16)
        send_ref[n, BLOCK + 16 : BLOCK + LOCAL, :] = parts


def spread_kernel(place_ref, got_ref, spread_ref, local_ref):
    for z in range(Z):
        local_ref[z] = got_ref[z, BLOCK:, :]

    def put(n, carry):
        for z in range(Z):
            spread_ref[n, z * ROWS : (z + 1) * ROWS, 0:128] = got_ref[z, 0:ROWS, :]
            spread_ref[n, z * ROWS : (z + 1) * ROWS, 128:256] = got_ref[z, ROWS:BLOCK, :]
        return carry

    lax.fori_loop(0, X * Y, put, 0)


def repeat_kernel(place_ref, mine_ref, local_ref, send_ref):
    for q in range(Y):
        send_ref[q] = local_ref[...]


def recourse_steps(core, mine_ref, other_ref, rec_ref, short_ref, grad_ref, rounded_ref):
    def one_step(inner, carry):
        square = jnp.zeros((ROWS, 128), f32)
        for y in range(Y):
            acc = jnp.zeros((512, 128), f32)
            for x in range(X):
                for ref, chunk in ((mine_ref, 2 * x + core), (other_ref, 2 * x + 1 - core)):
                    at = pl.ds(pl.multiple_of(chunk * COLS, COLS), COLS)
                    acc = acc + jnp.dot(
                        ref[x * Y + y], rounded_ref[at, :], preferred_element_type=f32
                    )
            for z in range(Z):
                at = pl.ds((z * Y + y) * ROWS, ROWS)
                grad = acc[z * ROWS : (z + 1) * ROWS] - penalty * (short_ref[at, :] - rec_ref[at, :])
                grad_ref[at, :] = grad
                square = square + grad * grad
        square = jnp.sum(square, axis=0, keepdims=True)
        factor = stride / jnp.sqrt(square / SITE_COUNT + epsilon)

        def renew(j, carry):
            at = pl.ds(pl.multiple_of(j * 256, 256), 256)
            rec = jnp.maximum(rec_ref[at, :] - grad_ref[at, :] * factor, 0.0)
            rec_ref[at, :] = rec
            rounded_ref[at, :] = rec.astype(jnp.bfloat16)
            return carry

        lax.fori_loop(0, 8, renew, 0)
        return carry

    lax.fori_loop(0, 2, one_step, 0)


def pull_sums(share, rec_ref, short_ref, put):
    for z in range(Z):
        at = pl.ds(z * 128, 128)
        gap = penalty * (short_ref[at, :] - rec_ref[at, :]) * share
        put(z, jnp.sum(gap.T, axis=0, keepdims=True))


def first_kernel(
    place_ref, aux_ref, mine_ref, other_ref, local_ref, rec_ref, short_ref, pull_ref, grad_ref, rounded_ref
):
    lane, sub = lanes_of((ROWS, 128)), rows_of((ROWS, 128))
    picked = (lane % ROWS == sub) & (lane < 3 * ROWS)

    def load(b, carry):
        at = pl.ds(pl.multiple_of(b * ROWS, ROWS), ROWS)
        local = local_ref[b % Y, b // Y].astype(f32)
        both = jnp.concatenate([local[0:16], turn(local[0:16], HALF)], axis=0)
        rec = both + turn(both, -SCEN)
        old = jnp.sum(jnp.where(picked, local[40:41], 0.0), axis=1, keepdims=True)
        rec_ref[at, :] = rec
        rounded_ref[at, :] = rec.astype(bf16)
        short_ref[at, :] = turn(both, -2 * SCEN) - old
        return carry

    lax.fori_loop(0, Z * Y, load, 0, unroll=8)
    recourse_steps(place_ref[0], mine_ref, other_ref, rec_ref, short_ref, grad_ref, rounded_ref)

    def put(z, row):
        for n in range(Z):
            pull_ref[n, z : z + 1, :] = row

    pull_sums(aux_ref[0:1, :], rec_ref, short_ref, put)


def second_kernel(
    place_ref,
    aux_ref,
    mine_ref,
    other_ref,
    local_ref,
    rec_in_ref,
    short_in_ref,
    pulled_ref,
    send_ref,
    own_ref,
    rec_ref,
    pull_ref,
    short_ref,
    grad_ref,
    rounded_ref,
):
    total = pulled_ref[0]
    for n in range(1, Z):
        total = total + pulled_ref[n]
    pull_ref[0] = total
    lane, sub = lanes_of((ROWS, 128)), rows_of((ROWS, 128))
    picked = (lane % ROWS == sub) & (lane < 3 * ROWS)
    site = sub.astype(f32)

    def load(b, carry):
        at = pl.ds(pl.multiple_of(b * ROWS, ROWS), ROWS)
        local = local_ref[b % Y, b // Y, 16:48, :].astype(f32)
        index = local[16:24]
        pull = pick(pull_ref[0, pl.ds(b // Y, 1), :], index.astype(jnp.int32) + b % Y * ROWS)
        stock = jnp.maximum(local[0:8] + local[8:16] + learn_rate * pull, 0.0)
        change = jnp.where(picked, -local[24:25], 0.0)
        for k in range(8):
            change = change + jnp.where(index[k : k + 1] == site, stock[k : k + 1], 0.0)
        rec = rec_in_ref[at, :]
        rec_ref[at, :] = rec
        rounded_ref[at, :] = rec.astype(bf16)
        short_ref[at, :] = short_in_ref[at, :] - jnp.sum(change, axis=1, keepdims=True)
        return carry

    lax.fori_loop(0, Z * Y, load, 0, unroll=8)
    recourse_steps(place_ref[0], mine_ref, other_ref, rec_ref, short_ref, grad_ref, rounded_ref)

    def put(z, row):
        pull_ref[1, z : z + 1, :] = row

    pull_sums(aux_ref[0:1, :], rec_ref, short_ref, put)
    z, y = place_ref[1], place_ref[2]
    back = (128 - y * ROWS) % 128
    own_ref[...] = pltpu.roll(jnp.broadcast_to(pull_ref[0, pl.ds(z, 1), :], (8, 128)), back, 1)
    lane = lanes_of((8, 128))
    for n in range(Z):
        start = pl.multiple_of((n * Y + y) * ROWS, ROWS)
        pull = pltpu.roll(jnp.broadcast_to(pull_ref[1, n : n + 1, :], (8, 128)), back, 1)
        block = turn(pull, 4 * SCEN)
        for k in range(3, -1, -1):
            rows = rec_ref[pl.ds(start + 8 * k, 8), :]
            block = jnp.where(lane < (k + 1) * SCEN, turn(rows, k * SCEN), block)
        send_ref[n] = block


def fold_kernel(place_ref, got_ref, own_ref, aux_ref, mult_ref, rec_ref, send_ref):
    lane, sub = lanes_of((8, 128)), rows_of((8, 128))
    pull = got_ref[0]
    for n in range(1, Z):
        pull = pull + got_ref[n]
    pull = jnp.broadcast_to(turn(pull, -4 * SCEN)[0:1], (8, 128))
    pulls = jnp.where(sub == 0, own_ref[...], jnp.where(sub == 1, pull, aux_ref[8:16, :]))
    for g in range(GROUPS):
        send_ref[g, 0:8, :] = mult_ref[...]
        send_ref[g, 8:16, :] = pulls
    for m in range(2):
        for k in range(4):
            out = turn(got_ref[8 * m], -k * SCEN)
            for n in range(1, 8):
                moved = turn(got_ref[8 * m + n], (n - k) * SCEN)
                out = jnp.where(lane < n * SCEN, out, moved)
            rec_ref[8 * k : 8 * k + 8, m * 128 : m * 128 + 128] = out


def last_kernel(place_ref, got_ref, assign_ref, hold_ref, stock_ref, consensus_ref, mult_ref, all_ref):
    z, y, column = place_ref[1], place_ref[2], place_ref[3]
    index = assign_ref[...] - (z * Y + y) * ROWS
    hold = hold_ref[...]
    start = stock_ref[...]
    totals = [got_ref[g, 10:11, :] for g in range(GROUPS)]
    all_total = totals[0]
    for g in range(1, GROUPS):
        all_total = all_total + totals[g]
    mults = [got_ref[g, 0:8, :] for g in range(GROUPS)]
    stocks = []
    weighted = jnp.zeros((8, 128), f32)
    for g in range(GROUPS):
        pull = pick(got_ref[g, 8:9, :], index)
        stock = jnp.maximum(start - learn_rate * (hold + mults[g] - pull), 0.0)
        weighted = weighted + totals[g] * stock
        stocks.append(stock)
    consensus = weighted / all_total
    weighted = jnp.zeros((8, 128), f32)
    for g in range(GROUPS):
        pull = pick(got_ref[g, 9:10, :], index)
        apart = prox_weight * (stocks[g] - consensus)
        mults[g] = mults[g] + apart
        stock = jnp.maximum(stocks[g] - learn_rate * (hold + mults[g] - pull + apart), 0.0)
        weighted = weighted + totals[g] * stock
        stocks[g] = stock
    consensus = weighted / all_total
    consensus_ref[...] = consensus
    for g in range(GROUPS):
        all_ref[g] = mults[g] + prox_weight * (stocks[g] - consensus)
    mult_ref[...] = all_ref[column]


def run_kernel(kernel, outs, scratch, *args, hbm=0, vmem_mib=16):
    vmem = pl.BlockSpec(memory_space=pltpu.VMEM)
    return pl.pallas_call(
        kernel,
        out_shape=[jax.ShapeDtypeStruct(*out) for out in outs],
        in_specs=[pl.BlockSpec(memory_space=pltpu.SMEM)]
        + [pl.BlockSpec(memory_space=pl.ANY)] * hbm
        + [vmem] * (len(args) - 1 - hbm),
        out_specs=[vmem] * len(outs),
        scratch_shapes=[pltpu.VMEM(*entry) if isinstance(entry, tuple) else entry for entry in scratch],
        compiler_params=pltpu.CompilerParams(vmem_limit_bytes=vmem_mib * 1024 * 1024),
    )(*args)


def per_device(demand, recourse_init, transship, counts, assign, hold_cost, stock_init, mult_init):
    core = lax.axis_index("core")
    column = lax.axis_index("x") * CORE + core
    y = lax.axis_index("y")
    z = lax.axis_index("z")
    place = jnp.stack([core, z, y, column]).astype(jnp.int32)
    wide = ((SITE_COUNT, 128), f32)
    wide16 = ((SITE_COUNT, 128), bf16)
    tile = ((8, 128), f32)
    assign = assign.reshape(8, 128)
    hold_cost = hold_cost.reshape(8, 128)
    stock_init = stock_init.reshape(8, 128)
    mult_init = mult_init.reshape(8, 128)

    raw = (
        demand,
        recourse_init,
        counts.reshape(2, 128),
        assign,
        hold_cost,
        stock_init,
        mult_init,
    )
    send, aux = run_kernel(
        prep_kernel,
        [((Z, BLOCK + LOCAL, 128), bf16), ((16, 128), f32)],
        [(entry.shape, entry.dtype) for entry in raw]
        + [((ROWS, COLS), bf16), pltpu.SemaphoreType.DMA((8,))],
        place,
        transship,
        *raw,
        hbm=8,
        vmem_mib=60,
    )
    got = lax.all_to_all(send, "z", 0, 0, tiled=True)
    spread, local = run_kernel(
        spread_kernel,
        [((X * Y, Z * ROWS, COLS), bf16), ((Z, LOCAL, 128), bf16)],
        [],
        place,
        got,
    )
    mine = lax.all_to_all(spread, ("x", "y"), 0, 0, tiled=True)
    other = lax.ppermute(mine, "core", [(0, 1), (1, 0)])
    (local,) = run_kernel(repeat_kernel, [((Y, Z, LOCAL, 128), bf16)], [], place, mine, local, hbm=1)
    local = lax.all_to_all(local, "y", 0, 0, tiled=True)

    rec, short, pull = run_kernel(
        first_kernel,
        [wide, wide, ((Z, Z, 128), f32)],
        [wide, wide16],
        place,
        aux,
        mine,
        other,
        local,
    )
    pull = lax.all_to_all(pull, "z", 0, 0, tiled=True)
    send, own = run_kernel(
        second_kernel,
        [((Z, 8, 128), f32), tile],
        [wide, ((2, Z, 128), f32), wide, wide, wide16],
        place,
        aux,
        mine,
        other,
        local,
        rec,
        short,
        pull,
    )
    got = lax.all_to_all(send, "z", 0, 0, tiled=True)
    recourse, send = run_kernel(
        fold_kernel,
        [((ROWS, Z * SCEN), f32), ((GROUPS, 16, 128), f32)],
        [],
        place,
        got,
        own,
        aux,
        mult_init,
    )
    got = lax.all_to_all(send, ("x", "core"), 0, 0, tiled=True)
    consensus, multipliers = run_kernel(
        last_kernel,
        [tile, tile],
        [((GROUPS, 8, 128), f32)],
        place,
        got,
        assign,
        hold_cost,
        stock_init,
    )
    return (consensus.reshape(1024), multipliers.reshape(1, 1024), recourse)


def solution(mesh):
    grid = Mesh(mesh.devices.reshape(X, CORE, Z, Y), ("x", "core", "z", "y"))
    scen, dom = ("x", "core"), ("z", "y")
    in_specs = (
        P(dom, scen),
        P(dom, scen),
        P(dom, None),
        P(scen),
        P(dom),
        P(dom),
        P(dom),
        P(scen, dom),
    )
    out_specs = (P(dom), P(scen, dom), P(dom, scen))
    return jax.shard_map(
        per_device, mesh=grid, in_specs=in_specs, out_specs=out_specs, check_vma=False
    )
```

time: 168 us -> 191 us (1.14)
  blocking collectives: 107 us -> 151 us
  between operations: 14.1 us -> 0.7 us
  waiting for transfers between devices: 7.12 us -> 0.01 us
    all_to_all x5 -> x6, blocking collectives: 107 us -> 151 us  [the longest x2 53.6 us: per_device(): got = lax.all_to_all(send, 'z', 0, 0, tiled=True)]
    ppermute x1, waiting for transfers between devices: 7.11 us -> 0.01 us  [per_device(): other = lax.ppermute(mine, 'core', [(0, 1), (1, 0)])]
    pallas_call x5 -> x7, Pallas kernels: 24.2 us -> 25.8 us  [run_kernel(): pl.pallas_call(kernel, out_shape=[jax.ShapeDtypeStruct(*out) for out in o...]
  transfers between devices with their start and end apart: 2 -> 1, of which waited for: 1 -> 0; matrix products, arithmetic and copies ran while one was open for 0% -> 0% of each run, Pallas kernels for 1% -> 0%
where the time goes in v6:
time: 191 us; the launch traced here: 190 us
  blocking collectives  151 us (79%)
  Pallas kernels  25.8 us (14%)
  starting transfers between devices  11.2 us (6%)
    all_to_all x2, blocking collectives, per_device(): got = lax.all_to_all(send, 'z', 0, 0, tiled=True)  53.6 us
    all_to_all x1, blocking collectives, per_device(): mine = lax.all_to_all(spread, ('x', 'y'), 0, 0, tiled=True)  49.2 us
    pallas_call x7, Pallas kernels, run_kernel(): pl.pallas_call(kernel, out_shape=[jax.ShapeDtypeStruct(*out) for out in o...  25.8 us
    all_to_all x1, blocking collectives, per_device(): pull = lax.all_to_all(pull, 'z', 0, 0, tiled=True)  23.4 us
    all_to_all x1, blocking collectives, per_device(): local = lax.all_to_all(local, 'y', 0, 0, tiled=True)  14.6 us
    ppermute x1, starting transfers between devices, per_device(): other = lax.ppermute(mine, 'core', [(0, 1), (1, 0)])  11.2 us
    all_to_all x1, blocking collectives, per_device(): got = lax.all_to_all(send, ('x', 'core'), 0, 0, tiled=True)  10.3 us
  transfers between devices with their start and end apart: 1, of which 0 were waited for; matrix products, arithmetic and copies ran while one was open for 0% of the time, Pallas kernels for 0%

profile of v6, /device:TPU:1, one launch (start us, length us, event | category | flops | bytes accessed | tf_op | source)
XLA Modules:
  0.0 190.0 jit_solution(12762667657512267954)
XLA Ops:
  0.6 0.6 pad_add_fusion.place_ref
  1.3 2.7 %shard_map.103 = (bf16[16,112,128]{2,1,0:T(8,128)(2,1)}, f32[16,128]{1,0:T(8,128)}) custom-call(s32[4]{0:T(128)} %pad_add_fusion.place_ref, bf16[32,2048]{1,0:T(8,128)(2,1)} %transship_ref.1, s32[32,256]{1,0:T(8,128)} %refs_0_.1, f32[32,256]{1,0:T(8,128)} %refs_1_.1, s32[2,128]{1,0:T(2,128)} %bitcast.19, s32[8,128]{1,0:T(8,128)} %bitcast.13, ...), custom_call_target="tpu_custom_call" | custom-call | tf_op jit(solution)/shard_map/pallas_call | solution.py:309
  4.0 36.6 %all_to_all.30.got_ref = bf16[16,112,128]{2,1,0:T(8,128)(2,1)S(1)} all-to-all(bf16[16,112,128]{2,1,0:T(8,128)(2,1)} %get-tuple-element.17), channel_id=1, replica_groups=mesh['x'=4,'core'=2,'z'=16,'y'=4] {'z'}, dimensions={0} | all-to-all | bytes 917504 | tf_op jit(solution)/shard_map/all_to_all | solution.py:355
  40.6 0.0 copy-start.1
  40.6 0.7 copy-done.1
  41.3 1.3 shard_map.104
  42.6 49.2 %all_to_all.31.mine_ref = bf16[16,512,256]{2,1,0:T(8,128)(2,1)S(1)} all-to-all(bf16[16,512,256]{2,1,0:T(8,128)(2,1)S(1)} %get-tuple-element.18), channel_id=1, replica_groups=mesh['x'=4,'core'=2,'z'=16,'y'=4] {'x','y'}, dimensions={0} | all-to-all | bytes 8388608 | tf_op jit(solution)/shard_map/all_to_all | solution.py:363
  91.8 0.0 copy-start
  91.8 11.2 %collective-permute-start = (bf16[16,512,256]{2,1,0:T(8,128)(2,1)S(1)}, bf16[16,512,256]{2,1,0:T(8,128)(2,1)S(1)}, u32[]{:S(2)}, u32[]{:S(2)}) collective-permute-start(bf16[16,512,256]{2,1,0:T(8,128)(2,1)S(1)} %all_to_all.31.mine_ref), channel_id=1, source_target_pairs={{0,64},{64,0},{1,65},{65,1},{2,66},{66,2},{3,67},{67,3},{4,68},{68... | collective-permute-start | bytes 12582920 | tf_op jit(solution)/shard_map/ppermute | solution.py:364
  103.0 0.6 shard_map.105
  103.6 14.6 %all_to_all.32.local_ref = bf16[4,16,48,128]{3,2,1,0:T(8,128)(2,1)S(1)} all-to-all(bf16[4,16,48,128]{3,2,1,0:T(8,128)(2,1)S(1)} %shard_map.105), channel_id=1, replica_groups=mesh['x'=4,'core'=2,'z'=16,'y'=4] {'y'}, dimensions={0} | all-to-all | bytes 1572864 | tf_op jit(solution)/shard_map/all_to_all | solution.py:366
  118.2 0.0 collective-permute-done.other_ref
  118.2 0.0 copy-done
  118.2 10.0 %shard_map.106 = (f32[2048,128]{1,0:T(8,128)S(1)}, f32[2048,128]{1,0:T(8,128)S(1)}, f32[16,16,128]{2,1,0:T(8,128)S(1)}) custom-call(s32[4]{0:T(128)S(1)} %copy-done.1, f32[16,128]{1,0:T(8,128)S(1)} %copy-done, bf16[16,512,256]{2,1,0:T(8,128)(2,1)S(1)} %all_to_all.31.mine_ref, bf16[16,512,256]{2,1,0:T(8,128)(2,1)S(1)} %collective-permute-done.other_ref, ...), custom_call_target="tpu_custom_call" | custom-call | tf_op jit(solution)/shard_map/pallas_call | solution.py:309
  128.2 23.4 %all_to_all.33.pulled_ref = f32[16,16,128]{2,1,0:T(8,128)S(1)} all-to-all(f32[16,16,128]{2,1,0:T(8,128)S(1)} %get-tuple-element.22), channel_id=1, replica_groups=mesh['x'=4,'core'=2,'z'=16,'y'=4] {'z'}, dimensions={0} | all-to-all | bytes 262144 | tf_op jit(solution)/shard_map/all_to_all | solution.py:378
  151.5 0.0 copy-start.2
  151.5 0.0 copy-start.3
  151.5 0.0 copy-start.4
  151.6 0.0 copy-start.5
  151.6 8.6 %shard_map.107 = (f32[16,8,128]{2,1,0:T(8,128)S(1)}, f32[8,128]{1,0:T(8,128)S(1)}) custom-call(s32[4]{0:T(128)S(1)} %copy-done.1, f32[16,128]{1,0:T(8,128)S(1)} %copy-done, bf16[16,512,256]{2,1,0:T(8,128)(2,1)S(1)} %all_to_all.31.mine_ref, bf16[16,512,256]{2,1,0:T(8,128)(2,1)S(1)} %collective-permute-done.other_ref, ...), custom_call_target="tpu_custom_call" | custom-call | tf_op jit(solution)/shard_map/pallas_call | solution.py:309
  160.1 17.0 %all_to_all.34.got_ref = f32[16,8,128]{2,1,0:T(8,128)S(1)} all-to-all(f32[16,8,128]{2,1,0:T(8,128)S(1)} %get-tuple-element.23), channel_id=1, replica_groups=mesh['x'=4,'core'=2,'z'=16,'y'=4] {'z'}, dimensions={0} | all-to-all | bytes 131072 | tf_op jit(solution)/shard_map/all_to_all | solution.py:392
  177.2 0.0 copy-done.2
  177.2 1.3 shard_map.108
  178.5 10.3 %all_to_all.35.got_ref = f32[8,16,128]{2,1,0:T(8,128)S(1)} all-to-all(f32[8,16,128]{2,1,0:T(8,128)S(1)} %get-tuple-element.25), channel_id=1, replica_groups=mesh['x'=4,'core'=2,'z'=16,'y'=4] {'x','core'}, dimensions={0} | all-to-all | bytes 131072 | tf_op jit(solution)/shard_map/all_to_all | solution.py:403
  188.7 0.0 copy-done.3
  188.8 0.0 copy-done.4
  188.8 0.0 copy-done.5
  188.8 1.3 shard_map.109
Async XLA Ops:
  40.6 0.7 copy-start.1
  91.8 26.4 %copy-start = (f32[16,128]{1,0:T(8,128)S(1)}, f32[16,128]{1,0:T(8,128)}, u32[]{:S(2)}) copy-start(f32[16,128]{1,0:T(8,128)} %get-tuple-element.16.aux_ref) | copy-start | bytes 24580
  91.8 26.4 %collective-permute-start = (bf16[16,512,256]{2,1,0:T(8,128)(2,1)S(1)}, bf16[16,512,256]{2,1,0:T(8,128)(2,1)S(1)}, u32[]{:S(2)}, u32[]{:S(2)}) collective-permute-start(bf16[16,512,256]{2,1,0:T(8,128)(2,1)S(1)} %all_to_all.31.mine_ref), channel_id=1, source_target_pairs={{0,64},{64,0},{1,65},{65,1},{2,66},{66,2},{3,67},{67,3},{4,68},{68... | collective-permute-start | bytes 12582920 | tf_op jit(solution)/shard_map/ppermute | solution.py:364
  151.5 25.6 %copy-start.2 = (f32[1,1024]{1,0:T(1,128)S(1)}, f32[1,1024]{1,0:T(1,128)}, u32[]{:S(2)}) copy-start(f32[1,1024]{1,0:T(1,128)} %param.15) | copy-start | bytes 12292
  151.5 37.2 %copy-start.3 = (s32[1024]{0:T(1024)S(1)}, s32[1024]{0:T(1024)}, u32[]{:S(2)}) copy-start(s32[1024]{0:T(1024)} %param.12) | copy-start | bytes 12292
  151.5 37.2 %copy-start.4 = (f32[1024]{0:T(1024)S(1)}, f32[1024]{0:T(1024)}, u32[]{:S(2)}) copy-start(f32[1024]{0:T(1024)} %param.13) | copy-start | bytes 12292
  151.6 37.2 %copy-start.5 = (f32[1024]{0:T(1024)S(1)}, f32[1024]{0:T(1024)}, u32[]{:S(2)}) copy-start(f32[1024]{0:T(1024)} %param.14) | copy-start | bytes 12292

commit v7 on v4

--- a/solution.py
+++ b/solution.py
@@ -36,17 +36,22 @@
     )
 
 
-def prep_kernel(place_ref, *refs):
-    inputs, (packed_ref, aux_ref), copies = refs[:7], refs[7:9], refs[9:16]
+def prep_kernel(place_ref, transship_ref, *refs):
+    inputs, (packed_ref, aux_ref, spread_ref), copies = refs[:7], refs[7:10], refs[10:17]
+    block_ref, sems = refs[17], refs[18]
+    at = pl.ds(pl.multiple_of(place_ref[3] * COLS, COLS), COLS)
     started = [
-        pltpu.make_async_copy(source, target, refs[16].at[k])
+        pltpu.make_async_copy(source, target, sems.at[k])
         for k, (source, target) in enumerate(zip(inputs, copies))
     ]
+    started.append(pltpu.make_async_copy(transship_ref.at[:, at], block_ref, sems.at[7]))
     for copy in started:
         copy.start()
     for copy in started:
         copy.wait()
     demand_ref, rec_ref, counts_ref, assign_ref, hold_ref, stock_ref, mult_ref = copies
+    for n in range(Z):
+        spread_ref[n] = block_ref[...]
     z, y = place_ref[1], place_ref[2]
     weights = counts_ref[...].astype(f32)
     total = jnp.sum(jnp.sum(weights, axis=1, keepdims=True), axis=0, keepdims=True)
@@ -80,13 +85,6 @@
         packed_ref[q, ROWS + 16 : ROWS + 24, :] = jnp.broadcast_to(as_row, (8, 128))
 
 
-def spread_z_kernel(place_ref, packed_ref, transship_ref, spread_ref):
-    at = pl.ds(pl.multiple_of(place_ref[3] * COLS, COLS), COLS)
-    block = transship_ref[:, at]
-    for z in range(Z):
-        spread_ref[z] = block
-
-
 def recourse_steps(core, mine_ref, other_ref, rec_ref, short_ref, grad_ref, rounded_ref):
     def one_step(inner, carry):
         square = jnp.zeros((ROWS, 128), f32)
@@ -126,18 +124,28 @@
         put(z, jnp.sum(gap.T, axis=0, keepdims=True))
 
 
-def first_kernel(
-    place_ref, aux_ref, mine_ref, other_ref, packed_ref, rec_ref, short_ref, pull_ref, grad_ref, rounded_ref
-):
+def unpack_kernel(place_ref, packed_ref, rec_ref, short_ref):
     def load(b, carry):
         at = pl.ds(pl.multiple_of(b * ROWS, ROWS), ROWS)
         both = packed_ref[b, 0:ROWS, :]
         rec_ref[at, :] = both
-        rounded_ref[at, :] = both.astype(jnp.bfloat16)
         short_ref[at, :] = pltpu.roll(both, SCEN, 1)
         return carry
 
     lax.fori_loop(0, Z * Y, load, 0, unroll=8)
+
+
+def first_kernel(
+    place_ref, aux_ref, mine_ref, other_ref, rec_in_ref, short_ref, rec_ref, pull_ref, grad_ref, rounded_ref
+):
+    def load(j, carry):
+        at = pl.ds(pl.multiple_of(j * 256, 256), 256)
+        rec = rec_in_ref[at, :]
+        rec_ref[at, :] = rec
+        rounded_ref[at, :] = rec.astype(jnp.bfloat16)
+        return carry
+
+    lax.fori_loop(0, 8, load, 0)
     recourse_steps(place_ref[0], mine_ref, other_ref, rec_ref, short_ref, grad_ref, rounded_ref)
 
     def put(z, row):
@@ -254,7 +262,7 @@
         rec_ref[16:32, tile] = jnp.where(low, pltpu.roll(even, SCEN, 1), odd)
 
 
-def run_kernel(kernel, outs, scratch, *args, hbm=0, vmem_mib=16):
+def run_kernel(kernel, outs, scratch, *args, hbm=0, vmem_mib=16, flops=0):
     vmem = pl.BlockSpec(memory_space=pltpu.VMEM)
     outs = [out if isinstance(out, jax.ShapeDtypeStruct) else jax.ShapeDtypeStruct(out, f32) for out in outs]
     return pl.pallas_call(
@@ -265,6 +273,7 @@
         + [vmem] * (len(args) - 1 - hbm),
         out_specs=[vmem] * len(outs),
         scratch_shapes=[pltpu.VMEM(*entry) if isinstance(entry, tuple) else entry for entry in scratch],
+        cost_estimate=pl.CostEstimate(flops=flops, bytes_accessed=0, transcendentals=0) if flops else None,
         compiler_params=pltpu.CompilerParams(vmem_limit_bytes=vmem_mib * 1024 * 1024),
     )(*args)
 
@@ -285,6 +294,7 @@
     z = lax.axis_index("z")
     place = jnp.stack([core, z, y, column]).astype(jnp.int32)
     wide = (SITE_COUNT, 128)
+    bf16 = jnp.bfloat16
     assign = assign.reshape(8, 128)
     hold_cost = hold_cost.reshape(8, 128)
     stock_init = stock_init.reshape(8, 128)
@@ -299,52 +309,46 @@
         stock_init,
         mult_init,
     )
-    packed, aux = run_kernel(
+    packed, aux, block = run_kernel(
         prep_kernel,
-        [(Y, ROWS + PARTS, 128), (16, 128)],
-        [(entry.shape, entry.dtype) for entry in raw] + [pltpu.SemaphoreType.DMA((7,))],
+        [(Y, ROWS + PARTS, 128), (16, 128), jax.ShapeDtypeStruct((Z, ROWS, COLS), bf16)],
+        [(entry.shape, entry.dtype) for entry in raw]
+        + [((ROWS, COLS), bf16), pltpu.SemaphoreType.DMA((8,))],
         place,
+        transship,
         *raw,
-        hbm=len(raw),
+        hbm=8,
         vmem_mib=60,
     )
     packed = lax.all_to_all(packed, "y", 0, 0, tiled=True)
-    bf16 = jnp.bfloat16
     always = column * COLS >= 0
 
-    def spread_z(transship, packed):
-        (block,) = run_kernel(
-            spread_z_kernel,
-            [jax.ShapeDtypeStruct((Z, ROWS, COLS), bf16)],
-            [],
-            place,
-            packed,
-            transship,
-            hbm=1,
-        )
+    def spread_z(block, packed):
         return lax.all_to_all(block, "z", 0, 0, tiled=True).reshape(Z * ROWS, COLS)
 
     def spread_xy(along_z):
         spread = jnp.broadcast_to(along_z[None], (X * Y, Z * ROWS, COLS))
         return lax.all_to_all(spread, ("x", "y"), 0, 0, tiled=True)
 
-    def swap_cores(mine):
-        return lax.ppermute(mine, "core", [(0, 1), (1, 0)])
+    def swap_cores(mine, gathered):
+        other = lax.ppermute(mine, "core", [(0, 1), (1, 0)])
+        return other, *run_kernel(unpack_kernel, [wide, wide], [], place, gathered, flops=2_000_000_000)
 
     gathered = lax.all_gather(packed, "z", axis=0, tiled=True)
-    along_z = one_block(always, spread_z, transship, packed)
+    along_z = one_block(always, spread_z, block, packed)
     mine = one_block(always, spread_xy, along_z)
-    other = one_block(always, swap_cores, mine)
-
-    rec, short, pull1 = run_kernel(
+    other, rec, short = one_block(always, swap_cores, mine, gathered)
+
+    rec, pull1 = run_kernel(
         first_kernel,
-        [wide, wide, (Y, Z, 128)],
-        [(wide, f32), (wide, jnp.bfloat16)],
+        [wide, (Y, Z, 128)],
+        [(wide, f32), (wide, bf16)],
         place,
         aux,
         mine,
         other,
-        gathered,
+        rec,
+        short,
     )
     pull1 = lax.all_to_all(pull1, "y", 0, 0, tiled=True)
     (send,) = run_kernel(

time: 168 us -> 165 us (0.982)
  waiting for transfers between devices: 7.12 us -> 4.8 us
    ppermute x1, waiting for transfers between devices: 7.11 us -> 4.78 us  [swap_cores(): other = lax.ppermute(mine, 'core', [(0, 1), (1, 0)])]
where the time goes in v7:
time: 165 us; the launch traced here: 163 us
  blocking collectives  108 us (65%)
  Pallas kernels  25 us (15%)
  between operations  14.1 us (9%)
  starting transfers between devices  10.7 us (6%)
  waiting for transfers between devices  4.8 us (3%)
    all_to_all x1, blocking collectives, spread_xy(): return lax.all_to_all(spread, ('x', 'y'), 0, 0, tiled=True)  47.8 us
    all_to_all x1, blocking collectives, spread_z(): return lax.all_to_all(block, 'z', 0, 0, tiled=True).reshape(Z * ROWS, COLS)  27.5 us
    pallas_call x5, Pallas kernels, run_kernel(): pl.pallas_call(kernel, out_shape=outs, in_specs=[pl.BlockSpec(memory_spac...  25 us
    all_to_all x1, blocking collectives, per_device(): got = lax.all_to_all(send, ('x', 'core', 'y'), 0, 0, tiled=True)  15.7 us
    ppermute x1, starting transfers between devices, swap_cores(): other = lax.ppermute(mine, 'core', [(0, 1), (1, 0)])  10.6 us
    all_to_all x1, blocking collectives, per_device(): packed = lax.all_to_all(packed, 'y', 0, 0, tiled=True)  9.87 us
    all_to_all x1, blocking collectives, per_device(): pull1 = lax.all_to_all(pull1, 'y', 0, 0, tiled=True)  6.65 us
    ppermute x1, waiting for transfers between devices, swap_cores(): other = lax.ppermute(mine, 'core', [(0, 1), (1, 0)])  4.78 us
  transfers between devices with their start and end apart: 2, of which 1 were waited for; matrix products, arithmetic and copies ran while one was open for 0% of the time, Pallas kernels for 1%

profile of v7, /device:TPU:1, one launch (start us, length us, event | category | flops | bytes accessed | tf_op | source)
XLA Modules:
  0.0 162.7 jit_solution(18357193626120919808)
XLA Ops:
  7.2 0.0 all-gather.2.cloned.1.call-start
  7.2 0.1 pad_add_fusion.place_ref
  7.3 2.3 %shard_map.103 = (f32[4,56,128]{2,1,0:T(8,128)}, f32[16,128]{1,0:T(8,128)}, bf16[16,32,256]{2,1,0:T(8,128)(2,1)S(1)}) custom-call(s32[4]{0:T(128)S(1)} %pad_add_fusion.place_ref, bf16[32,2048]{1,0:T(8,128)(2,1)} %transship_ref.1, s32[32,256]{1,0:T(8,128)} %refs_0_.1, f32[32,256]{1,0:T(8,128)} %refs_1_.1, s32[2,128]{1,0:T(2,128)} %bitcast.21, ...), custom_call_target="tpu_custom_call" | custom-call | tf_op jit(solution)/shard_map/pallas_call | solution.py:268
  9.6 9.9 %all_to_all.25 = f32[4,56,128]{2,1,0:T(8,128)} all-to-all(f32[4,56,128]{2,1,0:T(8,128)} %get-tuple-element.35), channel_id=1, replica_groups=mesh['x'=4,'core'=2,'z'=16,'y'=4] {'y'}, dimensions={0} | all-to-all | bytes 229376 | tf_op jit(solution)/shard_map/all_to_all | solution.py:323
  19.4 0.0 all-gather.2.cloned.1.call-update
  19.5 27.5 %conditional.3 = (bf16[512,256]{1,0:T(8,128)(2,1)S(1)}) conditional(s32[]{:T(128)} %convert_element_type.2, () %tuple.29, bf16[16,32,256]{2,1,0:T(8,128)(2,1)S(1)} %get-tuple-element.34), branch_computations={%region_0.0_spmd, %region_1.0_spmd} | conditional | bytes 524296 | solution.py:287
  19.5 27.5 %all_to_all.23 = bf16[16,32,256]{2,1,0:T(8,128)(2,1)S(1)} all-to-all(bf16[16,32,256]{2,1,0:T(8,128)(2,1)S(1)} %param.1), channel_id=1, replica_groups=mesh['x'=4,'core'=2,'z'=16,'y'=4] {'z'}, dimensions={0} | all-to-all | bytes 524288 | tf_op jit(solution)/shard_map/cond/branch_1_fun/all_to_all | solution.py:327
  47.0 48.2 %conditional.4 = (bf16[16,512,256]{2,1,0:T(8,128)(2,1)}) conditional(s32[]{:T(128)} %convert_element_type.2, () %tuple.28, bf16[512,256]{1,0:T(8,128)(2,1)S(1)} %get-tuple-element.50), branch_computations={%region_2.0_spmd, %region_3.0_spmd} | conditional | bytes 12845064 | solution.py:287
  47.0 0.4 broadcast_in_dim.0
  47.4 47.8 %all_to_all.24 = bf16[16,512,256]{2,1,0:T(8,128)(2,1)} all-to-all(bf16[16,512,256]{2,1,0:T(8,128)(2,1)S(1)} %broadcast_in_dim.0), channel_id=1, replica_groups=mesh['x'=4,'core'=2,'z'=16,'y'=4] {'x','y'}, dimensions={0} | all-to-all | bytes 8388608 | tf_op jit(solution)/shard_map/cond/branch_1_fun/all_to_all | solution.py:331
  95.2 0.0 all-gather.2.cloned.1.call-done.packed_ref
  95.2 0.0 copy-start
  95.2 17.7 %conditional.5 = (bf16[16,512,256]{2,1,0:T(8,128)(2,1)}, f32[2048,128]{1,0:T(8,128)S(1)}, f32[2048,128]{1,0:T(8,128)S(1)}) conditional(s32[]{:T(128)} %convert_element_type.2, () %tuple.30, (bf16[16,512,256]{2,1,0:T(8,128)(2,1)}, s32[4]{0:T(128)S(1)}, f32[64,56,128]{2,1,0:T(8,128)}) %tuple.31), branch_computations={%region_4.0_spmd, %region_5.0_spmd} | conditional | flops 2000000000 | bytes 16777280 | solution.py:287
  95.2 10.6 %collective-permute-start = (bf16[16,512,256]{2,1,0:T(8,128)(2,1)}, bf16[16,512,256]{2,1,0:T(8,128)(2,1)}, u32[]{:S(2)}, u32[]{:S(2)}) collective-permute-start(bf16[16,512,256]{2,1,0:T(8,128)(2,1)} %get-tuple-element.14), channel_id=1, source_target_pairs={{0,64},{64,0},{1,65},{65,1},{2,66},{66,2},{3,67},{67,3},{4,68},{68... | collective-permute-start | bytes 12582920 | tf_op jit(solution)/shard_map/cond/branch_1_fun/ppermute | solution.py:334
  105.8 2.3 %branch_1_fun.1 = (f32[2048,128]{1,0:T(8,128)S(1)}, f32[2048,128]{1,0:T(8,128)S(1)}) custom-call(s32[4]{0:T(128)S(1)} %get-tuple-element.15.place_ref, f32[64,56,128]{2,1,0:T(8,128)} %get-tuple-element.16.packed_ref), custom_call_target="tpu_custom_call" | custom-call | flops 2000000000 | tf_op jit(solution)/shard_map/cond/branch_1_fun/pallas_call | solution.py:268
  108.2 4.8 %collective-permute-done = bf16[16,512,256]{2,1,0:T(8,128)(2,1)} collective-permute-done((bf16[16,512,256]{2,1,0:T(8,128)(2,1)}, bf16[16,512,256]{2,1,0:T(8,128)(2,1)}, u32[]{:S(2)}, u32[]{:S(2)}) %collective-permute-start) | collective-permute-done | bytes 4194336 | tf_op jit(solution)/shard_map/cond/branch_1_fun/ppermute | solution.py:334
  112.9 0.0 copy-done
  112.9 0.0 copy-start.1
  112.9 0.0 copy-start.5
  112.9 0.0 copy-start.6
  113.0 9.2 %shard_map.104 = (f32[2048,128]{1,0:T(8,128)S(1)}, f32[4,16,128]{2,1,0:T(8,128)S(1)}) custom-call(s32[4]{0:T(128)S(1)} %pad_add_fusion.place_ref, f32[16,128]{1,0:T(8,128)S(1)} %copy-done, bf16[16,512,256]{2,1,0:T(8,128)(2,1)} %get-tuple-element.51.mine_ref, bf16[16,512,256]{2,1,0:T(8,128)(2,1)} %get-tuple-element.36.other_ref, ...), custom_call_target="tpu_custom_call" | custom-call | tf_op jit(solution)/shard_map/pallas_call | solution.py:268
  122.2 6.7 %all_to_all.26.pulled_ref = f32[4,16,128]{2,1,0:T(8,128)S(1)} all-to-all(f32[4,16,128]{2,1,0:T(8,128)S(1)} %get-tuple-element.40), channel_id=1, replica_groups=mesh['x'=4,'core'=2,'z'=16,'y'=4] {'y'}, dimensions={0} | all-to-all | bytes 65536 | tf_op jit(solution)/shard_map/all_to_all | solution.py:353
  128.8 0.0 copy-done.1
  128.8 0.0 copy-done.5
  128.8 0.0 copy-done.6
  128.8 0.0 copy-start.2
  128.8 0.0 copy-start.3
  128.9 0.0 copy-start.4
  128.9 9.9 %shard_map.105 = f32[32,32,128]{2,1,0:T(8,128)S(1)} custom-call(s32[4]{0:T(128)S(1)} %pad_add_fusion.place_ref, f32[16,128]{1,0:T(8,128)S(1)} %copy-done, bf16[16,512,256]{2,1,0:T(8,128)(2,1)S(1)} %copy-done.5, bf16[16,512,256]{2,1,0:T(8,128)(2,1)} %get-tuple-element.36.other_ref, f32[64,56,128]{2,1,0:T(8,128)S(1)} %copy-done.6, ...), custom_call_target="tpu_custom_call" | custom-call | tf_op jit(solution)/shard_map/pallas_call | solution.py:268
  138.8 15.7 %all_to_all.27.got_ref = f32[32,32,128]{2,1,0:T(8,128)S(1)} all-to-all(f32[32,32,128]{2,1,0:T(8,128)S(1)} %shard_map.105), channel_id=1, replica_groups=mesh['x'=4,'core'=2,'z'=16,'y'=4] {'x','core','y'}, dimensions={0} | all-to-all | bytes 1048576 | tf_op jit(solution)/shard_map/all_to_all | solution.py:368
  154.5 0.0 copy-done.2
  154.5 0.0 copy-done.3
  154.5 0.0 copy-done.4
  154.6 1.3 shard_map.106
Async XLA Ops:
  7.2 88.0 %all-gather.2.cloned.1.call-start = ((), (), s32[]{:S(2)}) async-start(), calls=%async_computation.5 | async-start | bytes 1949696 | tf_op jit(solution)/shard_map/all_gather | solution.py:337
  95.2 17.7 %copy-start = (f32[16,128]{1,0:T(8,128)S(1)}, f32[16,128]{1,0:T(8,128)}, u32[]{:S(2)}) copy-start(f32[16,128]{1,0:T(8,128)} %get-tuple-element.33.aux_ref) | copy-start | bytes 24580
  95.2 17.7 %collective-permute-start = (bf16[16,512,256]{2,1,0:T(8,128)(2,1)}, bf16[16,512,256]{2,1,0:T(8,128)(2,1)}, u32[]{:S(2)}, u32[]{:S(2)}) collective-permute-start(bf16[16,512,256]{2,1,0:T(8,128)(2,1)} %get-tuple-element.14), channel_id=1, source_target_pairs={{0,64},{64,0},{1,65},{65,1},{2,66},{66,2},{3,67},{67,3},{4,68},{68... | collective-permute-start | bytes 12582920 | tf_op jit(solution)/shard_map/cond/branch_1_fun/ppermute | solution.py:334
  112.9 15.9 %copy-start.1 = (f32[1,1024]{1,0:T(1,128)S(1)}, f32[1,1024]{1,0:T(1,128)}, u32[]{:S(2)}) copy-start(f32[1,1024]{1,0:T(1,128)} %param.21) | copy-start | bytes 12292
  112.9 15.9 %copy-start.5 = (bf16[16,512,256]{2,1,0:T(8,128)(2,1)S(1)}, bf16[16,512,256]{2,1,0:T(8,128)(2,1)}, u32[]{:S(2)}) copy-start(bf16[16,512,256]{2,1,0:T(8,128)(2,1)} %get-tuple-element.51.mine_ref) | copy-start | bytes 12582916
  112.9 15.9 %copy-start.6 = (f32[64,56,128]{2,1,0:T(8,128)S(1)}, f32[64,56,128]{2,1,0:T(8,128)}, u32[]{:S(2)}) copy-start(f32[64,56,128]{2,1,0:T(8,128)} %all-gather.2.cloned.1.call-done.packed_ref) | copy-start | bytes 5505028
  128.8 25.7 %copy-start.2 = (s32[1024]{0:T(1024)S(1)}, s32[1024]{0:T(1024)}, u32[]{:S(2)}) copy-start(s32[1024]{0:T(1024)} %param.18) | copy-start | bytes 12292
  128.8 25.7 %copy-start.3 = (f32[1024]{0:T(1024)S(1)}, f32[1024]{0:T(1024)}, u32[]{:S(2)}) copy-start(f32[1024]{0:T(1024)} %param.19) | copy-start | bytes 12292
  128.9 25.7 %copy-start.4 = (f32[1024]{0:T(1024)S(1)}, f32[1024]{0:T(1024)}, u32[]{:S(2)}) copy-start(f32[1024]{0:T(1024)} %param.20) | copy-start | bytes 12292
Sparse Core Ops, SparseCore 0:
  19.6 72.6 all-gather.1

commit v8 on v7

--- a/solution.py
+++ b/solution.py
@@ -330,52 +330,52 @@
         spread = jnp.broadcast_to(along_z[None], (X * Y, Z * ROWS, COLS))
         return lax.all_to_all(spread, ("x", "y"), 0, 0, tiled=True)
 
-    def swap_cores(mine, gathered):
+    def finish(mine, gathered, aux):
         other = lax.ppermute(mine, "core", [(0, 1), (1, 0)])
-        return other, *run_kernel(unpack_kernel, [wide, wide], [], place, gathered, flops=2_000_000_000)
+        rec, short = run_kernel(unpack_kernel, [wide, wide], [], place, gathered, flops=2_000_000_000)
+        rec, pull1 = run_kernel(
+            first_kernel,
+            [wide, (Y, Z, 128)],
+            [(wide, f32), (wide, bf16)],
+            place,
+            aux,
+            mine,
+            other,
+            rec,
+            short,
+        )
+        pull1 = lax.all_to_all(pull1, "y", 0, 0, tiled=True)
+        (send,) = run_kernel(
+            second_kernel,
+            [(GROUPS * Y, 32, 128)],
+            [(wide, f32), ((2, Z, 128), f32), (wide, f32), (wide, f32), (wide, jnp.bfloat16)],
+            place,
+            aux,
+            mine,
+            other,
+            gathered,
+            rec,
+            short,
+            pull1,
+            mult_init,
+        )
+        got = lax.all_to_all(send, ("x", "core", "y"), 0, 0, tiled=True)
+        consensus, multipliers, recourse = run_kernel(
+            last_kernel,
+            [(8, 128), (8, 128), (ROWS, Y * SCEN)],
+            [((GROUPS, 8, 128), f32)],
+            place,
+            got,
+            assign,
+            hold_cost,
+            stock_init,
+        )
+        return consensus, multipliers, recourse
 
     gathered = lax.all_gather(packed, "z", axis=0, tiled=True)
     along_z = one_block(always, spread_z, block, packed)
     mine = one_block(always, spread_xy, along_z)
-    other, rec, short = one_block(always, swap_cores, mine, gathered)
-
-    rec, pull1 = run_kernel(
-        first_kernel,
-        [wide, (Y, Z, 128)],
-        [(wide, f32), (wide, bf16)],
-        place,
-        aux,
-        mine,
-        other,
-        rec,
-        short,
-    )
-    pull1 = lax.all_to_all(pull1, "y", 0, 0, tiled=True)
-    (send,) = run_kernel(
-        second_kernel,
-        [(GROUPS * Y, 32, 128)],
-        [(wide, f32), ((2, Z, 128), f32), (wide, f32), (wide, f32), (wide, jnp.bfloat16)],
-        place,
-        aux,
-        mine,
-        other,
-        gathered,
-        rec,
-        short,
-        pull1,
-        mult_init,
-    )
-    got = lax.all_to_all(send, ("x", "core", "y"), 0, 0, tiled=True)
-    consensus, multipliers, recourse = run_kernel(
-        last_kernel,
-        [(8, 128), (8, 128), (ROWS, Y * SCEN)],
-        [((GROUPS, 8, 128), f32)],
-        place,
-        got,
-        assign,
-        hold_cost,
-        stock_init,
-    )
+    consensus, multipliers, recourse = one_block(always, finish, mine, gathered, aux)
     return (consensus.reshape(1024), multipliers.reshape(1, 1024), recourse)
 
 

time: 165 us -> 160 us (0.970)
  Pallas kernels: 25 us -> 20.2 us
    pallas_call x5, Pallas kernels: 25 us -> 20.2 us  [run_kernel(): pl.pallas_call(kernel, out_shape=outs, in_specs=[pl.BlockSpec(memory_spac...]
where the time goes in v8:
time: 160 us; the launch traced here: 158 us
  blocking collectives  108 us (68%)
  Pallas kernels  20.2 us (13%)
  between operations  14.1 us (9%)
  starting transfers between devices  10.8 us (7%)
  waiting for transfers between devices  4.67 us (3%)
    all_to_all x1, blocking collectives, spread_xy(): return lax.all_to_all(spread, ('x', 'y'), 0, 0, tiled=True)  47.8 us
    all_to_all x1, blocking collectives, spread_z(): return lax.all_to_all(block, 'z', 0, 0, tiled=True).reshape(Z * ROWS, COLS)  27.5 us
    pallas_call x5, Pallas kernels, run_kernel(): pl.pallas_call(kernel, out_shape=outs, in_specs=[pl.BlockSpec(memory_spac...  20.2 us
    all_to_all x1, blocking collectives, finish(): got = lax.all_to_all(send, ('x', 'core', 'y'), 0, 0, tiled=True)  15.7 us
    ppermute x1, starting transfers between devices, finish(): other = lax.ppermute(mine, 'core', [(0, 1), (1, 0)])  10.8 us
    all_to_all x1, blocking collectives, per_device(): packed = lax.all_to_all(packed, 'y', 0, 0, tiled=True)  9.87 us
    all_to_all x1, blocking collectives, finish(): pull1 = lax.all_to_all(pull1, 'y', 0, 0, tiled=True)  6.65 us
    ppermute x1, waiting for transfers between devices, finish(): other = lax.ppermute(mine, 'core', [(0, 1), (1, 0)])  4.65 us
  transfers between devices with their start and end apart: 2, of which 1 were waited for; matrix products, arithmetic and copies ran while one was open for 0% of the time, Pallas kernels for 1%

profile of v8, /device:TPU:1, one launch (start us, length us, event | category | flops | bytes accessed | tf_op | source)
XLA Modules:
  0.0 157.9 jit_solution(13291346645089996150)
XLA Ops:
  7.2 0.0 all-gather.2.cloned.1.call-start
  7.2 0.1 pad_add_fusion.place_ref
  7.3 2.3 %shard_map.103 = (f32[4,56,128]{2,1,0:T(8,128)}, f32[16,128]{1,0:T(8,128)S(1)}, bf16[16,32,256]{2,1,0:T(8,128)(2,1)S(1)}) custom-call(s32[4]{0:T(128)S(1)} %pad_add_fusion.place_ref, bf16[32,2048]{1,0:T(8,128)(2,1)} %transship_ref.1, s32[32,256]{1,0:T(8,128)} %refs_0_.1, f32[32,256]{1,0:T(8,128)} %refs_1_.1, s32[2,128]{1,0:T(2,128)} %bitcast.23, ...), custom_call_target="tpu_custom_call" | custom-call | tf_op jit(solution)/shard_map/pallas_call | solution.py:268
  9.6 9.9 %all_to_all.25 = f32[4,56,128]{2,1,0:T(8,128)} all-to-all(f32[4,56,128]{2,1,0:T(8,128)} %get-tuple-element.54), channel_id=1, replica_groups=mesh['x'=4,'core'=2,'z'=16,'y'=4] {'y'}, dimensions={0} | all-to-all | bytes 229376 | tf_op jit(solution)/shard_map/all_to_all | solution.py:323
  19.4 0.0 all-gather.2.cloned.1.call-update
  19.5 27.5 %conditional.3 = (bf16[512,256]{1,0:T(8,128)(2,1)S(1)}) conditional(s32[]{:T(128)} %convert_element_type.2, () %tuple.34, bf16[16,32,256]{2,1,0:T(8,128)(2,1)S(1)} %get-tuple-element.53), branch_computations={%region_0.0_spmd, %region_1.0_spmd} | conditional | bytes 524296 | solution.py:287
  19.5 27.5 %all_to_all.21 = bf16[16,32,256]{2,1,0:T(8,128)(2,1)S(1)} all-to-all(bf16[16,32,256]{2,1,0:T(8,128)(2,1)S(1)} %param.1), channel_id=1, replica_groups=mesh['x'=4,'core'=2,'z'=16,'y'=4] {'z'}, dimensions={0} | all-to-all | bytes 524288 | tf_op jit(solution)/shard_map/cond/branch_1_fun/all_to_all | solution.py:327
  47.0 0.0 copy-start.2
  47.0 0.0 copy-start.3
  47.0 0.0 copy-start.4
  47.0 0.0 copy-start.5
  47.0 48.2 %conditional.4 = (bf16[16,512,256]{2,1,0:T(8,128)(2,1)}) conditional(s32[]{:T(128)} %convert_element_type.2, () %tuple.33, bf16[512,256]{1,0:T(8,128)(2,1)S(1)} %get-tuple-element.65), branch_computations={%region_2.0_spmd, %region_3.0_spmd} | conditional | bytes 12845064 | solution.py:287
  47.0 0.4 broadcast_in_dim.0
  47.4 47.8 %all_to_all.22 = bf16[16,512,256]{2,1,0:T(8,128)(2,1)} all-to-all(bf16[16,512,256]{2,1,0:T(8,128)(2,1)S(1)} %broadcast_in_dim.0), channel_id=1, replica_groups=mesh['x'=4,'core'=2,'z'=16,'y'=4] {'x','y'}, dimensions={0} | all-to-all | bytes 8388608 | tf_op jit(solution)/shard_map/cond/branch_1_fun/all_to_all | solution.py:331
  95.2 0.0 all-gather.2.cloned.1.call-done
  95.2 0.0 copy-done.2
  95.2 0.0 copy-done.3
  95.2 0.0 copy-done.4
  95.2 0.0 copy-done.5
  95.2 55.8 %conditional.5 = (f32[32,256]{1,0:T(8,128)}, f32[1024]{0:T(1024)}, f32[1,1024]{1,0:T(1,128)}) conditional(s32[]{:T(128)} %convert_element_type.2, () %tuple.32, (bf16[16,512,256]{2,1,0:T(8,128)(2,1)}, s32[4]{0:T(128)S(1)}, f32[64,56,128]{2,1,0:T(8,128)}, f32[16,128]{1,0:T(8,128)S(1)}, f32[8,128]{1,0:T(8,128)S(1)}, /*index=5*/s32[8,128]{1,0:T(8,128)S(1)}, ...), branch_computations={%region_4.0_spmd, %region_5.0_spmd} | conditional | flops 2000000000 | bytes 42008696 | solution.py:287
  95.2 0.0 copy-start
  95.3 10.8 %collective-permute-start = (bf16[16,512,256]{2,1,0:T(8,128)(2,1)}, bf16[16,512,256]{2,1,0:T(8,128)(2,1)S(1)}, u32[]{:S(2)}, u32[]{:S(2)}) collective-permute-start(bf16[16,512,256]{2,1,0:T(8,128)(2,1)} %get-tuple-element.31.mine_ref), channel_id=1, source_target_pairs={{0,64},{64,0},{1,65},{65,1},{2,66},{66,2},{3,67},{67,3},{4,68},{68... | collective-permute-start | bytes 12582920 | tf_op jit(solution)/shard_map/cond/branch_1_fun/ppermute | solution.py:334
  106.0 2.3 %branch_1_fun.4 = (f32[2048,128]{1,0:T(8,128)S(1)}, f32[2048,128]{1,0:T(8,128)S(1)}) custom-call(s32[4]{0:T(128)S(1)} %get-tuple-element.29.place_ref, f32[64,56,128]{2,1,0:T(8,128)} %get-tuple-element.32.packed_ref), custom_call_target="tpu_custom_call" | custom-call | flops 2000000000 | tf_op jit(solution)/shard_map/cond/branch_1_fun/pallas_call | solution.py:268
  108.4 4.6 %collective-permute-done.other_ref = bf16[16,512,256]{2,1,0:T(8,128)(2,1)S(1)} collective-permute-done((bf16[16,512,256]{2,1,0:T(8,128)(2,1)}, bf16[16,512,256]{2,1,0:T(8,128)(2,1)S(1)}, u32[]{:S(2)}, u32[]{:S(2)}) %collective-permute-start) | collective-permute-done | bytes 4194336 | tf_op jit(solution)/shard_map/cond/branch_1_fun/ppermute | solution.py:334
  113.0 0.0 copy-done
  113.0 0.0 copy-start.1
  113.0 6.1 %branch_1_fun.5 = (f32[2048,128]{1,0:T(8,128)S(1)}, f32[4,16,128]{2,1,0:T(8,128)S(1)}) custom-call(s32[4]{0:T(128)S(1)} %get-tuple-element.29.place_ref, f32[16,128]{1,0:T(8,128)S(1)} %get-tuple-element.30.aux_ref, bf16[16,512,256]{2,1,0:T(8,128)(2,1)S(1)} %copy-done, bf16[16,512,256]{2,1,0:T(8,128)(2,1)S(1)} %collective-permute-done.other_ref, ...), custom_call_target="tpu_custom_call" | custom-call | tf_op jit(solution)/shard_map/cond/branch_1_fun/pallas_call | solution.py:268
  119.1 6.7 %all_to_all.23.pulled_ref = f32[4,16,128]{2,1,0:T(8,128)S(1)} all-to-all(f32[4,16,128]{2,1,0:T(8,128)S(1)} %get-tuple-element.36), channel_id=1, replica_groups=mesh['x'=4,'core'=2,'z'=16,'y'=4] {'y'}, dimensions={0} | all-to-all | bytes 65536 | tf_op jit(solution)/shard_map/cond/branch_1_fun/all_to_all | solution.py:347
  125.8 0.0 copy-done.1
  125.8 8.2 %branch_1_fun.6 = f32[32,32,128]{2,1,0:T(8,128)S(1)} custom-call(s32[4]{0:T(128)S(1)} %get-tuple-element.29.place_ref, f32[16,128]{1,0:T(8,128)S(1)} %get-tuple-element.30.aux_ref, bf16[16,512,256]{2,1,0:T(8,128)(2,1)S(1)} %copy-done, bf16[16,512,256]{2,1,0:T(8,128)(2,1)S(1)} %collective-permute-done.other_ref, f32[64,56,128]{2,1,0:T(8,128)S(1)} %copy-done.1, ...), custom_call_target="tpu_custom_call" | custom-call | tf_op jit(solution)/shard_map/cond/branch_1_fun/pallas_call | solution.py:268
  134.0 15.7 %all_to_all.24.got_ref = f32[32,32,128]{2,1,0:T(8,128)S(1)} all-to-all(f32[32,32,128]{2,1,0:T(8,128)S(1)} %branch_1_fun.6), channel_id=1, replica_groups=mesh['x'=4,'core'=2,'z'=16,'y'=4] {'x','core','y'}, dimensions={0} | all-to-all | bytes 1048576 | tf_op jit(solution)/shard_map/cond/branch_1_fun/all_to_all | solution.py:362
  149.8 1.3 branch_1_fun.7
Async XLA Ops:
  7.2 88.0 %all-gather.2.cloned.1.call-start = ((), (), s32[]{:S(2)}) async-start(), calls=%async_computation.5 | async-start | bytes 1949696 | tf_op jit(solution)/shard_map/all_gather | solution.py:375
  47.0 48.2 %copy-start.2 = (s32[1024]{0:T(1024)S(1)}, s32[1024]{0:T(1024)}, u32[]{:S(2)}) copy-start(s32[1024]{0:T(1024)} %param.18) | copy-start | bytes 12292
  47.0 48.2 %copy-start.3 = (f32[1024]{0:T(1024)S(1)}, f32[1024]{0:T(1024)}, u32[]{:S(2)}) copy-start(f32[1024]{0:T(1024)} %param.19) | copy-start | bytes 12292
  47.0 48.2 %copy-start.4 = (f32[1024]{0:T(1024)S(1)}, f32[1024]{0:T(1024)}, u32[]{:S(2)}) copy-start(f32[1024]{0:T(1024)} %param.20) | copy-start | bytes 12292
  47.0 48.3 %copy-start.5 = (f32[1,1024]{1,0:T(1,128)S(1)}, f32[1,1024]{1,0:T(1,128)}, u32[]{:S(2)}) copy-start(f32[1,1024]{1,0:T(1,128)} %param.21) | copy-start | bytes 12292
  95.2 17.8 %copy-start = (bf16[16,512,256]{2,1,0:T(8,128)(2,1)S(1)}, bf16[16,512,256]{2,1,0:T(8,128)(2,1)}, u32[]{:S(2)}) copy-start(bf16[16,512,256]{2,1,0:T(8,128)(2,1)} %get-tuple-element.31.mine_ref) | copy-start | bytes 12582916 | tf_op jit(solution)/shard_map/cond
  95.3 17.8 %collective-permute-start = (bf16[16,512,256]{2,1,0:T(8,128)(2,1)}, bf16[16,512,256]{2,1,0:T(8,128)(2,1)S(1)}, u32[]{:S(2)}, u32[]{:S(2)}) collective-permute-start(bf16[16,512,256]{2,1,0:T(8,128)(2,1)} %get-tuple-element.31.mine_ref), channel_id=1, source_target_pairs={{0,64},{64,0},{1,65},{65,1},{2,66},{66,2},{3,67},{67,3},{4,68},{68... | collective-permute-start | bytes 12582920 | tf_op jit(solution)/shard_map/cond/branch_1_fun/ppermute | solution.py:334
  113.0 12.8 %copy-start.1 = (f32[64,56,128]{2,1,0:T(8,128)S(1)}, f32[64,56,128]{2,1,0:T(8,128)}, u32[]{:S(2)}) copy-start(f32[64,56,128]{2,1,0:T(8,128)} %get-tuple-element.32.packed_ref) | copy-start | bytes 5505028 | tf_op jit(solution)/shard_map/cond
Sparse Core Ops, SparseCore 0:
  19.6 72.6 all-gather.1

commit v9 on v8

--- a/solution.py
+++ b/solution.py
@@ -197,7 +197,8 @@
         pull_ref[1, z : z + 1, :] = row
 
     pull_sums(aux_ref[0:1, :], rec_ref, short_ref, put)
-    z = place_ref[1]
+    z, column = place_ref[1], place_ref[3]
+    mult = jnp.concatenate([mult_ref[...], mult_ref[...]], axis=0)
     sub = rows_of((8, 128))
     pulls = jnp.where(
         sub == 0,
@@ -211,36 +212,37 @@
         lower = rec_ref[pl.ds(start + 16, 16), :]
         pair = jnp.where(low, upper, pltpu.roll(lower, SCEN, 1))
         for g in range(GROUPS):
-            send_ref[g * Y + q, 0:8, :] = mult_ref[...]
-            send_ref[g * Y + q, 8:16, :] = pulls
-            send_ref[g * Y + q, 16:32, :] = pair
+            send_ref[g * Y + q, 0:16, :] = jnp.where(column == g, pair, mult)
+            send_ref[g * Y + q, 16:24, :] = pulls
 
 
 def last_kernel(
-    place_ref, got_ref, assign_ref, hold_ref, stock_ref, consensus_ref, mult_ref, rec_ref, all_ref
+    place_ref, got_ref, assign_ref, hold_ref, stock_ref, own_ref, consensus_ref, mult_ref, rec_ref, all_ref
 ):
     z, y, column = place_ref[1], place_ref[2], place_ref[3]
     index = assign_ref[...] - z * (Y * ROWS)
     hold = hold_ref[...]
     start = stock_ref[...]
-    totals = [got_ref[g * Y, 10:11, :] for g in range(GROUPS)]
+    totals = [got_ref[g * Y, 18:19, :] for g in range(GROUPS)]
     all_total = totals[0]
     for g in range(1, GROUPS):
         all_total = all_total + totals[g]
-    mults = [got_ref[g * Y + y, 0:8, :] for g in range(GROUPS)]
+    mults = [
+        jnp.where(column == g, own_ref[...], got_ref[g * Y + y, 0:8, :]) for g in range(GROUPS)
+    ]
     stocks = []
     weighted = jnp.zeros((8, 128), f32)
     for g in range(GROUPS):
-        pull = pick(got_ref[g * Y, 8:9, :], index)
+        pull = pick(got_ref[g * Y, 16:17, :], index)
         stock = jnp.maximum(start - learn_rate * (hold + mults[g] - pull), 0.0)
         weighted = weighted + totals[g] * stock
         stocks.append(stock)
     consensus = weighted / all_total
     weighted = jnp.zeros((8, 128), f32)
     for g in range(GROUPS):
-        row = got_ref[g * Y, 9:10, :]
+        row = got_ref[g * Y, 17:18, :]
         for q in range(1, Y):
-            row = row + got_ref[g * Y + q, 9:10, :]
+            row = row + got_ref[g * Y + q, 17:18, :]
         pull = pick(row, index)
         apart = prox_weight * (stocks[g] - consensus)
         mults[g] = mults[g] + apart
@@ -256,8 +258,8 @@
     low = lanes_of((16, 128)) < SCEN
     for m in range(2):
         tile = slice(m * 128, m * 128 + 128)
-        even = got_ref[column * Y + 2 * m, 16:32, :]
-        odd = got_ref[column * Y + 2 * m + 1, 16:32, :]
+        even = got_ref[column * Y + 2 * m, 0:16, :]
+        odd = got_ref[column * Y + 2 * m + 1, 0:16, :]
         rec_ref[0:16, tile] = jnp.where(low, even, pltpu.roll(odd, SCEN, 1))
         rec_ref[16:32, tile] = jnp.where(low, pltpu.roll(even, SCEN, 1), odd)
 
@@ -347,7 +349,7 @@
         pull1 = lax.all_to_all(pull1, "y", 0, 0, tiled=True)
         (send,) = run_kernel(
             second_kernel,
-            [(GROUPS * Y, 32, 128)],
+            [(GROUPS * Y, 24, 128)],
             [(wide, f32), ((2, Z, 128), f32), (wide, f32), (wide, f32), (wide, jnp.bfloat16)],
             place,
             aux,
@@ -369,6 +371,7 @@
             assign,
             hold_cost,
             stock_init,
+            mult_init,
         )
         return consensus, multipliers, recourse
 

time: 160 us -> 159 us (level)
  no operation moved by 1% of the time
where the time goes in v9:
time: 159 us; the launch traced here: 157 us
  blocking collectives  107 us (67%)
  Pallas kernels  20.2 us (13%)
  between operations  14.1 us (9%)
  starting transfers between devices  10.8 us (7%)
  waiting for transfers between devices  4.67 us (3%)
    all_to_all x1, blocking collectives, spread_xy(): return lax.all_to_all(spread, ('x', 'y'), 0, 0, tiled=True)  47.8 us
    all_to_all x1, blocking collectives, spread_z(): return lax.all_to_all(block, 'z', 0, 0, tiled=True).reshape(Z * ROWS, COLS)  27.5 us
    pallas_call x5, Pallas kernels, run_kernel(): pl.pallas_call(kernel, out_shape=outs, in_specs=[pl.BlockSpec(memory_spac...  20.2 us
    all_to_all x1, blocking collectives, finish(): got = lax.all_to_all(send, ('x', 'core', 'y'), 0, 0, tiled=True)  14.8 us
    ppermute x1, starting transfers between devices, finish(): other = lax.ppermute(mine, 'core', [(0, 1), (1, 0)])  10.8 us
    all_to_all x1, blocking collectives, per_device(): packed = lax.all_to_all(packed, 'y', 0, 0, tiled=True)  9.87 us
    all_to_all x1, blocking collectives, finish(): pull1 = lax.all_to_all(pull1, 'y', 0, 0, tiled=True)  6.65 us
    ppermute x1, waiting for transfers between devices, finish(): other = lax.ppermute(mine, 'core', [(0, 1), (1, 0)])  4.65 us
  transfers between devices with their start and end apart: 2, of which 1 were waited for; matrix products, arithmetic and copies ran while one was open for 0% of the time, Pallas kernels for 1%

profile of v9, /device:TPU:1, one launch (start us, length us, event | category | flops | bytes accessed | tf_op | source)
XLA Modules:
  0.0 156.9 jit_solution(9511047433536143995)
XLA Ops:
  7.2 0.0 all-gather.2.cloned.1.call-start
  7.2 0.1 pad_add_fusion.place_ref
  7.3 2.3 %shard_map.103 = (f32[4,56,128]{2,1,0:T(8,128)}, f32[16,128]{1,0:T(8,128)S(1)}, bf16[16,32,256]{2,1,0:T(8,128)(2,1)S(1)}) custom-call(s32[4]{0:T(128)S(1)} %pad_add_fusion.place_ref, bf16[32,2048]{1,0:T(8,128)(2,1)} %transship_ref.1, s32[32,256]{1,0:T(8,128)} %refs_0_.1, f32[32,256]{1,0:T(8,128)} %refs_1_.1, s32[2,128]{1,0:T(2,128)} %bitcast.23, ...), custom_call_target="tpu_custom_call" | custom-call | tf_op jit(solution)/shard_map/pallas_call | solution.py:270
  9.6 9.9 %all_to_all.25 = f32[4,56,128]{2,1,0:T(8,128)} all-to-all(f32[4,56,128]{2,1,0:T(8,128)} %get-tuple-element.54), channel_id=1, replica_groups=mesh['x'=4,'core'=2,'z'=16,'y'=4] {'y'}, dimensions={0} | all-to-all | bytes 229376 | tf_op jit(solution)/shard_map/all_to_all | solution.py:325
  19.4 0.0 all-gather.2.cloned.1.call-update
  19.5 27.5 %conditional.3 = (bf16[512,256]{1,0:T(8,128)(2,1)S(1)}) conditional(s32[]{:T(128)} %convert_element_type.2, () %tuple.34, bf16[16,32,256]{2,1,0:T(8,128)(2,1)S(1)} %get-tuple-element.53), branch_computations={%region_0.0_spmd, %region_1.0_spmd} | conditional | bytes 524296 | solution.py:289
  19.5 27.5 %all_to_all.21 = bf16[16,32,256]{2,1,0:T(8,128)(2,1)S(1)} all-to-all(bf16[16,32,256]{2,1,0:T(8,128)(2,1)S(1)} %param.1), channel_id=1, replica_groups=mesh['x'=4,'core'=2,'z'=16,'y'=4] {'z'}, dimensions={0} | all-to-all | bytes 524288 | tf_op jit(solution)/shard_map/cond/branch_1_fun/all_to_all | solution.py:329
  47.0 0.0 copy-start.2
  47.0 0.0 copy-start.3
  47.0 0.0 copy-start.4
  47.0 0.0 copy-start.5
  47.0 48.2 %conditional.4 = (bf16[16,512,256]{2,1,0:T(8,128)(2,1)}) conditional(s32[]{:T(128)} %convert_element_type.2, () %tuple.33, bf16[512,256]{1,0:T(8,128)(2,1)S(1)} %get-tuple-element.65), branch_computations={%region_2.0_spmd, %region_3.0_spmd} | conditional | bytes 12845064 | solution.py:289
  47.0 0.4 broadcast_in_dim.0
  47.4 47.8 %all_to_all.22 = bf16[16,512,256]{2,1,0:T(8,128)(2,1)} all-to-all(bf16[16,512,256]{2,1,0:T(8,128)(2,1)S(1)} %broadcast_in_dim.0), channel_id=1, replica_groups=mesh['x'=4,'core'=2,'z'=16,'y'=4] {'x','y'}, dimensions={0} | all-to-all | bytes 8388608 | tf_op jit(solution)/shard_map/cond/branch_1_fun/all_to_all | solution.py:333
  95.2 0.0 all-gather.2.cloned.1.call-done
  95.2 0.0 copy-done.2
  95.2 0.0 copy-done.3
  95.2 0.0 copy-done.4
  95.2 0.0 copy-done.5
  95.2 54.8 %conditional.5 = (f32[32,256]{1,0:T(8,128)}, f32[1024]{0:T(1024)}, f32[1,1024]{1,0:T(1,128)}) conditional(s32[]{:T(128)} %convert_element_type.2, () %tuple.32, (bf16[16,512,256]{2,1,0:T(8,128)(2,1)}, s32[4]{0:T(128)S(1)}, f32[64,56,128]{2,1,0:T(8,128)}, f32[16,128]{1,0:T(8,128)S(1)}, f32[8,128]{1,0:T(8,128)S(1)}, /*index=5*/s32[8,128]{1,0:T(8,128)S(1)}, ...), branch_computations={%region_4.0_spmd, %region_5.0_spmd} | conditional | flops 2000000000 | bytes 41746552 | solution.py:289
  95.2 0.0 copy-start
  95.3 10.8 %collective-permute-start = (bf16[16,512,256]{2,1,0:T(8,128)(2,1)}, bf16[16,512,256]{2,1,0:T(8,128)(2,1)S(1)}, u32[]{:S(2)}, u32[]{:S(2)}) collective-permute-start(bf16[16,512,256]{2,1,0:T(8,128)(2,1)} %get-tuple-element.31.mine_ref), channel_id=1, source_target_pairs={{0,64},{64,0},{1,65},{65,1},{2,66},{66,2},{3,67},{67,3},{4,68},{68... | collective-permute-start | bytes 12582920 | tf_op jit(solution)/shard_map/cond/branch_1_fun/ppermute | solution.py:336
  106.0 2.3 %branch_1_fun.4 = (f32[2048,128]{1,0:T(8,128)S(1)}, f32[2048,128]{1,0:T(8,128)S(1)}) custom-call(s32[4]{0:T(128)S(1)} %get-tuple-element.29.place_ref, f32[64,56,128]{2,1,0:T(8,128)} %get-tuple-element.32.packed_ref), custom_call_target="tpu_custom_call" | custom-call | flops 2000000000 | tf_op jit(solution)/shard_map/cond/branch_1_fun/pallas_call | solution.py:270
  108.4 4.6 %collective-permute-done.other_ref = bf16[16,512,256]{2,1,0:T(8,128)(2,1)S(1)} collective-permute-done((bf16[16,512,256]{2,1,0:T(8,128)(2,1)}, bf16[16,512,256]{2,1,0:T(8,128)(2,1)S(1)}, u32[]{:S(2)}, u32[]{:S(2)}) %collective-permute-start) | collective-permute-done | bytes 4194336 | tf_op jit(solution)/shard_map/cond/branch_1_fun/ppermute | solution.py:336
  113.0 0.0 copy-done
  113.0 0.0 copy-start.1
  113.0 6.1 %branch_1_fun.5 = (f32[2048,128]{1,0:T(8,128)S(1)}, f32[4,16,128]{2,1,0:T(8,128)S(1)}) custom-call(s32[4]{0:T(128)S(1)} %get-tuple-element.29.place_ref, f32[16,128]{1,0:T(8,128)S(1)} %get-tuple-element.30.aux_ref, bf16[16,512,256]{2,1,0:T(8,128)(2,1)S(1)} %copy-done, bf16[16,512,256]{2,1,0:T(8,128)(2,1)S(1)} %collective-permute-done.other_ref, ...), custom_call_target="tpu_custom_call" | custom-call | tf_op jit(solution)/shard_map/cond/branch_1_fun/pallas_call | solution.py:270
  119.1 6.7 %all_to_all.23.pulled_ref = f32[4,16,128]{2,1,0:T(8,128)S(1)} all-to-all(f32[4,16,128]{2,1,0:T(8,128)S(1)} %get-tuple-element.36), channel_id=1, replica_groups=mesh['x'=4,'core'=2,'z'=16,'y'=4] {'y'}, dimensions={0} | all-to-all | bytes 65536 | tf_op jit(solution)/shard_map/cond/branch_1_fun/all_to_all | solution.py:349
  125.8 0.0 copy-done.1
  125.8 8.2 %branch_1_fun.6 = f32[32,24,128]{2,1,0:T(8,128)S(1)} custom-call(s32[4]{0:T(128)S(1)} %get-tuple-element.29.place_ref, f32[16,128]{1,0:T(8,128)S(1)} %get-tuple-element.30.aux_ref, bf16[16,512,256]{2,1,0:T(8,128)(2,1)S(1)} %copy-done, bf16[16,512,256]{2,1,0:T(8,128)(2,1)S(1)} %collective-permute-done.other_ref, f32[64,56,128]{2,1,0:T(8,128)S(1)} %copy-done.1, ...), custom_call_target="tpu_custom_call" | custom-call | tf_op jit(solution)/shard_map/cond/branch_1_fun/pallas_call | solution.py:270
  134.0 14.8 %all_to_all.24.got_ref = f32[32,24,128]{2,1,0:T(8,128)S(1)} all-to-all(f32[32,24,128]{2,1,0:T(8,128)S(1)} %branch_1_fun.6), channel_id=1, replica_groups=mesh['x'=4,'core'=2,'z'=16,'y'=4] {'x','core','y'}, dimensions={0} | all-to-all | bytes 786432 | tf_op jit(solution)/shard_map/cond/branch_1_fun/all_to_all | solution.py:364
  148.7 1.3 branch_1_fun.7
Async XLA Ops:
  7.2 88.0 %all-gather.2.cloned.1.call-start = ((), (), s32[]{:S(2)}) async-start(), calls=%async_computation.5 | async-start | bytes 1949696 | tf_op jit(solution)/shard_map/all_gather | solution.py:378
  47.0 48.2 %copy-start.2 = (f32[1,1024]{1,0:T(1,128)S(1)}, f32[1,1024]{1,0:T(1,128)}, u32[]{:S(2)}) copy-start(f32[1,1024]{1,0:T(1,128)} %param.21) | copy-start | bytes 12292
  47.0 48.2 %copy-start.3 = (s32[1024]{0:T(1024)S(1)}, s32[1024]{0:T(1024)}, u32[]{:S(2)}) copy-start(s32[1024]{0:T(1024)} %param.18) | copy-start | bytes 12292
  47.0 48.2 %copy-start.4 = (f32[1024]{0:T(1024)S(1)}, f32[1024]{0:T(1024)}, u32[]{:S(2)}) copy-start(f32[1024]{0:T(1024)} %param.19) | copy-start | bytes 12292
  47.0 48.3 %copy-start.5 = (f32[1024]{0:T(1024)S(1)}, f32[1024]{0:T(1024)}, u32[]{:S(2)}) copy-start(f32[1024]{0:T(1024)} %param.20) | copy-start | bytes 12292
  95.2 17.8 %copy-start = (bf16[16,512,256]{2,1,0:T(8,128)(2,1)S(1)}, bf16[16,512,256]{2,1,0:T(8,128)(2,1)}, u32[]{:S(2)}) copy-start(bf16[16,512,256]{2,1,0:T(8,128)(2,1)} %get-tuple-element.31.mine_ref) | copy-start | bytes 12582916 | tf_op jit(solution)/shard_map/cond
  95.3 17.8 %collective-permute-start = (bf16[16,512,256]{2,1,0:T(8,128)(2,1)}, bf16[16,512,256]{2,1,0:T(8,128)(2,1)S(1)}, u32[]{:S(2)}, u32[]{:S(2)}) collective-permute-start(bf16[16,512,256]{2,1,0:T(8,128)(2,1)} %get-tuple-element.31.mine_ref), channel_id=1, source_target_pairs={{0,64},{64,0},{1,65},{65,1},{2,66},{66,2},{3,67},{67,3},{4,68},{68... | collective-permute-start | bytes 12582920 | tf_op jit(solution)/shard_map/cond/branch_1_fun/ppermute | solution.py:336
  113.0 12.8 %copy-start.1 = (f32[64,56,128]{2,1,0:T(8,128)S(1)}, f32[64,56,128]{2,1,0:T(8,128)}, u32[]{:S(2)}) copy-start(f32[64,56,128]{2,1,0:T(8,128)} %get-tuple-element.32.packed_ref) | copy-start | bytes 5505028 | tf_op jit(solution)/shard_map/cond
Sparse Core Ops, SparseCore 0:
  19.6 72.6 all-gather.1

commit v10 on v8

--- a/solution.py
+++ b/solution.py
@@ -166,6 +166,8 @@
     pulled_ref,
     mult_ref,
     send_ref,
+    own_pull_ref,
+    own_short_ref,
     rec_ref,
     pull_ref,
     short_ref,
@@ -197,13 +199,16 @@
         pull_ref[1, z : z + 1, :] = row
 
     pull_sums(aux_ref[0:1, :], rec_ref, short_ref, put)
-    z = place_ref[1]
+    z, y, column = place_ref[1], place_ref[2], place_ref[3]
     sub = rows_of((8, 128))
+    own_pull_ref[...] = jnp.broadcast_to(pull_ref[0, pl.ds(z, 1), :], (8, 128))
+    own_short_ref[...] = short_ref[pl.ds(pl.multiple_of((z * Y + y) * ROWS, ROWS), ROWS), :]
     pulls = jnp.where(
         sub == 0,
         pull_ref[0, pl.ds(z, 1), :],
         jnp.where(sub == 1, pull_ref[1, pl.ds(z, 1), :], aux_ref[8:9, :]),
     )
+    others = jnp.concatenate([mult_ref[...], pulls], axis=0)
     low = lanes_of((16, 128)) < SCEN
     for q in range(Y):
         start = pl.multiple_of((z * Y + q) * ROWS, ROWS)
@@ -211,27 +216,66 @@
         lower = rec_ref[pl.ds(start + 16, 16), :]
         pair = jnp.where(low, upper, pltpu.roll(lower, SCEN, 1))
         for g in range(GROUPS):
-            send_ref[g * Y + q, 0:8, :] = mult_ref[...]
-            send_ref[g * Y + q, 8:16, :] = pulls
-            send_ref[g * Y + q, 16:32, :] = pair
+            send_ref[g * Y + q] = jnp.where(column == g, pair, others)
 
 
 def last_kernel(
-    place_ref, got_ref, assign_ref, hold_ref, stock_ref, consensus_ref, mult_ref, rec_ref, all_ref
+    place_ref,
+    got_ref,
+    assign_ref,
+    hold_ref,
+    stock_ref,
+    own_mult_ref,
+    own_pull_ref,
+    own_short_ref,
+    demand_ref,
+    counts_ref,
+    consensus_ref,
+    mult_ref,
+    rec_ref,
+    all_ref,
 ):
     z, y, column = place_ref[1], place_ref[2], place_ref[3]
+    low = lanes_of((16, 128)) < SCEN
+    for m in range(2):
+        tile = slice(m * 128, m * 128 + 128)
+        even = got_ref[column * Y + 2 * m]
+        odd = got_ref[column * Y + 2 * m + 1]
+        rec_ref[0:16, tile] = jnp.where(low, even, pltpu.roll(odd, SCEN, 1))
+        rec_ref[16:32, tile] = jnp.where(low, pltpu.roll(even, SCEN, 1), odd)
+
+    weights = counts_ref[...].astype(f32)
+    own_total = jnp.sum(jnp.sum(weights, axis=1, keepdims=True), axis=0, keepdims=True)
+    share = weights / own_total
+    demand = demand_ref[...].astype(f32)
+    part = jnp.where(y >= 2, demand[:, 128:256], demand[:, 0:128])
+    part = jnp.where(y % 2 == 1, pltpu.roll(part, SCEN, 1), part)
+    stock_sum = (part - own_short_ref[...])[:, 0:1]
+    gap = jnp.zeros((ROWS, 128), f32)
+    for m in range(2):
+        tile = slice(m * 128, m * 128 + 128)
+        short = demand[:, tile] - stock_sum
+        gap = gap + penalty * (short - rec_ref[:, tile]) * share[m : m + 1]
+    gap = jnp.sum(gap, axis=1, keepdims=True)
+    own = lanes_of((ROWS, 128)) == rows_of((ROWS, 128)) + y * ROWS
+    own_last = jnp.sum(jnp.where(own, gap, 0.0), axis=0, keepdims=True)
+
+    def from_group(g, mine, theirs):
+        return jnp.where(column == g, mine, theirs)
+
     index = assign_ref[...] - z * (Y * ROWS)
     hold = hold_ref[...]
     start = stock_ref[...]
-    totals = [got_ref[g * Y, 10:11, :] for g in range(GROUPS)]
+    own_total = jnp.broadcast_to(own_total, (1, 128))
+    totals = [from_group(g, own_total, got_ref[g * Y, 10:11, :]) for g in range(GROUPS)]
     all_total = totals[0]
     for g in range(1, GROUPS):
         all_total = all_total + totals[g]
-    mults = [got_ref[g * Y + y, 0:8, :] for g in range(GROUPS)]
+    mults = [from_group(g, own_mult_ref[...], got_ref[g * Y + y, 0:8, :]) for g in range(GROUPS)]
     stocks = []
     weighted = jnp.zeros((8, 128), f32)
     for g in range(GROUPS):
-        pull = pick(got_ref[g * Y, 8:9, :], index)
+        pull = pick(from_group(g, own_pull_ref[0:1, :], got_ref[g * Y, 8:9, :]), index)
         stock = jnp.maximum(start - learn_rate * (hold + mults[g] - pull), 0.0)
         weighted = weighted + totals[g] * stock
         stocks.append(stock)
@@ -241,7 +285,7 @@
         row = got_ref[g * Y, 9:10, :]
         for q in range(1, Y):
             row = row + got_ref[g * Y + q, 9:10, :]
-        pull = pick(row, index)
+        pull = pick(from_group(g, own_last, row), index)
         apart = prox_weight * (stocks[g] - consensus)
         mults[g] = mults[g] + apart
         stock = jnp.maximum(stocks[g] - learn_rate * (hold + mults[g] - pull + apart), 0.0)
@@ -252,14 +296,6 @@
     for g in range(GROUPS):
         all_ref[g] = mults[g] + prox_weight * (stocks[g] - consensus)
     mult_ref[...] = all_ref[column]
-
-    low = lanes_of((16, 128)) < SCEN
-    for m in range(2):
-        tile = slice(m * 128, m * 128 + 128)
-        even = got_ref[column * Y + 2 * m, 16:32, :]
-        odd = got_ref[column * Y + 2 * m + 1, 16:32, :]
-        rec_ref[0:16, tile] = jnp.where(low, even, pltpu.roll(odd, SCEN, 1))
-        rec_ref[16:32, tile] = jnp.where(low, pltpu.roll(even, SCEN, 1), odd)
 
 
 def run_kernel(kernel, outs, scratch, *args, hbm=0, vmem_mib=16, flops=0):
@@ -345,9 +381,9 @@
             short,
         )
         pull1 = lax.all_to_all(pull1, "y", 0, 0, tiled=True)
-        (send,) = run_kernel(
+        send, own_pull, own_short = run_kernel(
             second_kernel,
-            [(GROUPS * Y, 32, 128)],
+            [(GROUPS * Y, 16, 128), (8, 128), (ROWS, 128)],
             [(wide, f32), ((2, Z, 128), f32), (wide, f32), (wide, f32), (wide, jnp.bfloat16)],
             place,
             aux,
@@ -369,6 +405,11 @@
             assign,
             hold_cost,
             stock_init,
+            mult_init,
+            own_pull,
+            own_short,
+            demand,
+            counts.reshape(2, 128),
         )
         return consensus, multipliers, recourse
 

time: 160 us -> 158 us (0.988)
  blocking collectives: 108 us -> 105 us
    all_to_all x1, blocking collectives: 15.7 us -> 13.5 us  [finish(): got = lax.all_to_all(send, ('x', 'core', 'y'), 0, 0, tiled=True)]
where the time goes in v10:
time: 158 us; the launch traced here: 156 us
  blocking collectives  105 us (66%)
  Pallas kernels  20.5 us (13%)
  between operations  14.1 us (9%)
  starting transfers between devices  10.8 us (7%)
  waiting for transfers between devices  4.67 us (3%)
    all_to_all x1, blocking collectives, spread_xy(): return lax.all_to_all(spread, ('x', 'y'), 0, 0, tiled=True)  47.8 us
    all_to_all x1, blocking collectives, spread_z(): return lax.all_to_all(block, 'z', 0, 0, tiled=True).reshape(Z * ROWS, COLS)  27.5 us
    pallas_call x5, Pallas kernels, run_kernel(): pl.pallas_call(kernel, out_shape=outs, in_specs=[pl.BlockSpec(memory_spac...  20.5 us
    all_to_all x1, blocking collectives, finish(): got = lax.all_to_all(send, ('x', 'core', 'y'), 0, 0, tiled=True)  13.5 us
    ppermute x1, starting transfers between devices, finish(): other = lax.ppermute(mine, 'core', [(0, 1), (1, 0)])  10.8 us
    all_to_all x1, blocking collectives, per_device(): packed = lax.all_to_all(packed, 'y', 0, 0, tiled=True)  9.87 us
    all_to_all x1, blocking collectives, finish(): pull1 = lax.all_to_all(pull1, 'y', 0, 0, tiled=True)  6.65 us
    ppermute x1, waiting for transfers between devices, finish(): other = lax.ppermute(mine, 'core', [(0, 1), (1, 0)])  4.65 us
  transfers between devices with their start and end apart: 2, of which 1 were waited for; matrix products, arithmetic and copies ran while one was open for 0% of the time, Pallas kernels for 1%

profile of v10, /device:TPU:1, one launch (start us, length us, event | category | flops | bytes accessed | tf_op | source)
XLA Modules:
  0.0 156.0 jit_solution(16682784265990150349)
XLA Ops:
  7.2 0.0 all-gather.2.cloned.1.call-start
  7.2 0.1 pad_add_fusion.place_ref
  7.3 2.3 %shard_map.103 = (f32[4,56,128]{2,1,0:T(8,128)}, f32[16,128]{1,0:T(8,128)S(1)}, bf16[16,32,256]{2,1,0:T(8,128)(2,1)S(1)}) custom-call(s32[4]{0:T(128)S(1)} %pad_add_fusion.place_ref, bf16[32,2048]{1,0:T(8,128)(2,1)} %transship_ref.1, s32[32,256]{1,0:T(8,128)} %refs_0_.1, f32[32,256]{1,0:T(8,128)} %refs_1_.1, s32[2,128]{1,0:T(2,128)} %bitcast.22, ...), custom_call_target="tpu_custom_call" | custom-call | tf_op jit(solution)/shard_map/pallas_call | solution.py:304
  9.6 9.9 %all_to_all.25 = f32[4,56,128]{2,1,0:T(8,128)} all-to-all(f32[4,56,128]{2,1,0:T(8,128)} %get-tuple-element.63), channel_id=1, replica_groups=mesh['x'=4,'core'=2,'z'=16,'y'=4] {'y'}, dimensions={0} | all-to-all | bytes 229376 | tf_op jit(solution)/shard_map/all_to_all | solution.py:359
  19.4 0.0 all-gather.2.cloned.1.call-update
  19.5 27.5 %conditional.3 = (bf16[512,256]{1,0:T(8,128)(2,1)S(1)}) conditional(s32[]{:T(128)} %convert_element_type.2, () %tuple.34, bf16[16,32,256]{2,1,0:T(8,128)(2,1)S(1)} %get-tuple-element.62), branch_computations={%region_0.0_spmd, %region_1.0_spmd} | conditional | bytes 524296 | solution.py:323
  19.5 27.5 %all_to_all.21 = bf16[16,32,256]{2,1,0:T(8,128)(2,1)S(1)} all-to-all(bf16[16,32,256]{2,1,0:T(8,128)(2,1)S(1)} %param.1), channel_id=1, replica_groups=mesh['x'=4,'core'=2,'z'=16,'y'=4] {'z'}, dimensions={0} | all-to-all | bytes 524288 | tf_op jit(solution)/shard_map/cond/branch_1_fun/all_to_all | solution.py:363
  47.0 0.0 copy-start.2
  47.0 0.0 copy-start.3
  47.0 0.0 copy-start.4
  47.0 0.0 copy-start.5
  47.0 0.0 copy-start.6
  47.0 0.0 copy-start.7
  47.0 48.2 %conditional.4 = (bf16[16,512,256]{2,1,0:T(8,128)(2,1)}) conditional(s32[]{:T(128)} %convert_element_type.2, () %tuple.33, bf16[512,256]{1,0:T(8,128)(2,1)S(1)} %get-tuple-element.74), branch_computations={%region_2.0_spmd, %region_3.0_spmd} | conditional | bytes 12845064 | solution.py:323
  47.0 0.4 broadcast_in_dim.0
  47.4 47.8 %all_to_all.22 = bf16[16,512,256]{2,1,0:T(8,128)(2,1)} all-to-all(bf16[16,512,256]{2,1,0:T(8,128)(2,1)S(1)} %broadcast_in_dim.0), channel_id=1, replica_groups=mesh['x'=4,'core'=2,'z'=16,'y'=4] {'x','y'}, dimensions={0} | all-to-all | bytes 8388608 | tf_op jit(solution)/shard_map/cond/branch_1_fun/all_to_all | solution.py:367
  95.2 0.0 all-gather.2.cloned.1.call-done
  95.2 0.0 copy-done.2
  95.2 0.0 copy-done.3
  95.2 0.0 copy-done.4
  95.2 0.0 copy-done.5
  95.3 0.0 copy-done.6
  95.3 0.0 copy-done.7
  95.3 53.9 %conditional.5 = (f32[32,256]{1,0:T(8,128)}, f32[1024]{0:T(1024)}, f32[1,1024]{1,0:T(1,128)}) conditional(s32[]{:T(128)} %convert_element_type.2, () %tuple.32, (bf16[16,512,256]{2,1,0:T(8,128)(2,1)}, s32[4]{0:T(128)S(1)}, f32[64,56,128]{2,1,0:T(8,128)}, f32[16,128]{1,0:T(8,128)S(1)}, f32[8,128]{1,0:T(8,128)S(1)}, /*index=5*/s32[256]{0:T(256)S(1)}, ...), branch_computations={%region_4.0_spmd, %region_5.0_spmd} | conditional | flops 2000000000 | bytes 41484408 | solution.py:323
  95.3 0.0 copy-start
  95.3 10.8 %collective-permute-start = (bf16[16,512,256]{2,1,0:T(8,128)(2,1)}, bf16[16,512,256]{2,1,0:T(8,128)(2,1)S(1)}, u32[]{:S(2)}, u32[]{:S(2)}) collective-permute-start(bf16[16,512,256]{2,1,0:T(8,128)(2,1)} %get-tuple-element.35.mine_ref), channel_id=1, source_target_pairs={{0,64},{64,0},{1,65},{65,1},{2,66},{66,2},{3,67},{67,3},{4,68},{68... | collective-permute-start | bytes 12582920 | tf_op jit(solution)/shard_map/cond/branch_1_fun/ppermute | solution.py:370
  106.1 2.3 %branch_1_fun.4 = (f32[2048,128]{1,0:T(8,128)S(1)}, f32[2048,128]{1,0:T(8,128)S(1)}) custom-call(s32[4]{0:T(128)S(1)} %get-tuple-element.33.place_ref, f32[64,56,128]{2,1,0:T(8,128)} %get-tuple-element.36.packed_ref), custom_call_target="tpu_custom_call" | custom-call | flops 2000000000 | tf_op jit(solution)/shard_map/cond/branch_1_fun/pallas_call | solution.py:304
  108.4 4.6 %collective-permute-done.other_ref = bf16[16,512,256]{2,1,0:T(8,128)(2,1)S(1)} collective-permute-done((bf16[16,512,256]{2,1,0:T(8,128)(2,1)}, bf16[16,512,256]{2,1,0:T(8,128)(2,1)S(1)}, u32[]{:S(2)}, u32[]{:S(2)}) %collective-permute-start) | collective-permute-done | bytes 4194336 | tf_op jit(solution)/shard_map/cond/branch_1_fun/ppermute | solution.py:370
  113.0 0.0 copy-done
  113.0 0.0 copy-start.1
  113.0 6.2 %branch_1_fun.5 = (f32[2048,128]{1,0:T(8,128)S(1)}, f32[4,16,128]{2,1,0:T(8,128)S(1)}) custom-call(s32[4]{0:T(128)S(1)} %get-tuple-element.33.place_ref, f32[16,128]{1,0:T(8,128)S(1)} %get-tuple-element.34.aux_ref, bf16[16,512,256]{2,1,0:T(8,128)(2,1)S(1)} %copy-done, bf16[16,512,256]{2,1,0:T(8,128)(2,1)S(1)} %collective-permute-done.other_ref, ...), custom_call_target="tpu_custom_call" | custom-call | tf_op jit(solution)/shard_map/cond/branch_1_fun/pallas_call | solution.py:304
  119.3 6.7 %all_to_all.23.pulled_ref = f32[4,16,128]{2,1,0:T(8,128)S(1)} all-to-all(f32[4,16,128]{2,1,0:T(8,128)S(1)} %get-tuple-element.40), channel_id=1, replica_groups=mesh['x'=4,'core'=2,'z'=16,'y'=4] {'y'}, dimensions={0} | all-to-all | bytes 65536 | tf_op jit(solution)/shard_map/cond/branch_1_fun/all_to_all | solution.py:383
  125.9 0.0 copy-done.1
  125.9 8.2 %branch_1_fun.6 = (f32[32,16,128]{2,1,0:T(8,128)S(1)}, f32[8,128]{1,0:T(8,128)S(1)}, f32[32,128]{1,0:T(8,128)S(1)}) custom-call(s32[4]{0:T(128)S(1)} %get-tuple-element.33.place_ref, f32[16,128]{1,0:T(8,128)S(1)} %get-tuple-element.34.aux_ref, bf16[16,512,256]{2,1,0:T(8,128)(2,1)S(1)} %copy-done, bf16[16,512,256]{2,1,0:T(8,128)(2,1)S(1)} %collective-permute-done.other_ref, ...), custom_call_target="tpu_custom_call" | custom-call | tf_op jit(solution)/shard_map/cond/branch_1_fun/pallas_call | solution.py:304
  134.2 13.5 %all_to_all.24.got_ref = f32[32,16,128]{2,1,0:T(8,128)S(1)} all-to-all(f32[32,16,128]{2,1,0:T(8,128)S(1)} %get-tuple-element.42), channel_id=1, replica_groups=mesh['x'=4,'core'=2,'z'=16,'y'=4] {'x','core','y'}, dimensions={0} | all-to-all | bytes 524288 | tf_op jit(solution)/shard_map/cond/branch_1_fun/all_to_all | solution.py:398
  147.7 1.5 branch_1_fun.7
Async XLA Ops:
  7.2 88.1 %all-gather.2.cloned.1.call-start = ((), (), s32[]{:S(2)}) async-start(), calls=%async_computation.5 | async-start | bytes 1949696 | tf_op jit(solution)/shard_map/all_gather | solution.py:416
  47.0 48.3 %copy-start.2 = (s32[32,256]{1,0:T(8,128)S(1)}, s32[32,256]{1,0:T(8,128)}, u32[]{:S(2)}) copy-start(s32[32,256]{1,0:T(8,128)} %refs_0_.1) | copy-start | bytes 98308
  47.0 48.3 %copy-start.3 = (f32[1,1024]{1,0:T(1,128)S(1)}, f32[1,1024]{1,0:T(1,128)}, u32[]{:S(2)}) copy-start(f32[1,1024]{1,0:T(1,128)} %param.21) | copy-start | bytes 12292
  47.0 48.3 %copy-start.4 = (s32[1024]{0:T(1024)S(1)}, s32[1024]{0:T(1024)}, u32[]{:S(2)}) copy-start(s32[1024]{0:T(1024)} %param.18) | copy-start | bytes 12292
  47.0 48.3 %copy-start.5 = (f32[1024]{0:T(1024)S(1)}, f32[1024]{0:T(1024)}, u32[]{:S(2)}) copy-start(f32[1024]{0:T(1024)} %param.19) | copy-start | bytes 12292
  47.0 48.3 %copy-start.6 = (f32[1024]{0:T(1024)S(1)}, f32[1024]{0:T(1024)}, u32[]{:S(2)}) copy-start(f32[1024]{0:T(1024)} %param.20) | copy-start | bytes 12292
  47.0 48.3 %copy-start.7 = (s32[256]{0:T(256)S(1)}, s32[256]{0:T(256)}, u32[]{:S(2)}) copy-start(s32[256]{0:T(256)} %param.17) | copy-start | bytes 3076
  95.3 17.8 %copy-start = (bf16[16,512,256]{2,1,0:T(8,128)(2,1)S(1)}, bf16[16,512,256]{2,1,0:T(8,128)(2,1)}, u32[]{:S(2)}) copy-start(bf16[16,512,256]{2,1,0:T(8,128)(2,1)} %get-tuple-element.35.mine_ref) | copy-start | bytes 12582916 | tf_op jit(solution)/shard_map/cond
  95.3 17.8 %collective-permute-start = (bf16[16,512,256]{2,1,0:T(8,128)(2,1)}, bf16[16,512,256]{2,1,0:T(8,128)(2,1)S(1)}, u32[]{:S(2)}, u32[]{:S(2)}) collective-permute-start(bf16[16,512,256]{2,1,0:T(8,128)(2,1)} %get-tuple-element.35.mine_ref), channel_id=1, source_target_pairs={{0,64},{64,0},{1,65},{65,1},{2,66},{66,2},{3,67},{67,3},{4,68},{68... | collective-permute-start | bytes 12582920 | tf_op jit(solution)/shard_map/cond/branch_1_fun/ppermute | solution.py:370
  113.0 12.9 %copy-start.1 = (f32[64,56,128]{2,1,0:T(8,128)S(1)}, f32[64,56,128]{2,1,0:T(8,128)}, u32[]{:S(2)}) copy-start(f32[64,56,128]{2,1,0:T(8,128)} %get-tuple-element.36.packed_ref) | copy-start | bytes 5505028 | tf_op jit(solution)/shard_map/cond
Sparse Core Ops, SparseCore 0:
  19.6 72.6 all-gather.1
